TPU v7x, 32 devices: a whole 2x2x4 slice. The times are simulated.
32 devices in a mesh: groups: 2 (over y), lon: 4 (over z), lat: 2 (over x), dp: 2 (over core).
Axes of the slice: x: 2, y: 2, z: 4, core: 2. Of those that a mesh axis runs over, the one named last changes fastest.
Arguments:
- fine_field: bfloat16 [8, 128, 128, 128], P(('groups', 'dp'), 'lat', 'lon'), parts along dimension 0, may hold values from -6 to 6
- grad_out: bfloat16 [8, 64, 64, 256], P(('groups', 'dp'), 'lat', 'lon'), parts along dimension 0, may hold values from -6 to 6
- conv_kernel: float32 [49, 256], replicated, may hold values from -0.875 to 0.875
- norm_gain: float32 [256], replicated, may hold values from 0.1 to 1.9
- w_expand: bfloat16 [256, 1024], replicated, may hold values from -0.375 to 0.375
- w_contract: bfloat16 [1024, 256], replicated, may hold values from -0.1875 to 0.1875
- w_merge: bfloat16 [512, 256], replicated, may hold values from -0.25 to 0.25
Outputs:
- section_out: bfloat16 [8, 64, 64, 256], P(('groups', 'dp'), 'lat', 'lon'), parts along dimension 0
- grad_fine: bfloat16 [8, 128, 128, 128], P(('groups', 'dp'), 'lat', 'lon'), parts along dimension 0
- grad_kernel: float32 [98, 256], P('groups', 'dp'), parts along dimension 0
- grad_gain: float32 [512], P(('groups', 'dp')), parts along dimension 0
- grad_expand: float32 [512, 1024], P(('groups', 'dp')), parts along dimension 0
- grad_contract: float32 [2048, 256], P(('groups', 'dp')), parts along dimension 0
- grad_merge: float32 [1024, 256], P(('groups', 'dp')), parts along dimension 0
There are 2 independent parts, one for each index of `groups`. A program takes and returns all parts, laid end to end along the dimension named above; an argument that names none is the same for every part. Nothing has to cross between parts.
All inputs are finite; a program needn't handle non-finite values.
Results may differ from a plain program's by a relative error of at most 0.012.
Values may be sent and summed in bfloat16 or wider, within the bound.
No kernel may reach another device: no remote copies, remote signals or barrier semaphores. Data moves between devices by JAX's collectives and lax.ppermute only.
A program may use at most 64 MiB of HBM per device.

v0:
```python
import math

import jax
import jax.numpy as jnp
from jax import lax
from jax.sharding import PartitionSpec as P

KS = 7


def padded_2(x, sides, width, wrap):
    for axis, dim in sides:
        size, length = (lax.axis_size(axis), x.shape[dim])
        up = [(i, (i + 1) % size) for i in range(size if wrap else size - 1)]
        down = [(j, i) for i, j in up]
        last = lax.slice_in_dim(x, length - width, length, axis=dim)
        leading = lax.slice_in_dim(x, 0, width, axis=dim)
        before = lax.ppermute(last, axis, up)
        after = lax.ppermute(leading, axis, down)
        x = jnp.concatenate([before, x, after], axis=dim)
    return x


def normalize(values):
    centered = values - jnp.mean(values, axis=-1, keepdims=True)
    inverse = lax.rsqrt(jnp.mean(centered * centered, axis=-1, keepdims=True) + 1e-06)
    return (centered * inverse, inverse)


def norm_back(upstream, normed, inverse):
    return inverse * (
        upstream
        - jnp.mean(upstream, axis=-1, keepdims=True)
        - normed * jnp.mean(upstream * normed, axis=-1, keepdims=True)
    )


def gelu_slope(pre_act):
    return (
        0.5 * (1.0 + lax.erf(pre_act * 0.7071067811865476))
        + pre_act * jnp.exp(-0.5 * pre_act * pre_act) * 0.3989422804014327
    )


def extend(field):
    margin = KS // 2
    looped = padded_2(field, (("lon", 2),), margin, True)
    return padded_2(looped, (("lat", 1),), margin, False)


def depthwise(padded, kernel, lat_rows, lon_cols, flipped):
    total = jnp.zeros(padded.shape[:1] + (lat_rows, lon_cols, padded.shape[3]), jnp.float32)
    for kernel_row in range(KS):
        for kernel_col in range(KS):
            start_row = KS - 1 - kernel_row if flipped else kernel_row
            start_col = KS - 1 - kernel_col if flipped else kernel_col
            window = padded[
                :, start_row : start_row + lat_rows, start_col : start_col + lon_cols, :
            ].astype(jnp.float32)
            total = total + window * kernel[kernel_row * KS + kernel_col]
    return total


def kernel_terms(padded, upstream, lat_rows, lon_cols):
    terms = []
    for kernel_row in range(KS):
        for kernel_col in range(KS):
            window = padded[
                :, kernel_row : kernel_row + lat_rows, kernel_col : kernel_col + lon_cols, :
            ].astype(jnp.float32)
            terms.append(jnp.sum(window * upstream, axis=(0, 1, 2)))
    return jnp.stack(terms)


def inner_rows(left, right):
    return lax.dot_general(
        left, right, (((0,), (0,)), ((), ())), preferred_element_type=jnp.float32
    )


def body(fine_field, grad_out, conv_kernel, norm_gain, w_expand, w_contract, w_merge):
    samples, fine_rows, fine_cols, narrow = fine_field.shape
    lat_rows = fine_rows // 2
    lon_cols = fine_cols // 2
    channels = w_merge.shape[1]
    fine_unit, fine_inv = normalize(fine_field.astype(jnp.float32))
    fine_normed = fine_unit.astype(jnp.bfloat16)
    patches = (
        fine_normed.reshape(samples, lat_rows, 2, lon_cols, 2, narrow)
        .transpose(0, 1, 3, 2, 4, 5)
        .reshape(-1, 4 * narrow)
    )
    coarse = (
        jnp.dot(patches, w_merge, preferred_element_type=jnp.float32)
        .astype(jnp.bfloat16)
        .reshape(samples, lat_rows, lon_cols, channels)
    )
    padded = extend(coarse)
    mixed = depthwise(padded, conv_kernel, lat_rows, lon_cols, False)
    unit, inverse = normalize(mixed)
    normed = (unit * norm_gain).astype(jnp.bfloat16).reshape(-1, channels)
    pre_act = jnp.dot(normed, w_expand, preferred_element_type=jnp.float32)
    hidden = jax.nn.gelu(pre_act, approximate=False).astype(jnp.bfloat16)
    branch = jnp.dot(hidden, w_contract, preferred_element_type=jnp.float32)
    section_out = (
        (coarse.reshape(-1, channels).astype(jnp.float32) + branch)
        .astype(jnp.bfloat16)
        .reshape(samples, lat_rows, lon_cols, channels)
    )
    total_rows = lat_rows * lax.axis_size("lat")
    first_row = lax.axis_index("lat") * lat_rows
    latitude = math.pi * (
        ((first_row + jnp.arange(lat_rows, dtype=jnp.int32)).astype(jnp.float32) + 0.5) / total_rows
        - 0.5
    )
    weighted = (
        (grad_out.astype(jnp.float32) * jnp.cos(latitude)[None, :, None, None])
        .astype(jnp.bfloat16)
        .reshape(-1, channels)
    )
    term_contract = inner_rows(hidden, weighted)
    back_hidden = lax.dot_general(
        weighted, w_contract, (((1,), (1,)), ((), ())), preferred_element_type=jnp.float32
    )
    slope = (back_hidden * gelu_slope(pre_act)).astype(jnp.bfloat16)
    term_expand = inner_rows(normed, slope)
    back_normed = lax.dot_general(
        slope, w_expand, (((1,), (1,)), ((), ())), preferred_element_type=jnp.float32
    ).reshape(samples, lat_rows, lon_cols, channels)
    term_gain = jnp.sum(back_normed * unit, axis=(0, 1, 2))
    back_mixed = norm_back(back_normed * norm_gain, unit, inverse)
    term_kernel = kernel_terms(padded, back_mixed, lat_rows, lon_cols)
    back_low = back_mixed.astype(jnp.bfloat16)
    spread_back = depthwise(extend(back_low), conv_kernel, lat_rows, lon_cols, True)
    back_coarse = (
        (weighted.astype(jnp.float32).reshape(samples, lat_rows, lon_cols, channels) + spread_back)
        .astype(jnp.bfloat16)
        .reshape(-1, channels)
    )
    term_merge = inner_rows(patches, back_coarse)
    back_patch = lax.dot_general(
        back_coarse, w_merge, (((1,), (1,)), ((), ())), preferred_element_type=jnp.float32
    )
    back_fine = (
        back_patch.reshape(samples, lat_rows, lon_cols, 2, 2, narrow)
        .transpose(0, 1, 3, 2, 4, 5)
        .reshape(samples, fine_rows, fine_cols, narrow)
    )
    grad_fine = norm_back(back_fine, fine_unit, fine_inv).astype(jnp.bfloat16)
    kernel_side = jnp.transpose(term_kernel)
    owned = (
        lax.psum_scatter(
            term_expand.astype(jnp.bfloat16), "dp", scatter_dimension=0, tiled=True
        ).astype(jnp.float32),
        lax.psum_scatter(
            term_contract.astype(jnp.bfloat16), "dp", scatter_dimension=0, tiled=True
        ).astype(jnp.float32),
        lax.psum_scatter(
            term_merge.astype(jnp.bfloat16), "dp", scatter_dimension=0, tiled=True
        ).astype(jnp.float32),
        lax.psum_scatter(
            kernel_side.astype(jnp.bfloat16), "dp", scatter_dimension=0, tiled=True
        ).astype(jnp.float32),
        lax.psum_scatter(
            term_gain.astype(jnp.bfloat16), "dp", scatter_dimension=0, tiled=True
        ).astype(jnp.float32),
    )
    summed = lax.psum((owned[0], owned[1], owned[2], owned[3], owned[4]), ("lon", "lat"))
    all_cells = samples * lax.axis_size("dp") * total_rows * lon_cols * lax.axis_size("lon")
    factor = 1.0 / math.sqrt(all_cells)
    return (
        section_out,
        grad_fine,
        jnp.transpose(summed[3]) * factor,
        summed[4] * factor,
        summed[0] * factor,
        summed[1] * factor,
        summed[2] * factor,
    )


def solution(mesh):
    placed = (
        P(("groups", "dp"), "lat", "lon", None),
        P(("groups", "dp"), "lat", "lon", None),
        P(),
        P(),
        P(),
        P(),
        P(),
    )
    return jax.shard_map(
        body,
        mesh=mesh,
        in_specs=placed,
        out_specs=(
            P(("groups", "dp"), "lat", "lon", None),
            P(("groups", "dp"), "lat", "lon", None),
            P("groups", "dp"),
            P(("groups", "dp")),
            P(("groups", "dp"), None),
            P(("groups", "dp"), None),
            P(("groups", "dp"), None),
        ),
        check_vma=False,
    )
```

profile of v0, /device:TPU:0, one launch (start us, length us, event | category | flops | bytes accessed | tf_op | source)
XLA Modules:
  0.0 224.2 jit_solution(15273327608458585673)
XLA Ops:
  7.2 1.9 convert_reduce_fusion
  9.2 2.4 %fusion.25 = f32[2,64,32]{2,1,0:T(8,128)S(1)} fusion(bf16[2,64,32,128]{3,2,1,0:T(8,128)(2,1)} %param.7, f32[2,64,32]{2,1,0:T(8,128)S(1)} %broadcast_multiply_fusion.5), kind=kLoop, calls=%fused_computation.37 | loop fusion | flops 2093056 | bytes 1081344 | tf_op jit(solution)/shard_map/reduce_sum | solution.py:26
  11.6 2.3 %fusion.20 = bf16[2,64,32,128]{3,2,1,0:T(8,128)(2,1)S(1)} fusion(bf16[2,64,32,128]{3,2,1,0:T(8,128)(2,1)} %param.7, f32[2,64,32]{2,1,0:T(8,128)S(1)} %add_rsqrt_fusion, f32[2,64,32]{2,1,0:T(8,128)S(1)} %broadcast_multiply_fusion.5), kind=kLoop, calls=%fused_computation.32 | loop fusion | flops 2097152 | bytes 2129920 | tf_op jit(solution)/shard_map/convert_element_type | solution.py:87
  13.9 0.9 copy.33
  15.9 3.1 %collective-permute-start = (bf16[2,32,3,256]{3,2,1,0:T(4,128)(2,1)S(1)}, bf16[2,32,3,256]{3,2,1,0:T(4,128)(2,1)S(1)}, u32[]{:S(2)}, u32[]{:S(2)}) collective-permute-start(bf16[2,32,3,256]{3,2,1,0:T(4,128)(2,1)S(1)} %get-tuple-element.86), channel_id=1, source_target_pairs={{0,4},{4,8},{8,12},{12,0},{1,5},{5,9},{9,13},{13,1},{2,6},{6,10},{... | collective-permute-start | bytes 294920 | tf_op jit(solution)/shard_map/ppermute | solution.py:18
  19.0 2.1 collective-permute-start.1
  21.1 1.7 fusion.138
  23.2 1.1 fusion.137
  24.4 0.9 collective-permute-done
  25.3 1.4 collective-permute-done.1
  26.8 3.4 %collective-permute-start.2 = (bf16[2,3,22,256]{3,2,1,0:T(8,128)(2,1)S(1)}, bf16[2,3,22,256]{3,2,1,0:T(8,128)(2,1)S(1)}, u32[]{:S(2)}, u32[]{:S(2)}) collective-permute-start(bf16[2,3,22,256]{3,2,1,0:T(8,128)(2,1)S(1)} %get-tuple-element.82), channel_id=1, source_target_pairs={{0,2},{1,3},{4,6},{5,7},{8,10},{9,11},{12,14},{13,15},{16,18},{17,... | collective-permute-start | bytes 202760 | tf_op jit(solution)/shard_map/ppermute | solution.py:18
  30.2 1.5 collective-permute-start.3
  31.7 0.9 fusion.139
  32.8 3.7 %collective-permute-done.3 = bf16[2,3,22,256]{3,2,1,0:T(8,128)(2,1)S(1)} collective-permute-done((bf16[2,3,22,256]{3,2,1,0:T(8,128)(2,1)S(1)}, bf16[2,3,22,256]{3,2,1,0:T(8,128)(2,1)S(1)}, u32[]{:S(2)}, u32[]{:S(2)}) %collective-permute-start.3) | collective-permute-done | bytes 67616 | tf_op jit(solution)/shard_map/ppermute | solution.py:19
  37.2 10.5 %fusion.133 = (f32[2,32,16]{2,1,0:T(8,128)S(1)}, f32[2,32,16,256]{3,2,1,0:T(8,128)S(1)}) fusion(f32[256]{0:T(256)S(1)} %bitcast.212, bf16[2,35,22,256]{3,2,1,0:T(8,128)(2,1)S(1)} %get-tuple-element.81, f32[256]{0:T(256)S(1)} %bitcast.214, f32[256]{0:T(256)S(1)} %bitcast.158, f32[256]{0:T(256)S(1)} %bitcast.160, f32[256]{0:T(256)S(1)} %bitcast.162, ...), kind=kLoop, calls=%fused_computation.304 | loop fusion | flops 43252736 | bytes 23843840 | tf_op jit(solution)/shard_map/reduce_sum | solution.py:25
  48.8 10.7 %fusion.2 = (bf16[1024,1024]{1,0:T(8,128)(2,1)}, f32[1024,1024]{1,0:T(8,128)S(1)}) fusion(bf16[1024,256]{1,0:T(8,128)(2,1)S(1)} %bitcast.112, bf16[256,1024]{1,0:T(8,128)(2,1)S(1)} %copy-done), kind=kOutput, calls=%fused_computation.4 | convolution fusion | flops 605028352 | bytes 7340032 | tf_op jit(solution)/shard_map/dot_general | solution.py:102
  59.5 2.2 fusion.8
  61.7 1.3 copy-done.8
  63.0 1.7 multiply_reduce_fusion.2
  64.8 2.8 %multiply_reduce_fusion = (bf16[256]{0:T(256)(128)(2,1)}, f32[2,32,16]{2,1,0:T(8,128)S(1)}) fusion(f32[2,32,16,256]{3,2,1,0:T(8,128)S(1)} %get-tuple-element.74, f32[2,32,16]{2,1,0:T(8,128)S(1)} %add_rsqrt_fusion.1, f32[2,32,16]{2,1,0:T(8,128)S(1)} %broadcast_multiply_fusion.7, f32[1024,256]{1,0:T(8,128)} %get-tuple-element.140, ...), kind=kLoop, calls=%fused_computation.241 | loop fusion | flops 1833728 | bytes 3159552 | tf_op jit(solution)/shard_map/reduce_sum | solution.py:130
  68.7 1.4 div.41
  70.1 4.4 %fusion.123 = (bf16[256]{0:T(256)(128)(2,1)S(1)}, bf16[256]{0:T(256)(128)(2,1)S(1)}, bf16[256]{0:T(256)(128)(2,1)S(1)}, bf16[256]{0:T(256)(128)(2,1)S(1)}, bf16[...) fusion(bf16[2,35,22,256]{3,2,1,0:T(8,128)(2,1)S(1)} %get-tuple-, ...), kind=kLoop, calls=%fused_computation.239 | loop fusion | flops 15986176 | bytes 12609536 | tf_op jit(solution)/shard_map/reduce_sum | solution.py:71
  74.5 1.9 fusion.105
  76.6 1.2 collective-permute-start.4
  77.8 2.7 %collective-permute-start.5 = (bf16[2,32,3,256]{3,2,1,0:T(4,128)(2,1)S(1)}, bf16[2,32,3,256]{3,2,1,0:T(4,128)(2,1)S(1)}, u32[]{:S(2)}, u32[]{:S(2)}) collective-permute-start(bf16[2,32,3,256]{3,2,1,0:T(4,128)(2,1)S(1)} %get-tuple-element.84), channel_id=1, source_target_pairs={{4,0},{8,4},{12,8},{0,12},{5,1},{9,5},{13,9},{1,13},{6,2},{10,6},{... | collective-permute-start | bytes 294920 | tf_op jit(solution)/shard_map/ppermute | solution.py:19
  80.4 2.6 %fusion.72 = (bf16[256]{0:T(256)(128)(2,1)S(1)}, bf16[256]{0:T(256)(128)(2,1)S(1)}, bf16[256]{0:T(256)(128)(2,1)S(1)}, bf16[256]{0:T(256)(128)(2,1)S(1)}, bf16[2...) fusion(f32[2,32,16,256]{3,2,1,0:T(8,128)S(1)} %get-tuple-elemen, ...), kind=kLoop, calls=%fused_computation.188 | loop fusion | flops 14151168 | bytes 10494976 | tf_op jit(solution)/shard_map/reduce_sum | solution.py:71
  83.5 0.7 collective-permute-done.5
  84.3 1.3 collective-permute-start.6
  85.6 5.2 %collective-permute-start.7 = (bf16[2,3,22,256]{3,2,1,0:T(8,128)(2,1)S(1)}, bf16[2,3,22,256]{3,2,1,0:T(8,128)(2,1)}, u32[]{:S(2)}, u32[]{:S(2)}) collective-permute-start(bf16[2,3,22,256]{3,2,1,0:T(8,128)(2,1)S(1)} %get-tuple-element.79), channel_id=1, source_target_pairs={{0,2},{1,3},{4,6},{5,7},{8,10},{9,11},{12,14},{13,15},{16,18},{17,... | collective-permute-start | bytes 202760 | tf_op jit(solution)/shard_map/ppermute | solution.py:18
  92.0 0.7 copy.29
  93.5 1.4 pad_maximum_fusion.1
  94.9 9.0 %add_convert_fusion = bf16[2,32,16,256]{3,2,1,0:T(8,128)(2,1)S(1)} fusion(bf16[2,32,16,256]{3,2,1,0:T(8,128)(2,1)S(1)} %get-tuple-element.75, bf16[2,32,3,256]{3,2,1,0:T(4,128)(2,1)S(1)} %collective-permute-done.4, bf16[2,32,3,256]{3,2,1,0:T(4,128)(2,1)S(1)} %collective-permute-done.5, bf16[2,35,22,256]{3,2,1,0:T(8,128)(2,1)S(1)} %get-tuple-element.77, ...), kind=kLoop, calls=%fused_computation.242 | loop fusion | flops 44564480 | bytes 23839872 | tf_op jit(solution)/shard_map/convert_element_type | solution.py:137
  103.9 0.7 copy-done.11
  104.7 1.2 convolution_convert_fusion.3
  105.9 3.3 %convolution_convert_fusion.2 = bf16[256,1024]{1,0:T(8,128)(2,1)} fusion(bf16[1024,256]{1,0:T(8,128)(2,1)} %bitcast.113, bf16[1024,1024]{1,0:T(8,128)(2,1)} %copy-done.8), kind=kOutput, calls=%fused_computation.140 | convolution fusion | flops 537133056 | bytes 3145728 | tf_op jit(solution)/shard_map/dot_general | solution.py:76
  110.6 2.7 %all-reduce = bf16[256]{0:T(256)(128)(2,1)S(1)} all-reduce(bf16[256]{0:T(256)(128)(2,1)S(1)} %copy-done.76), channel_id=3, replica_groups=mesh['groups'=2,'lon'=4,'lat'=2,'dp'=2] {'dp'}, use_global_device_ids=true, to_apply=%region_60.0.clone | all-reduce | flops 256 | bytes 1024
  113.4 3.2 %convolution_convert_fusion.1 = bf16[1024,256]{1,0:T(8,128)(2,1)} fusion(bf16[1024,1024]{1,0:T(8,128)(2,1)} %get-tuple-element.137, bf16[1024,256]{1,0:T(8,128)(2,1)S(1)} %bitcast.116), kind=kOutput, calls=%fused_computation.139 | convolution fusion | flops 537133056 | bytes 3145728 | tf_op jit(solution)/shard_map/dot_general | solution.py:76
  116.6 3.2 %fusion.26 = bf16[1024,256]{1,0:T(8,128)(2,1)} fusion(bf16[1024,1024]{1,0:T(8,128)(2,1)} %get-tuple-element.137, bf16[1024,256]{1,0:T(8,128)(2,1)S(1)} %copy-done.78, bf16[1024,256]{1,0:T(8,128)(2,1)S(1)} %copy-done.4), kind=kOutput, calls=%fused_computation.141 | convolution fusion | flops 537657344 | bytes 3670016 | tf_op jit(solution)/shard_map/dot_general | solution.py:104
  119.8 0.8 copy.30
  120.7 1.0 fusion.140
  121.7 2.4 %copy.22 = f32[2,32,2,16,2,128]{5,4,3,2,1,0:T(2,128)} copy(f32[2,32,2,16,2,128]{5,3,4,2,1,0:T(8,128)S(1)} %get-tuple-element.142) | data formatting | bytes 4194304 | tf_op jit(solution)/shard_map/transpose | solution.py:146
  124.2 1.0 copy.28
  125.7 5.8 %fusion.21 = f32[2,64,32]{2,1,0:T(8,128)S(1)} fusion(f32[2,64,32,128]{3,2,1,0:T(8,128)} %bitcast.107, bf16[2,64,32,128]{3,2,1,0:T(8,128)(2,1)S(1)} %copy-done.1, f32[2,64,32]{2,1,0:T(8,128)S(1)} %copy-done.17, f32[2,64,32]{2,1,0:T(8,128)S(1)} %copy-done.15), kind=kLoop, calls=%fused_computation.33 | loop fusion | flops 2617344 | bytes 3194880 | tf_op jit(solution)/shard_map/reduce_sum | solution.py:34
  131.5 3.3 %fusion.24 = bf16[2,64,32,128]{3,2,1,0:T(8,128)(2,1)} fusion(bf16[2,64,32,128]{3,2,1,0:T(8,128)(2,1)S(1)} %copy-done.1, f32[2,64,32,128]{3,2,1,0:T(8,128)S(1)} %bitcast.108, f32[2,64,32]{2,1,0:T(8,128)S(1)} %broadcast_multiply_fusion.4, f32[2,64,32]{2,1,0:T(8,128)S(1)} %reshape.169, f32[2,64,32]{2,1,0:T(8,128)S(1)} %copy-done.17, f32[2,64,32]{2,1,0:T(8,128)S(1)} %copy-done.15), kind=kLoop, calls=%fused_computation.36 | loop fusion | flops 4194304 | bytes 4259840 | tf_op jit(solution)/shard_map/convert_element_type | solution.py:149
  134.8 1.9 reduce-scatter.9.cloned.1.call-done
  136.7 77.5 %all-reduce.3 = (f32[128,49]{0,1:T(8,128)S(1)}, f32[128]{0:T(128)S(1)}, f32[128,1024]{1,0:T(8,128)S(1)}, f32[512,256]{1,0:T(8,128)S(1)}, f32[256,256]{1,0:T(8,128)S(1)}) all-reduce(bf16[128,49]{0,1:T(8,128)(2,1)S(1)} %copy.30, f32[128]{0:T(128)S(1)} %dynamic-slice_convert_fusion, ...), channel_id=1, replica_groups=mesh['groups'=2,'lon'=4,'lat'=2,'dp'=2] {'lon','lat'}, use_global_device_ids=true, to_apply=%region_58.0 | all-reduce | flops 334080 | bytes 2004736 | tf_op jit(solution)/shard_map/psum | solution.py:168
  214.2 0.8 broadcast_multiply_fusion
  215.0 0.8 broadcast_multiply_fusion.1
  (250 shorter events, 9.6 us)
Async XLA Ops:
  7.2 41.6 %copy-start = (bf16[256,1024]{1,0:T(8,128)(2,1)S(1)}, bf16[256,1024]{1,0:T(8,128)(2,1)}, u32[]{:S(2)}) copy-start(bf16[256,1024]{1,0:T(8,128)(2,1)} %param.11) | copy-start | bytes 1572868
  7.2 112.6 %reduce-scatter.13.cloned.1.call-start = ((), (), s32[]{:S(2)}) async-start(), calls=%async_computation.7 | async-start | bytes 98304
  15.3 17.5 %copy-start.6 = (bf16[1024,512]{1,0:T(8,128)(2,1)}, bf16[1024,512]{1,0:T(8,128)(2,1)S(1)}, u32[]{:S(2)}) copy-start(bf16[1024,512]{1,0:T(8,128)(2,1)S(1)} %reshape.159) | copy-start | bytes 3145732
  15.8 21.2 %copy-start.2 = (bf16[1024,256]{1,0:T(8,128)(2,1)}, bf16[1024,256]{1,0:T(8,128)(2,1)S(1)}, u32[]{:S(2)}) copy-start(bf16[1024,256]{1,0:T(8,128)(2,1)S(1)} %convolution_convert_fusion) | copy-start | bytes 1572868
  15.9 9.4 %collective-permute-start = (bf16[2,32,3,256]{3,2,1,0:T(4,128)(2,1)S(1)}, bf16[2,32,3,256]{3,2,1,0:T(4,128)(2,1)S(1)}, u32[]{:S(2)}, u32[]{:S(2)}) collective-permute-start(bf16[2,32,3,256]{3,2,1,0:T(4,128)(2,1)S(1)} %get-tuple-element.86), channel_id=1, source_target_pairs={{0,4},{4,8},{8,12},{12,0},{1,5},{5,9},{9,13},{13,1},{2,6},{6,10},{... | collective-permute-start | bytes 294920 | tf_op jit(solution)/shard_map/ppermute | solution.py:18
  19.0 7.8 %collective-permute-start.1 = (bf16[2,32,3,256]{3,2,1,0:T(4,128)(2,1)S(1)}, bf16[2,32,3,256]{3,2,1,0:T(4,128)(2,1)S(1)}, u32[]{:S(2)}, u32[]{:S(2)}) collective-permute-start(bf16[2,32,3,256]{3,2,1,0:T(4,128)(2,1)S(1)} %get-tuple-element.87), channel_id=1, source_target_pairs={{4,0},{8,4},{12,8},{0,12},{5,1},{9,5},{13,9},{1,13},{6,2},{10,6},{... | collective-permute-start | bytes 294920 | tf_op jit(solution)/shard_map/ppermute | solution.py:19
  23.1 36.4 %copy-start.22 = (bf16[2,32,16,256]{3,2,1,0:T(8,128)(2,1)}, bf16[2,32,16,256]{3,2,1,0:T(8,128)(2,1)S(1)}, u32[]{:S(2)}) copy-start(bf16[2,32,16,256]{3,2,1,0:T(8,128)(2,1)S(1)} %multiply_convert_fusion) | copy-start | bytes 1572868
  24.2 23.4 %copy-start.45 = (f32[1,256]{1,0:T(1,128)}, f32[1,256]{1,0:T(1,128)S(1)}, u32[]{:S(2)}) copy-start(f32[1,256]{1,0:T(1,128)S(1)} %get-tuple-element.88) | copy-start | bytes 3076
  24.3 23.4 %copy-start.46 = (f32[1,256]{1,0:T(1,128)}, f32[1,256]{1,0:T(1,128)S(1)}, u32[]{:S(2)}) copy-start(f32[1,256]{1,0:T(1,128)S(1)} %get-tuple-element.89) | copy-start | bytes 3076
  24.3 23.4 %copy-start.47 = (f32[1,256]{1,0:T(1,128)}, f32[1,256]{1,0:T(1,128)S(1)}, u32[]{:S(2)}) copy-start(f32[1,256]{1,0:T(1,128)S(1)} %get-tuple-element.90) | copy-start | bytes 3076
  24.3 23.4 %copy-start.48 = (f32[1,256]{1,0:T(1,128)}, f32[1,256]{1,0:T(1,128)S(1)}, u32[]{:S(2)}) copy-start(f32[1,256]{1,0:T(1,128)S(1)} %get-tuple-element.91) | copy-start | bytes 3076
  24.3 23.4 %copy-start.49 = (f32[1,256]{1,0:T(1,128)}, f32[1,256]{1,0:T(1,128)S(1)}, u32[]{:S(2)}) copy-start(f32[1,256]{1,0:T(1,128)S(1)} %get-tuple-element.92) | copy-start | bytes 3076
  24.3 23.4 %copy-start.50 = (f32[1,256]{1,0:T(1,128)}, f32[1,256]{1,0:T(1,128)S(1)}, u32[]{:S(2)}) copy-start(f32[1,256]{1,0:T(1,128)S(1)} %get-tuple-element.93) | copy-start | bytes 3076
  24.3 23.4 %copy-start.51 = (f32[1,256]{1,0:T(1,128)}, f32[1,256]{1,0:T(1,128)S(1)}, u32[]{:S(2)}) copy-start(f32[1,256]{1,0:T(1,128)S(1)} %get-tuple-element.94) | copy-start | bytes 3076
  24.3 23.4 %copy-start.52 = (f32[1,256]{1,0:T(1,128)}, f32[1,256]{1,0:T(1,128)S(1)}, u32[]{:S(2)}) copy-start(f32[1,256]{1,0:T(1,128)S(1)} %get-tuple-element.95) | copy-start | bytes 3076
  24.3 23.4 %copy-start.53 = (f32[1,256]{1,0:T(1,128)}, f32[1,256]{1,0:T(1,128)S(1)}, u32[]{:S(2)}) copy-start(f32[1,256]{1,0:T(1,128)S(1)} %get-tuple-element.96) | copy-start | bytes 3076
  24.3 23.4 %copy-start.54 = (f32[1,256]{1,0:T(1,128)}, f32[1,256]{1,0:T(1,128)S(1)}, u32[]{:S(2)}) copy-start(f32[1,256]{1,0:T(1,128)S(1)} %get-tuple-element.97) | copy-start | bytes 3076
  24.3 23.4 %copy-start.55 = (f32[1,256]{1,0:T(1,128)}, f32[1,256]{1,0:T(1,128)S(1)}, u32[]{:S(2)}) copy-start(f32[1,256]{1,0:T(1,128)S(1)} %get-tuple-element.98) | copy-start | bytes 3076
  24.4 23.4 %copy-start.56 = (f32[1,256]{1,0:T(1,128)}, f32[1,256]{1,0:T(1,128)S(1)}, u32[]{:S(2)}) copy-start(f32[1,256]{1,0:T(1,128)S(1)} %get-tuple-element.99) | copy-start | bytes 3076
  24.4 23.4 %copy-start.57 = (f32[1,256]{1,0:T(1,128)}, f32[1,256]{1,0:T(1,128)S(1)}, u32[]{:S(2)}) copy-start(f32[1,256]{1,0:T(1,128)S(1)} %get-tuple-element.100) | copy-start | bytes 3076
  24.4 23.4 %copy-start.58 = (f32[1,256]{1,0:T(1,128)}, f32[1,256]{1,0:T(1,128)S(1)}, u32[]{:S(2)}) copy-start(f32[1,256]{1,0:T(1,128)S(1)} %get-tuple-element.101) | copy-start | bytes 3076
  24.4 23.4 %copy-start.59 = (f32[1,256]{1,0:T(1,128)}, f32[1,256]{1,0:T(1,128)S(1)}, u32[]{:S(2)}) copy-start(f32[1,256]{1,0:T(1,128)S(1)} %get-tuple-element.102) | copy-start | bytes 3076
  24.4 23.4 %copy-start.60 = (f32[1,256]{1,0:T(1,128)}, f32[1,256]{1,0:T(1,128)S(1)}, u32[]{:S(2)}) copy-start(f32[1,256]{1,0:T(1,128)S(1)} %get-tuple-element.103) | copy-start | bytes 3076
  24.4 23.4 %copy-start.61 = (f32[1,256]{1,0:T(1,128)}, f32[1,256]{1,0:T(1,128)S(1)}, u32[]{:S(2)}) copy-start(f32[1,256]{1,0:T(1,128)S(1)} %get-tuple-element.104) | copy-start | bytes 3076
  24.4 23.4 %copy-start.62 = (f32[1,256]{1,0:T(1,128)}, f32[1,256]{1,0:T(1,128)S(1)}, u32[]{:S(2)}) copy-start(f32[1,256]{1,0:T(1,128)S(1)} %get-tuple-element.105) | copy-start | bytes 3076
  24.4 23.4 %copy-start.63 = (f32[1,256]{1,0:T(1,128)}, f32[1,256]{1,0:T(1,128)S(1)}, u32[]{:S(2)}) copy-start(f32[1,256]{1,0:T(1,128)S(1)} %get-tuple-element.106) | copy-start | bytes 3076
  26.8 5.9 %collective-permute-start.2 = (bf16[2,3,22,256]{3,2,1,0:T(8,128)(2,1)S(1)}, bf16[2,3,22,256]{3,2,1,0:T(8,128)(2,1)S(1)}, u32[]{:S(2)}, u32[]{:S(2)}) collective-permute-start(bf16[2,3,22,256]{3,2,1,0:T(8,128)(2,1)S(1)} %get-tuple-element.82), channel_id=1, source_target_pairs={{0,2},{1,3},{4,6},{5,7},{8,10},{9,11},{12,14},{13,15},{16,18},{17,... | collective-permute-start | bytes 202760 | tf_op jit(solution)/shard_map/ppermute | solution.py:18
  30.2 6.2 %collective-permute-start.3 = (bf16[2,3,22,256]{3,2,1,0:T(8,128)(2,1)S(1)}, bf16[2,3,22,256]{3,2,1,0:T(8,128)(2,1)S(1)}, u32[]{:S(2)}, u32[]{:S(2)}) collective-permute-start(bf16[2,3,22,256]{3,2,1,0:T(8,128)(2,1)S(1)} %get-tuple-element.83), channel_id=1, source_target_pairs={{2,0},{3,1},{6,4},{7,5},{10,8},{11,9},{14,12},{15,13},{18,16},{19,... | collective-permute-start | bytes 202760 | tf_op jit(solution)/shard_map/ppermute | solution.py:19
  32.6 15.2 %copy-start.64 = (f32[1,256]{1,0:T(1,128)}, f32[1,256]{1,0:T(1,128)S(1)}, u32[]{:S(2)}) copy-start(f32[1,256]{1,0:T(1,128)S(1)} %get-tuple-element.126) | copy-start | bytes 3076
  32.6 15.2 %copy-start.65 = (f32[1,256]{1,0:T(1,128)}, f32[1,256]{1,0:T(1,128)S(1)}, u32[]{:S(2)}) copy-start(f32[1,256]{1,0:T(1,128)S(1)} %get-tuple-element.127) | copy-start | bytes 3076
  32.6 15.2 %copy-start.66 = (f32[1,256]{1,0:T(1,128)}, f32[1,256]{1,0:T(1,128)S(1)}, u32[]{:S(2)}) copy-start(f32[1,256]{1,0:T(1,128)S(1)} %get-tuple-element.128) | copy-start | bytes 3076
  32.7 15.2 %copy-start.67 = (f32[1,256]{1,0:T(1,128)}, f32[1,256]{1,0:T(1,128)S(1)}, u32[]{:S(2)}) copy-start(f32[1,256]{1,0:T(1,128)S(1)} %get-tuple-element.129) | copy-start | bytes 3076
  32.7 15.2 %copy-start.68 = (f32[1,256]{1,0:T(1,128)}, f32[1,256]{1,0:T(1,128)S(1)}, u32[]{:S(2)}) copy-start(f32[1,256]{1,0:T(1,128)S(1)} %get-tuple-element.130) | copy-start | bytes 3076
  32.7 15.2 %copy-start.69 = (f32[1,256]{1,0:T(1,128)}, f32[1,256]{1,0:T(1,128)S(1)}, u32[]{:S(2)}) copy-start(f32[1,256]{1,0:T(1,128)S(1)} %get-tuple-element.131) | copy-start | bytes 3076
  32.7 15.2 %copy-start.70 = (f32[1,256]{1,0:T(1,128)}, f32[1,256]{1,0:T(1,128)S(1)}, u32[]{:S(2)}) copy-start(f32[1,256]{1,0:T(1,128)S(1)} %get-tuple-element.132) | copy-start | bytes 3076
  32.7 15.2 %copy-start.71 = (f32[1,256]{1,0:T(1,128)}, f32[1,256]{1,0:T(1,128)S(1)}, u32[]{:S(2)}) copy-start(f32[1,256]{1,0:T(1,128)S(1)} %get-tuple-element.133) | copy-start | bytes 3076
  32.7 15.2 %copy-start.72 = (f32[1,256]{1,0:T(1,128)}, f32[1,256]{1,0:T(1,128)S(1)}, u32[]{:S(2)}) copy-start(f32[1,256]{1,0:T(1,128)S(1)} %get-tuple-element.134) | copy-start | bytes 3076
  32.7 15.2 %copy-start.73 = (f32[1,256]{1,0:T(1,128)}, f32[1,256]{1,0:T(1,128)S(1)}, u32[]{:S(2)}) copy-start(f32[1,256]{1,0:T(1,128)S(1)} %get-tuple-element.135) | copy-start | bytes 3076
  32.7 15.2 %copy-start.74 = (f32[1,256]{1,0:T(1,128)}, f32[1,256]{1,0:T(1,128)S(1)}, u32[]{:S(2)}) copy-start(f32[1,256]{1,0:T(1,128)S(1)} %get-tuple-element.136) | copy-start | bytes 3076
  48.0 16.8 %copy-start.20 = (f32[2,32,16]{2,1,0:T(8,128)}, f32[2,32,16]{2,1,0:T(8,128)S(1)}, u32[]{:S(2)}) copy-start(f32[2,32,16]{2,1,0:T(8,128)S(1)} %broadcast_multiply_fusion.7) | copy-start | bytes 12292
  48.4 16.3 %copy-start.21 = (f32[2,32,16]{2,1,0:T(8,128)}, f32[2,32,16]{2,1,0:T(8,128)S(1)}, u32[]{:S(2)}) copy-start(f32[2,32,16]{2,1,0:T(8,128)S(1)} %add_rsqrt_fusion.1) | copy-start | bytes 12292
  76.6 7.0 %collective-permute-start.4 = (bf16[2,32,3,256]{3,2,1,0:T(4,128)(2,1)S(1)}, bf16[2,32,3,256]{3,2,1,0:T(4,128)(2,1)S(1)}, u32[]{:S(2)}, u32[]{:S(2)}) collective-permute-start(bf16[2,32,3,256]{3,2,1,0:T(4,128)(2,1)S(1)} %get-tuple-element.85), channel_id=1, source_target_pairs={{0,4},{4,8},{8,12},{12,0},{1,5},{5,9},{9,13},{13,1},{2,6},{6,10},{... | collective-permute-start | bytes 294920 | tf_op jit(solution)/shard_map/ppermute | solution.py:18
  77.8 6.5 %collective-permute-start.5 = (bf16[2,32,3,256]{3,2,1,0:T(4,128)(2,1)S(1)}, bf16[2,32,3,256]{3,2,1,0:T(4,128)(2,1)S(1)}, u32[]{:S(2)}, u32[]{:S(2)}) collective-permute-start(bf16[2,32,3,256]{3,2,1,0:T(4,128)(2,1)S(1)} %get-tuple-element.84), channel_id=1, source_target_pairs={{4,0},{8,4},{12,8},{0,12},{5,1},{9,5},{13,9},{1,13},{6,2},{10,6},{... | collective-permute-start | bytes 294920 | tf_op jit(solution)/shard_map/ppermute | solution.py:19
  84.3 8.5 %collective-permute-start.6 = (bf16[2,3,22,256]{3,2,1,0:T(8,128)(2,1)S(1)}, bf16[2,3,22,256]{3,2,1,0:T(8,128)(2,1)S(1)}, u32[]{:S(2)}, u32[]{:S(2)}) collective-permute-start(bf16[2,3,22,256]{3,2,1,0:T(8,128)(2,1)S(1)} %get-tuple-element.78), channel_id=1, source_target_pairs={{2,0},{3,1},{6,4},{7,5},{10,8},{11,9},{14,12},{15,13},{18,16},{19,... | collective-permute-start | bytes 202760 | tf_op jit(solution)/shard_map/ppermute | solution.py:19
  85.6 7.8 %collective-permute-start.7 = (bf16[2,3,22,256]{3,2,1,0:T(8,128)(2,1)S(1)}, bf16[2,3,22,256]{3,2,1,0:T(8,128)(2,1)}, u32[]{:S(2)}, u32[]{:S(2)}) collective-permute-start(bf16[2,3,22,256]{3,2,1,0:T(8,128)(2,1)S(1)} %get-tuple-element.79), channel_id=1, source_target_pairs={{0,2},{1,3},{4,6},{5,7},{8,10},{9,11},{12,14},{13,15},{16,18},{17,... | collective-permute-start | bytes 202760 | tf_op jit(solution)/shard_map/ppermute | solution.py:18
  92.8 42.1 %reduce-scatter.11.cloned.1.call-start = ((), (), s32[]{:S(2)}) async-start(), calls=%async_computation.6 | async-start | bytes 393216 | tf_op jit(solution)/shard_map/reduce_scatter | solution.py:158
  105.9 29.0 %reduce-scatter.7.cloned.1.call-start = ((), (), s32[]{:S(2)}) async-start(), calls=%async_computation.4 | async-start | bytes 786432 | tf_op jit(solution)/shard_map/reduce_scatter | solution.py:152
  109.3 27.5 %reduce-scatter.9.cloned.1.call-start = ((), (), s32[]{:S(2)}) async-start(), calls=%async_computation.5 | async-start | bytes 786432 | tf_op jit(solution)/shard_map/reduce_scatter | solution.py:155
  (44 other events, 440.3 us)
Sparse Core Ops, SparseCore 0:
  92.9 7.1 reduce-scatter.12
  106.0 7.9 reduce-scatter.10
  116.3 9.1 reduce-scatter.6
  127.6 9.0 reduce-scatter.8
where the time goes:
time: 225 us; the launch traced here: 224 us
  blocking collectives  80.2 us (36%)
  other arithmetic  55.1 us (24%)
  matrix products  26.8 us (12%)
  starting transfers between devices  20.6 us (9%)
  local copies, waits for them, and re-layouts  16.2 us (7%)
  between operations  16.2 us (7%)
  waiting for transfers between devices  9.21 us (4%)
    psum x1, blocking collectives, body(): lax.psum((owned[0], owned[1], owned[2], owned[3], owned[4]), ('lon', 'lat'))  77.5 us
    ppermute x4, starting transfers between devices, padded_2(): before = lax.ppermute(last, axis, up)  12.9 us
    reduce_sum x2, other arithmetic, normalize(): centered = values - jnp.mean(values, axis=-1, keepdims=True)  12.4 us
    dot_general x1, matrix products, body(): pre_act = jnp.dot(normed, w_expand, preferred_element_type=jnp.float32)  10.7 us
    reduce_sum x4, other arithmetic, kernel_terms(): terms.append(jnp.sum(window * upstream, axis=(0, 1, 2)))  9.32 us
    convert_element_type x1, other arithmetic, body(): back_coarse = (weighted.astype(jnp.float32).reshape(samples, lat_rows, lo...  8.96 us
    dot_general x3, matrix products, inner_rows(): lax.dot_general(left, right, (((0,), (0,)), ((), ())), preferred_element_...  7.65 us
    ppermute x4, starting transfers between devices, padded_2(): after = lax.ppermute(leading, axis, down)  7.51 us
  transfers between devices with their start and end apart: 12, of which 6 were waited for; matrix products, arithmetic and copies ran while one was open for 20% of the time, Pallas kernels for 0%

commit v1 on v0

v1 whole, which is shorter than its diff:
```python
import functools
import math

import jax
import jax.numpy as jnp
from jax import lax
from jax.experimental import pallas as pl
from jax.experimental.pallas import tpu as pltpu
from jax.sharding import PartitionSpec as P

KS = 7
M = KS // 2
SUB = 8
LANE = 128
F32 = jnp.float32
BF16 = jnp.bfloat16


def kernel_call(fn, outs, args, scratch=(), flops=0):
    whole = pl.BlockSpec(memory_space=pltpu.VMEM)
    return pl.pallas_call(
        fn,
        out_shape=[jax.ShapeDtypeStruct(s, d) for s, d in outs],
        in_specs=[whole] * len(args),
        out_specs=[whole] * len(outs),
        scratch_shapes=[pltpu.VMEM(s, d) for s, d in scratch],
        compiler_params=pltpu.CompilerParams(vmem_limit_bytes=40 * 2**20),
        cost_estimate=pl.CostEstimate(
            flops=flops, bytes_accessed=sum(a.size * a.dtype.itemsize for a in args), transcendentals=0
        ),
    )(*args)


def rows(start, size):
    return pl.ds(start if isinstance(start, int) else pl.multiple_of(start, size & -size), size)


def dot(a, b):
    return jnp.dot(a, b, preferred_element_type=F32)


def dot_nt(a, b):
    return lax.dot_general(a, b, (((1,), (1,)), ((), ())), preferred_element_type=F32)


def dot_tn(a, b):
    return lax.dot_general(a, b, (((0,), (0,)), ((), ())), preferred_element_type=F32)


class Sizes:
    def __init__(self, fine_field, w_merge, w_expand):
        self.samples, fine_rows, fine_cols, self.narrow = fine_field.shape
        self.lat_rows, self.cols = fine_rows // 2, fine_cols // 2
        self.channels, self.wide = w_merge.shape[1], w_expand.shape[1]
        self.blocks = SUB // self.samples
        self.block_rows = self.lat_rows // self.blocks
        self.col = self.block_rows * SUB
        self.pad_rows = self.block_rows + 2 * M
        self.pad_col = self.pad_rows * SUB
        self.cells = self.cols * self.col
        self.fine = 4 * self.cells
        self.fine_stride = 2 * self.block_rows * fine_cols
        self.fine_cols = fine_cols
        self.halves = self.channels // LANE


def fine_stats(z, x):
    ones = jnp.full((z.narrow, z.narrow), 1.0 / z.narrow, BF16)
    centered = x.astype(F32) - dot(x, ones)
    inverse = lax.rsqrt(dot((centered * centered).astype(BF16), ones) + 1e-06)
    return centered * inverse, inverse


def fine_rows_of(z, j, i, p, q):
    return pl.ds((2 * i + p) * z.fine_cols + 2 * j + q, SUB, stride=z.fine_stride)


def edge_rows(z, scratch, before_ref, after_ref):
    for ref, first_row, block in ((after_ref, 0, 0), (before_ref, z.block_rows - M, z.blocks - 1)):
        parts = []
        for r in range(M):
            for s in range(z.samples):
                start = (first_row + r) * SUB + s * z.blocks + block
                parts.append(
                    jnp.concatenate(
                        [scratch[h, pl.ds(start, z.cols, stride=z.col), :] for h in range(z.halves)], axis=1
                    )
                )
        ref[...] = jnp.concatenate(parts, axis=0).astype(BF16)


def merge_kernel(z, fine_ref, w_ref, patches_ref, coarse_ref, last_ref, first_ref, unit_s, split_s):
    def norm_step(t, _):
        at = rows(t * 512, 512)
        unit_s[at, :] = fine_stats(z, fine_ref[at, :])[0]
        return 0

    lax.fori_loop(0, z.fine // 512, norm_step, 0)
    group = 4

    def step(g, _):
        for jj in range(group):
            j = g * group + jj
            quarters = []
            for p in range(2):
                for q in range(2):
                    quarters.append(
                        jnp.concatenate(
                            [unit_s[fine_rows_of(z, j, i, p, q), :] for i in range(z.block_rows)], axis=0
                        ).astype(BF16)
                    )
            patches_ref[rows(j * z.col, z.col), :] = jnp.concatenate(quarters, axis=1)
        at = rows(g * group * z.col, group * z.col)
        low = dot(patches_ref[at, :], w_ref[...]).astype(BF16)
        coarse_ref[at, :] = low
        for h in range(z.halves):
            split_s[h, at, :] = low[:, h * LANE : (h + 1) * LANE].astype(F32)
        return 0

    lax.fori_loop(0, z.cols // group, step, 0)
    edge_rows(z, split_s, last_ref, first_ref)


def weighted_kernel(z, grad_ref, cos_ref, out_ref, split_s):
    for h in range(z.halves):
        split_s[h, :, :] = grad_ref[:, h * LANE : (h + 1) * LANE].astype(F32)

    def step(j, _):
        for h in range(z.halves):
            col = jnp.concatenate(
                [
                    split_s[h, pl.ds(i * z.cols + j, SUB, stride=z.block_rows * z.cols), :]
                    for i in range(z.block_rows)
                ],
                axis=0,
            )
            out_ref[rows(j * z.col, z.col), h * LANE : (h + 1) * LANE] = (col * cos_ref[...]).astype(BF16)
        return 0

    lax.fori_loop(0, z.cols, step, 0)


def pad_kernel(z, lats, own_ref, before_ref, after_ref, pad_ref, left_ref, right_ref, halo_s):
    lat = lax.axis_index("lat")
    near = z.samples * M * z.cols
    halo_s[0:near, :] = jnp.where(lat > 0, before_ref[...].astype(F32), 0.0)
    halo_s[near : 2 * near, :] = jnp.where(lat < lats - 1, after_ref[...].astype(F32), 0.0)
    place = lax.broadcasted_iota(jnp.int32, (SUB, z.channels), 0)

    def halo(base, r, j, block, inner):
        for s in range(z.samples):
            line = halo_s[pl.ds(base + (r * z.samples + s) * z.cols + j, 1), :]
            inner = jnp.where(place == s * z.blocks + block, line, inner)
        return inner

    def step(j, _):
        own = own_ref[rows(j * z.col, z.col), :].astype(F32)
        pad_ref[rows(j * z.pad_col + M * SUB, SUB * z.block_rows), :] = own
        for r in range(M):
            i = z.block_rows - M + r
            up = pltpu.roll(own[i * SUB : (i + 1) * SUB], 1, 0)
            down = pltpu.roll(own[r * SUB : (r + 1) * SUB], SUB - 1, 0)
            pad_ref[rows(j * z.pad_col + r * SUB, SUB), :] = halo(0, r, j, 0, up)
            pad_ref[rows(j * z.pad_col + (M + z.block_rows + r) * SUB, SUB), :] = halo(
                near, r, j, z.blocks - 1, down
            )
        return 0

    lax.fori_loop(0, z.cols, step, 0)
    edge = M * z.pad_col
    left_ref[...] = pad_ref[0:edge, :].astype(BF16)
    right_ref[...] = pad_ref[z.cols * z.pad_col - edge :, :].astype(BF16)


def taps(z, pad, taps_s, start, h, flipped):
    lanes = slice(h * LANE, (h + 1) * LANE)
    total = jnp.zeros((z.block_rows, SUB, LANE), F32)
    for e in range(KS):
        column = pad[rows((start + e) * z.pad_col, z.pad_col), lanes].reshape(z.pad_rows, SUB, LANE)
        for a in range(KS):
            t = a * KS + e
            t = KS * KS - 1 - t if flipped else t
            total = total + column[a : a + z.block_rows] * taps_s[t * SUB : (t + 1) * SUB, lanes]
    return total.reshape(z.col, LANE)


def spread_taps(z, kern_ref, taps_s):
    for t in range(KS * KS):
        taps_s[t * SUB : (t + 1) * SUB, :] = jnp.broadcast_to(kern_ref[t : t + 1, :], (SUB, z.channels))


def gelu_parts(x):
    t = 1.0 / (1.0 + jnp.abs(x) * (0.3275911 * 0.7071067811865476))
    bell = jnp.exp(-0.5 * x * x)
    poly = 0.5 * 1.061405429
    for c in (-1.453152027, 1.421413741, -0.284496736, 0.254829592):
        poly = poly * t + 0.5 * c
    tail = poly * t * bell
    return jnp.where(x >= 0, 1.0 - tail, tail), x * bell * 0.3989422804014327


def row_mean(z, x):
    return jnp.sum(x, axis=-1, keepdims=True) * (1.0 / z.channels)


def section(z, pad, sources, groups, refs, scratch, chunk, section_ref, mixed_ref, taps_s):
    gain_ref, we_ref, wc_ref, coarse_ref, weighted_ref = refs
    unit_s, inv_s, normed_s, hidden_s, slope_s, weighted_s = scratch
    count = sum(g[2] for g in groups)

    def step(j, _):
        parts = [taps(z, pad, taps_s, sources(j), h, False) for h in range(z.halves)]
        at = rows(j * z.col, z.col)
        mean = sum(jnp.sum(p, axis=-1, keepdims=True) for p in parts) * (1.0 / z.channels)
        parts = [p - mean for p in parts]
        var = sum(jnp.sum(p * p, axis=-1, keepdims=True) for p in parts) * (1.0 / z.channels)
        inverse = lax.rsqrt(var + 1e-06)
        inv_s[at, :] = jnp.broadcast_to(inverse, (z.col, LANE))
        for h, p in enumerate(parts):
            lanes = slice(h * LANE, (h + 1) * LANE)
            unit = p * inverse
            unit_s[at, lanes] = unit
            normed_s[at, lanes] = (unit * gain_ref[:, lanes]).astype(BF16)
        return 0

    lax.fori_loop(0, count // z.col, step, 0)
    for low, full, size in groups:
        weighted_s[low : low + size, :] = weighted_ref[full : full + size, :]
    gain_sum = jnp.zeros((SUB, z.channels), F32)
    for low, full, size in groups:
        for c in range(size // chunk):
            at = slice(low + c * chunk, low + (c + 1) * chunk)
            place = slice(full + c * chunk, full + (c + 1) * chunk)
            part = 256
            for f in range(z.wide // part):
                cut = slice(f * part, (f + 1) * part)
                pre = dot(normed_s[at, :], we_ref[:, cut])
                back = dot_nt(weighted_s[at, :], wc_ref[cut, :])
                phi, density = gelu_parts(pre)
                hidden_s[at, cut] = (pre * phi).astype(BF16)
                slope_s[at, cut] = (back * (phi + density)).astype(BF16)
            branch = dot(hidden_s[at, :], wc_ref[...])
            section_ref[at, :] = (coarse_ref[place, :].astype(F32) + branch).astype(BF16)
            back = dot_nt(slope_s[at, :], we_ref[...])
            unit = unit_s[at, :]
            gain_sum = gain_sum + jnp.sum((back * unit).reshape(-1, SUB, z.channels), axis=0)
            back = back * gain_ref[...]
            inverse = jnp.concatenate([inv_s[at, :]] * z.halves, axis=1)
            mixed_ref[at, :] = inverse * (back - row_mean(z, back) - unit * row_mean(z, back * unit))
    return gain_sum


def inner_kernel(
    z, pad_ref, kern_ref, gain_ref, we_ref, wc_ref, coarse_ref, weighted_ref,
    section_ref, mixed_ref, expand_ref, contract_ref, gain_sum_ref, taps_s, *scratch,
):
    spread_taps(z, kern_ref, taps_s)
    size = (z.cols - 2 * M) * z.col
    refs = (gain_ref, we_ref, wc_ref, coarse_ref, weighted_ref)
    gain_sum_ref[...] = section(
        z, pad_ref, lambda j: j, [(0, M * z.col, size)], refs, scratch, size // 2, section_ref, mixed_ref, taps_s
    )
    unit_s, inv_s, normed_s, hidden_s, slope_s, weighted_s = scratch
    expand_ref[...] = dot_tn(normed_s[...], slope_s[...])
    contract_ref[...] = dot_tn(weighted_s[...], hidden_s[...])


def outer_kernel(
    z, pad_ref, left_ref, right_ref, kern_ref, gain_ref, we_ref, wc_ref, coarse_ref, weighted_ref,
    expand_ref, contract_ref, gain_sum_ref, inner_mixed_ref,
    section_ref, mixed_ref, mine_ref, other_ref, low_ref, last_ref, first_ref, gain_out_ref,
    taps_s, edge_s, sum_s, split_s, *scratch,
):
    spread_taps(z, kern_ref, taps_s)
    edge, near = M * z.pad_col, 2 * M * z.pad_col
    edge_s[0:edge, :] = left_ref[...].astype(F32)
    edge_s[edge : edge + near, :] = pad_ref[0:near, :]
    edge_s[edge + near : edge + 2 * near, :] = pad_ref[z.cols * z.pad_col - near :, :]
    edge_s[edge + 2 * near :, :] = right_ref[...].astype(F32)
    size = M * z.col
    refs = (gain_ref, we_ref, wc_ref, coarse_ref, weighted_ref)
    groups = [(0, 0, size), (size, z.cells - size, size)]
    gain_sum = section(
        z, edge_s, lambda j: jnp.where(j < M, j, j + 2 * M), groups, refs, scratch, size, section_ref, mixed_ref, taps_s
    )
    unit_s, inv_s, normed_s, hidden_s, slope_s, weighted_s = scratch
    gain_out_ref[...] = gain_sum + gain_sum_ref[...]
    sum_s[0, :, :] = expand_ref[...] + dot_tn(normed_s[...], slope_s[...])
    sum_s[1, :, :] = contract_ref[...] + dot_tn(weighted_s[...], hidden_s[...])
    own = lax.axis_index("dp")
    half, cut = z.channels // 2, z.wide // 2
    for ref, owner in ((mine_ref, own), (other_ref, 1 - own)):
        ref[0:half, :] = sum_s[0, rows(owner * half, half), :].astype(BF16)
        for t in range(2):
            ref[half:, t * cut : (t + 1) * cut] = sum_s[1, t * half : (t + 1) * half, rows(owner * cut, cut)].astype(
                BF16
            )
    low_ref[0:size, :] = mixed_ref[0:size, :].astype(BF16)
    low_ref[size : z.cells - size, :] = inner_mixed_ref[...].astype(BF16)
    low_ref[z.cells - size :, :] = mixed_ref[size:, :].astype(BF16)
    for h in range(z.halves):
        split_s[h, :, :] = low_ref[:, h * LANE : (h + 1) * LANE].astype(F32)
    edge_rows(z, split_s, last_ref, first_ref)


def terms_kernel(z, pad_ref, left_ref, right_ref, inner_ref, outer_ref, gain_ref, out_ref, full_s, mixed_s):
    edge = M * z.pad_col
    full_s[0:edge, :] = left_ref[...].astype(F32)
    full_s[edge : edge + z.cols * z.pad_col, :] = pad_ref[...]
    full_s[edge + z.cols * z.pad_col :, :] = right_ref[...].astype(F32)
    size = M * z.col
    mixed_s[0:size, :] = outer_ref[0:size, :]
    mixed_s[size : z.cells - size, :] = inner_ref[...]
    mixed_s[z.cells - size :, :] = outer_ref[size:, :]
    out_ref[...] = jnp.zeros_like(out_ref)
    for h in range(z.halves):
        lanes = slice(h * LANE, (h + 1) * LANE)
        for e in range(KS):

            def step(j, sums):
                column = full_s[rows((j + e) * z.pad_col, z.pad_col), lanes].reshape(z.pad_rows, SUB, LANE)
                back = mixed_s[rows(j * z.col, z.col), lanes].reshape(z.block_rows, SUB, LANE)
                return tuple(
                    sums[a] + jnp.sum(column[a : a + z.block_rows] * back, axis=0) for a in range(KS)
                )

            sums = lax.fori_loop(0, z.cols, step, tuple(jnp.zeros((SUB, LANE), F32) for _ in range(KS)))
            for a in range(KS):
                t = a * KS + e
                out_ref[t : t + 1, lanes] = jnp.sum(sums[a], axis=0, keepdims=True)
    out_ref[KS * KS : KS * KS + 1, :] = jnp.sum(gain_ref[...], axis=0, keepdims=True)


def back_kernel(
    z, pad_ref, left_ref, right_ref, kern_ref, weighted_ref, patches_ref, aux_ref,
    coarse_ref, mine_ref, other_ref, taps_s, full_s, sum_s,
):
    spread_taps(z, kern_ref, taps_s)
    edge = M * z.pad_col
    full_s[0:edge, :] = left_ref[...].astype(F32)
    full_s[edge : edge + z.cols * z.pad_col, :] = pad_ref[...]
    full_s[edge + z.cols * z.pad_col :, :] = right_ref[...].astype(F32)

    def step(j, _):
        at = rows(j * z.col, z.col)
        for h in range(z.halves):
            lanes = slice(h * LANE, (h + 1) * LANE)
            spread = taps(z, full_s, taps_s, j, h, True)
            coarse_ref[at, lanes] = (weighted_ref[at, lanes].astype(F32) + spread).astype(BF16)
        return 0

    lax.fori_loop(0, z.cols, step, 0)
    sum_s[...] = dot_tn(coarse_ref[...], patches_ref[...])
    own = lax.axis_index("dp")
    cut, depth = 2 * z.narrow, aux_ref.shape[0] // 2
    half = z.channels // 2
    for ref, owner in ((mine_ref, own), (other_ref, 1 - own)):
        ref[0 : z.channels, :] = sum_s[:, rows(owner * cut, cut)].astype(BF16)
        for t in range(2):
            ref[z.channels :, t * half : (t + 1) * half] = aux_ref[
                t * depth : (t + 1) * depth, rows(owner * half, half)
            ].astype(BF16)


def fine_kernel(z, coarse_ref, w_ref, fine_ref, out_ref, back_s):
    group = 4

    def step(g, _):
        back = dot_nt(coarse_ref[rows(g * group * z.col, group * z.col), :], w_ref[...])
        for jj in range(group):
            j = g * group + jj
            for p in range(2):
                for q in range(2):
                    lanes = slice((p * 2 + q) * z.narrow, (p * 2 + q + 1) * z.narrow)
                    for i in range(z.block_rows):
                        first = jj * z.col + i * SUB
                        back_s[fine_rows_of(z, j, i, p, q), :] = back[first : first + SUB, lanes]
        return 0

    lax.fori_loop(0, z.cols // group, step, 0)
    ones = jnp.full((z.narrow, z.narrow), 1.0 / z.narrow, BF16)

    def mean(x):
        high = x.astype(BF16)
        return dot(high, ones) + dot((x - high.astype(F32)).astype(BF16), ones)

    def norm_step(t, _):
        at = rows(t * 512, 512)
        unit, inverse = fine_stats(z, fine_ref[at, :])
        back = back_s[at, :]
        out_ref[at, :] = (inverse * (back - mean(back) - unit * mean(back * unit))).astype(BF16)
        return 0

    lax.fori_loop(0, z.fine // 512, norm_step, 0)


def section_kernel(z, inner_ref, outer_ref, out_ref, all_s, split_s):
    size = M * z.col
    all_s[0:size, :] = outer_ref[0:size, :].astype(F32)
    all_s[size : z.cells - size, :] = inner_ref[...].astype(F32)
    all_s[z.cells - size :, :] = outer_ref[size:, :].astype(F32)

    def step(j, _):
        for h in range(z.halves):
            for i in range(z.block_rows):
                split_s[h, pl.ds(i * z.cols + j, SUB, stride=z.block_rows * z.cols), :] = all_s[
                    rows(j * z.col + i * SUB, SUB), h * LANE : (h + 1) * LANE
                ]
        return 0

    lax.fori_loop(0, z.cols, step, 0)
    for h in range(z.halves):
        out_ref[:, h * LANE : (h + 1) * LANE] = split_s[h, :, :].astype(BF16)


def final_wide_kernel(z, factor, sum_ref, expand_ref, contract_ref):
    half, cut = z.channels // 2, z.wide // 2
    expand_ref[...] = sum_ref[0:half, :].astype(F32) * factor
    for t in range(2):
        part = sum_ref[half:, t * cut : (t + 1) * cut].astype(F32) * factor
        contract_ref[:, t * half : (t + 1) * half] = part.T


def final_small_kernel(z, factor, sum_ref, merge_ref, kernel_ref, gain_ref):
    merge_ref[...] = (sum_ref[0 : z.channels, :].astype(F32) * factor).T
    half = z.channels // 2
    tail = sum_ref[z.channels :, :].astype(F32) * factor
    depth = tail.shape[0]
    kernel_ref[0:depth, :] = tail[:, :half]
    kernel_ref[depth:, :] = tail[: KS * KS - depth, half:]
    gain_ref[...] = tail[KS * KS - depth : KS * KS - depth + 1, half:]


def swap(x, axis, distance):
    size = lax.axis_size(axis)
    return lax.ppermute(x, axis, [(i, i ^ distance) for i in range(size)])


def reduce_rows(x, halving):
    steps = []
    for axis in ("lat", "lon"):
        distance = 1
        while distance < lax.axis_size(axis):
            steps.append((axis, distance))
            distance *= 2
    done = []
    for n, (axis, distance) in enumerate(steps):
        if halving and n < len(steps) - 1:
            low = ((lax.axis_index(axis) // distance) % 2) == 0
            half = x.shape[0] // 2
            mine = jnp.where(low, x[:half], x[half:])
            send = jnp.where(low, x[half:], x[:half])
            got = swap(send, axis, distance)
            done.append((axis, distance, low))
        else:
            mine, got = x, swap(x, axis, distance)
        x = (mine.astype(F32) + got.astype(F32)).astype(BF16)
    for axis, distance, low in reversed(done):
        got = swap(x, axis, distance)
        x = jnp.concatenate([jnp.where(low, x, got), jnp.where(low, got, x)], axis=0)
    return x


def lat_margins(last, first):
    lats = lax.axis_size("lat")
    if lats == 2:
        got = swap(jnp.where(lax.axis_index("lat") == 0, last, first), "lat", 1)
        return got, got
    up = [(i, i + 1) for i in range(lats - 1)]
    return lax.ppermute(last, "lat", up), lax.ppermute(first, "lat", [(j, i) for i, j in up])


def lon_margins(left, right):
    size = lax.axis_size("lon")
    up = [(i, (i + 1) % size) for i in range(size)]
    return lax.ppermute(right, "lon", up), lax.ppermute(left, "lon", [(j, i) for i, j in up])


def body(fine_field, grad_out, conv_kernel, norm_gain, w_expand, w_contract, w_merge):
    z = Sizes(fine_field, w_merge, w_expand)
    ch, wide, lats = z.channels, z.wide, lax.axis_size("lat")
    fine = fine_field.reshape(z.fine, z.narrow)
    gain = norm_gain.reshape(1, ch)
    total_rows = z.lat_rows * lats
    place = jnp.arange(z.col, dtype=jnp.int32)
    row = lax.axis_index("lat") * z.lat_rows + (place % SUB) % z.blocks * z.block_rows + place // SUB
    latitude = math.pi * ((row.astype(F32) + 0.5) / total_rows - 0.5)
    cosine = jnp.broadcast_to(jnp.cos(latitude)[:, None], (z.col, LANE))

    part = functools.partial
    split = ((z.halves, z.cells, LANE), F32)
    edge = ((z.samples * M * z.cols, ch), BF16)
    patches, coarse, last, first = kernel_call(
        part(merge_kernel, z),
        [((z.cells, 4 * z.narrow), BF16), ((z.cells, ch), BF16), edge, edge],
        (fine, w_merge),
        [((z.fine, z.narrow), F32), split],
    )
    before, after = lat_margins(last, first)
    (weighted,) = kernel_call(
        part(weighted_kernel, z),
        [((z.cells, ch), BF16)],
        (grad_out.reshape(z.cells, ch), cosine),
        [split],
        flops=2_000_000_000,
    )
    slab = ((M * z.pad_col, ch), BF16)
    padded = ((z.cols * z.pad_col, ch), F32)
    pad_scratch = [((2 * z.samples * M * z.cols, ch), F32)]
    pad, left, right = kernel_call(part(pad_kernel, z, lats), [padded, slab, slab], (coarse, before, after), pad_scratch)
    left, right = lon_margins(left, right)

    taps_s = ((KS * KS * SUB, ch), F32)

    def section_scratch(count):
        return [
            ((count, ch), F32),
            ((count, LANE), F32),
            ((count, ch), BF16),
            ((count, wide), BF16),
            ((count, wide), BF16),
            ((count, ch), BF16),
        ]

    outer = 2 * M * z.col
    inner = z.cells - outer
    section_in, mixed_in, expand, contract, gain_sum = kernel_call(
        part(inner_kernel, z),
        [((inner, ch), BF16), ((inner, ch), F32), ((ch, wide), F32), ((ch, wide), F32), ((SUB, ch), F32)],
        (pad, conv_kernel, gain, w_expand, w_contract, coarse, weighted),
        [taps_s] + section_scratch(inner),
        flops=8_000_000_000,
    )
    section_out, mixed_out, mine, other, low, last, first, gain_sum = kernel_call(
        part(outer_kernel, z),
        [
            ((outer, ch), BF16),
            ((outer, ch), F32),
            ((ch, wide), BF16),
            ((ch, wide), BF16),
            ((z.cells, ch), BF16),
            edge,
            edge,
            ((SUB, ch), F32),
        ],
        (pad, left, right, conv_kernel, gain, w_expand, w_contract, coarse, weighted)
        + (expand, contract, gain_sum, mixed_in),
        [taps_s, ((6 * M * z.pad_col, ch), F32), ((2, ch, wide), F32), split] + section_scratch(outer),
        flops=8_000_000_000,
    )
    before, after = lat_margins(last, first)
    got = swap(other, "dp", 1)
    (section_all,) = kernel_call(
        part(section_kernel, z),
        [((z.cells, ch), BF16)],
        (section_in, section_out),
        [((z.cells, ch), F32), split],
        flops=2_000_000_000,
    )
    pad_low, left_low, right_low = kernel_call(
        part(pad_kernel, z, lats), [padded, slab, slab], (low, before, after), pad_scratch
    )
    left_low, right_low = lon_margins(left_low, right_low)
    full = (((z.cols + 2 * M) * z.pad_col, ch), F32)
    (aux,) = kernel_call(
        part(terms_kernel, z),
        [((64, ch), F32)],
        (pad, left, right, mixed_in, mixed_out, gain_sum),
        [full, ((z.cells, ch), F32)],
        flops=5_000_000_000,
    )
    wide_sum = reduce_rows((mine.astype(F32) + got.astype(F32)).astype(BF16), True)
    small = ((ch + 32, ch), BF16)
    back_coarse, mine, other = kernel_call(
        part(back_kernel, z),
        [((z.cells, ch), BF16), small, small],
        (pad_low, left_low, right_low, conv_kernel, weighted, patches, aux),
        [taps_s, full, ((ch, 4 * z.narrow), F32)],
        flops=5_000_000_000,
    )
    got = swap(other, "dp", 1)
    (grad_fine,) = kernel_call(
        part(fine_kernel, z),
        [((z.fine, z.narrow), BF16)],
        (back_coarse, w_merge, fine),
        [((z.fine, z.narrow), F32)],
        flops=5_000_000_000,
    )
    small_sum = reduce_rows((mine.astype(F32) + got.astype(F32)).astype(BF16), False)
    all_cells = z.samples * lax.axis_size("dp") * total_rows * z.cols * lax.axis_size("lon")
    factor = 1.0 / math.sqrt(all_cells)
    grad_expand, grad_contract = kernel_call(
        part(final_wide_kernel, z, factor), [((ch // 2, wide), F32), ((wide // 2, ch), F32)], (wide_sum,)
    )
    grad_merge, grad_kernel, grad_gain = kernel_call(
        part(final_small_kernel, z, factor),
        [((2 * z.narrow, ch), F32), ((KS * KS, ch // 2), F32), ((1, ch // 2), F32)],
        (small_sum,),
    )
    return (
        section_all.reshape(z.samples, z.lat_rows, z.cols, ch),
        grad_fine.reshape(fine_field.shape),
        grad_kernel,
        grad_gain.reshape(ch // 2),
        grad_expand,
        grad_contract,
        grad_merge,
    )


def solution(mesh):
    field = P(("groups", "dp"), "lat", "lon", None)
    owned = P(("groups", "dp"), None)
    return jax.shard_map(
        body,
        mesh=mesh,
        in_specs=(field, field, P(), P(), P(), P(), P()),
        out_specs=(field, field, P("groups", "dp"), P(("groups", "dp")), owned, owned, owned),
        check_vma=False,
    )
```

time: 225 us -> 92.5 us (0.41)
  blocking collectives: 80.2 us -> 0 us
  other arithmetic: 55.1 us -> 0.86 us
  Pallas kernels: 0 us -> 45.6 us
  matrix products: 26.8 us -> 0 us
  between operations: 16.2 us -> 0.92 us
  waiting for transfers between devices: 9.21 us -> 22.1 us
  local copies, waits for them, and re-layouts: 16.2 us -> 3.32 us
    psum x1 -> x0, blocking collectives: 77.5 us -> none  [body(): lax.psum((owned[0], owned[1], owned[2], owned[3], owned[4]), ('lon', 'lat'))]
    pallas_call x0 -> x12, Pallas kernels: none -> 45.6 us  [kernel_call(): pl.pallas_call(fn, out_shape=[jax.ShapeDtypeStruct(s, d) for s, d in outs...]
    reduce_sum x10 -> x0, other arithmetic: 33 us -> none  [the longest x2 12.4 us: normalize(): centered = values - jnp.mean(values, axis=-1, keepdims=True)]
    dot_general x9 -> x0, matrix products: 26.8 us -> none  [the longest x1 10.7 us: body(): pre_act = jnp.dot(normed, w_expand, preferred_element_type=jnp.float32)]
    ppermute x8 -> x16, waiting for transfers between devices: 7.24 us -> 22.1 us  [the longest x12 15.9 us: swap(): return lax.ppermute(x, axis, [(i, i ^ distance) for i in range(size)])]
    convert_element_type x6 -> x8, other arithmetic: 15.2 us -> 0.55 us  [the longest x6 0.32 us: reduce_rows(): x = (mine.astype(F32) + got.astype(F32)).astype(BF16)]
    slice x5 -> x0, local copies, waits for them, and re-layouts: 3.89 us -> none  [the longest x3 3.68 us: depthwise(): total = total + window * kernel[kernel_row * KS + kernel_col]]
    mul x5 -> x0, other arithmetic: 3.51 us -> none  [the longest x1 0.83 us: body(): summed[0] * factor]
  transfers between devices with their start and end apart: 12 -> 16, of which waited for: 6 -> 7; matrix products, arithmetic and copies ran while one was open for 20% -> 1% of each run, Pallas kernels for 0% -> 35%
where the time goes in v1:
time: 92.5 us; the launch traced here: 92.2 us
  Pallas kernels  45.6 us (49%)
  waiting for transfers between devices  22.1 us (24%)
  starting transfers between devices  19.5 us (21%)
  local copies, waits for them, and re-layouts  3.32 us (4%)
    pallas_call x12, Pallas kernels, kernel_call(): pl.pallas_call(fn, out_shape=[jax.ShapeDtypeStruct(s, d) for s, d in outs...  45.6 us
    ppermute x12, waiting for transfers between devices, swap(): return lax.ppermute(x, axis, [(i, i ^ distance) for i in range(size)])  15.9 us
    ppermute x12, starting transfers between devices, swap(): return lax.ppermute(x, axis, [(i, i ^ distance) for i in range(size)])  11.4 us
    ppermute x2, starting transfers between devices, lon_margins(): lax.ppermute(left, 'lon', [(j, i) for i, j in up])  5.9 us
    ppermute x2, waiting for transfers between devices, lon_margins(): lax.ppermute(right, 'lon', up)  4.51 us
    unnamed x18, local copies, waits for them, and re-layouts  3.25 us
    ppermute x2, starting transfers between devices, lon_margins(): lax.ppermute(right, 'lon', up)  2.21 us
  transfers between devices with their start and end apart: 16, of which 7 were waited for; matrix products, arithmetic and copies ran while one was open for 1% of the time, Pallas kernels for 35%

profile of v1, /device:TPU:0, one launch (start us, length us, event | category | flops | bytes accessed | tf_op | source)
XLA Modules:
  0.0 92.2 jit_solution(17954263731198477560)
XLA Ops:
  0.6 0.0 copy-start
  0.7 1.2 %copy-done = bf16[2,64,32,128]{3,2,1,0:T(8,128)(2,1)S(1)} copy-done((bf16[2,64,32,128]{3,2,1,0:T(8,128)(2,1)S(1)}, bf16[2,64,32,128]{3,2,1,0:T(8,128)(2,1)}, u32[]{:S(2)}) %copy-start) | copy-done | bytes 1048600
  1.9 0.9 %copy-done.2 = bf16[512,256]{1,0:T(8,128)(2,1)S(1)} copy-done((bf16[512,256]{1,0:T(8,128)(2,1)S(1)}, bf16[512,256]{1,0:T(8,128)(2,1)}, u32[]{:S(2)}) %copy-start.2) | copy-done | bytes 262168
  2.8 4.7 %shard_map.126 = (bf16[1024,512]{1,0:T(8,128)(2,1)S(1)}, bf16[1024,256]{1,0:T(8,128)(2,1)S(1)}, bf16[96,256]{1,0:T(8,128)(2,1)S(1)}, bf16[96,256]{1,0:T(8,128)(2,1)S(1)}) custom-call(bf16[4096,128]{1,0:T(8,128)(2,1)S(1)} %bitcast.6, bf16[512,256]{1,0:T(8,128)(2,1)S(1)} %copy-done.2), custom_call_target="tpu_custom_call" | custom-call | bytes 1310720 | tf_op jit(solution)/shard_map/pallas_call | solution.py:21
  7.6 3.0 %collective-permute-start = (bf16[96,256]{1,0:T(8,128)(2,1)S(1)}, bf16[96,256]{1,0:T(8,128)(2,1)S(1)}, u32[]{:S(2)}, u32[]{:S(2)}) collective-permute-start(bf16[96,256]{1,0:T(8,128)(2,1)S(1)} %broadcast_select_fusion.7), channel_id=1, source_target_pairs={{0,2},{2,0},{1,3},{3,1},{4,6},{6,4},{5,7},{7,5},{8,10},{10,8},{9,1... | collective-permute-start | bytes 147464 | tf_op jit(solution)/shard_map/ppermute | solution.py:436
  10.6 0.1 fusion.9
  10.6 0.1 broadcast_in_dim.2.cos_ref
  10.7 1.0 %copy-done.4 = bf16[2,32,16,256]{3,2,1,0:T(8,128)(2,1)S(1)} copy-done((bf16[2,32,16,256]{3,2,1,0:T(8,128)(2,1)S(1)}, bf16[2,32,16,256]{3,2,1,0:T(8,128)(2,1)}, u32[]{:S(2)}) %copy-start.4) | copy-done | bytes 524312
  11.8 0.8 shard_map.128.weighted_ref
  12.6 0.0 collective-permute-done.before_ref.after_ref
  12.6 0.6 shard_map.127
  13.2 2.2 %collective-permute-start.1 = (bf16[336,256]{1,0:T(8,128)(2,1)S(1)}, bf16[336,256]{1,0:T(8,128)(2,1)S(1)}, u32[]{:S(2)}, u32[]{:S(2)}) collective-permute-start(bf16[336,256]{1,0:T(8,128)(2,1)S(1)} %get-tuple-element.43), channel_id=1, source_target_pairs={{0,4},{4,8},{8,12},{12,0},{1,5},{5,9},{9,13},{13,1},{2,6},{6,10},{... | collective-permute-start | bytes 516104 | tf_op jit(solution)/shard_map/ppermute | solution.py:476
  15.4 2.1 %collective-permute-start.2 = (bf16[336,256]{1,0:T(8,128)(2,1)S(1)}, bf16[336,256]{1,0:T(8,128)(2,1)S(1)}, u32[]{:S(2)}, u32[]{:S(2)}) collective-permute-start(bf16[336,256]{1,0:T(8,128)(2,1)S(1)} %get-tuple-element.44), channel_id=1, source_target_pairs={{4,0},{8,4},{12,8},{0,12},{5,1},{9,5},{13,9},{1,13},{6,2},{10,6},{... | collective-permute-start | bytes 516104 | tf_op jit(solution)/shard_map/ppermute | solution.py:476
  17.5 8.8 %shard_map.129 = (bf16[640,256]{1,0:T(8,128)(2,1)S(1)}, f32[640,256]{1,0:T(8,128)S(1)}, f32[256,1024]{1,0:T(8,128)S(1)}, f32[256,1024]{1,0:T(8,128)S(1)}, f32[8,256]{1,0:T(8,128)S(1)}) custom-call(f32[1792,256]{1,0:T(8,128)S(1)} %get-tuple-element.41.pad_ref, f32[49,256]{1,0:T(8,128)S(1)} %copy-done.7, f32[1,256]{1,0:T(1,128)S(1)} %bitcast.9, ...), custom_call_target="tpu_custom_call" | custom-call | flops 8000000000 | bytes 3983360 | tf_op jit(solution)/shard_map/pallas_call | solution.py:21
  26.3 0.0 collective-permute-done.1.left_ref
  26.3 6.8 %shard_map.130 = (bf16[384,256]{1,0:T(8,128)(2,1)S(1)}, f32[384,256]{1,0:T(8,128)S(1)}, bf16[256,1024]{1,0:T(8,128)(2,1)S(1)}, bf16[256,1024]{1,0:T(8,128)(2,1)S...) custom-call(f32[1792,256]{1,0:T(8,128)S(1)} %get-tuple-element.41.pa, ...), custom_call_target="tpu_custom_call" | custom-call | flops 8000000000 | bytes 7088128 | tf_op jit(solution)/shard_map/pallas_call | solution.py:21
  33.1 1.7 %collective-permute-start.3 = (bf16[96,256]{1,0:T(8,128)(2,1)S(1)}, bf16[96,256]{1,0:T(8,128)(2,1)S(1)}, u32[]{:S(2)}, u32[]{:S(2)}) collective-permute-start(bf16[96,256]{1,0:T(8,128)(2,1)S(1)} %broadcast_select_fusion.6), channel_id=1, source_target_pairs={{0,2},{2,0},{1,3},{3,1},{4,6},{6,4},{5,7},{7,5},{8,10},{10,8},{9,1... | collective-permute-start | bytes 147464 | tf_op jit(solution)/shard_map/ppermute | solution.py:436
  34.9 5.8 %shard_map.133.aux_ref = f32[64,256]{1,0:T(8,128)S(1)} custom-call(f32[1792,256]{1,0:T(8,128)S(1)} %get-tuple-element.41.pad_ref, bf16[336,256]{1,0:T(8,128)(2,1)S(1)} %collective-permute-done.1.left_ref, bf16[336,256]{1,0:T(8,128)(2,1)S(1)} %collective-permute-done.2.right_ref, f32[640,256]{1,0:T(8,128)S(1)} %get-tuple-element.48.inner_mixed_ref.inner_ref, ...), custom_call_target="tpu_custom_call" | custom-call | flops 5000000000 | bytes 3235840 | tf_op jit(solution)/shard_map/pallas_call | solution.py:21
  40.7 1.8 %shard_map.131 = bf16[1024,256]{1,0:T(8,128)(2,1)} custom-call(bf16[640,256]{1,0:T(8,128)(2,1)S(1)} %get-tuple-element.42.inner_ref, bf16[384,256]{1,0:T(8,128)(2,1)S(1)} %get-tuple-element.49.outer_ref), custom_call_target="tpu_custom_call" | custom-call | flops 2000000000 | bytes 524288 | tf_op jit(solution)/shard_map/pallas_call | solution.py:21
  42.5 0.6 shard_map.132
  43.1 0.1 collective-permute-start.4
  43.2 3.8 %collective-permute-start.5 = (bf16[336,256]{1,0:T(8,128)(2,1)S(1)}, bf16[336,256]{1,0:T(8,128)(2,1)S(1)}, u32[]{:S(2)}, u32[]{:S(2)}) collective-permute-start(bf16[336,256]{1,0:T(8,128)(2,1)S(1)} %get-tuple-element.55), channel_id=1, source_target_pairs={{4,0},{8,4},{12,8},{0,12},{5,1},{9,5},{13,9},{1,13},{6,2},{10,6},{... | collective-permute-start | bytes 516104 | tf_op jit(solution)/shard_map/ppermute | solution.py:476
  47.0 0.2 add_convert_fusion
  47.2 0.4 collective-permute-start.11
  47.7 4.5 %collective-permute-done.4.left_ref = bf16[336,256]{1,0:T(8,128)(2,1)S(1)} collective-permute-done((bf16[336,256]{1,0:T(8,128)(2,1)S(1)}, bf16[336,256]{1,0:T(8,128)(2,1)S(1)}, u32[]{:S(2)}, u32[]{:S(2)}) %collective-permute-start.4) | collective-permute-done | bytes 172064 | tf_op jit(solution)/shard_map/ppermute | solution.py:476
  52.2 1.7 %collective-permute-done.5.right_ref = bf16[336,256]{1,0:T(8,128)(2,1)S(1)} collective-permute-done((bf16[336,256]{1,0:T(8,128)(2,1)S(1)}, bf16[336,256]{1,0:T(8,128)(2,1)S(1)}, u32[]{:S(2)}, u32[]{:S(2)}) %collective-permute-start.5) | collective-permute-done | bytes 172064 | tf_op jit(solution)/shard_map/ppermute | solution.py:476
  53.9 5.8 %shard_map.134 = (bf16[1024,256]{1,0:T(8,128)(2,1)S(1)}, bf16[288,256]{1,0:T(8,128)(2,1)S(1)}, bf16[288,256]{1,0:T(8,128)(2,1)S(1)}) custom-call(f32[1792,256]{1,0:T(8,128)S(1)} %get-tuple-element.53.pad_ref, bf16[336,256]{1,0:T(8,128)(2,1)S(1)} %collective-permute-done.4.left_ref, bf16[336,256]{1,0:T(8,128)(2,1)S(1)} %collective-permute-done.5.right_ref, ...), custom_call_target="tpu_custom_call" | custom-call | flops 5000000000 | bytes 3867648 | tf_op jit(solution)/shard_map/pallas_call | solution.py:21
  59.7 0.1 collective-permute-start.6
  59.8 0.1 add_convert_fusion.1
  60.0 0.0 copy-start.1
  60.0 0.0 copy-start.3
  60.0 0.9 collective-permute-start.12
  60.9 0.3 collective-permute-done.6
  61.2 0.4 collective-permute-start.7
  61.7 4.3 %collective-permute-done.12 = bf16[64,1024]{1,0:T(8,128)(2,1)S(1)} collective-permute-done((bf16[64,1024]{1,0:T(8,128)(2,1)S(1)}, bf16[64,1024]{1,0:T(8,128)(2,1)S(1)}, u32[]{:S(2)}, u32[]{:S(2)}) %collective-permute-start.12) | collective-permute-done | bytes 131104 | tf_op jit(solution)/shard_map/ppermute | solution.py:436
  66.0 0.1 add_convert_fusion.7
  66.0 2.2 %collective-permute-start.13 = (bf16[64,1024]{1,0:T(8,128)(2,1)S(1)}, bf16[64,1024]{1,0:T(8,128)(2,1)S(1)}, u32[]{:S(2)}, u32[]{:S(2)}) collective-permute-start(bf16[64,1024]{1,0:T(8,128)(2,1)S(1)} %add_convert_fusion.7), channel_id=1, source_target_pairs={{0,8},{4,12},{8,0},{12,4},{1,9},{5,13},{9,1},{13,5},{2,10},{6,14},... | collective-permute-start | bytes 393224 | tf_op jit(solution)/shard_map/ppermute | solution.py:436
  68.3 0.4 collective-permute-start.8
  68.6 6.4 %collective-permute-done.13 = bf16[64,1024]{1,0:T(8,128)(2,1)S(1)} collective-permute-done((bf16[64,1024]{1,0:T(8,128)(2,1)S(1)}, bf16[64,1024]{1,0:T(8,128)(2,1)S(1)}, u32[]{:S(2)}, u32[]{:S(2)}) %collective-permute-start.13) | collective-permute-done | bytes 131104 | tf_op jit(solution)/shard_map/ppermute | solution.py:436
  75.0 0.1 collective-permute-start.14
  75.1 0.9 collective-permute-done.8
  76.0 1.7 %collective-permute-start.9 = (bf16[288,256]{1,0:T(8,128)(2,1)S(1)}, bf16[288,256]{1,0:T(8,128)(2,1)S(1)}, u32[]{:S(2)}, u32[]{:S(2)}) collective-permute-start(bf16[288,256]{1,0:T(8,128)(2,1)S(1)} %add_convert_fusion.3), channel_id=1, source_target_pairs={{0,8},{4,12},{8,0},{12,4},{1,9},{5,13},{9,1},{13,5},{2,10},{6,14},... | collective-permute-start | bytes 442376 | tf_op jit(solution)/shard_map/ppermute | solution.py:436
  77.7 4.0 %collective-permute-done.14 = bf16[64,1024]{1,0:T(8,128)(2,1)S(1)} collective-permute-done((bf16[64,1024]{1,0:T(8,128)(2,1)S(1)}, bf16[64,1024]{1,0:T(8,128)(2,1)S(1)}, u32[]{:S(2)}, u32[]{:S(2)}) %collective-permute-start.14) | collective-permute-done | bytes 131104 | tf_op jit(solution)/shard_map/ppermute | solution.py:436
  81.8 0.5 collective-permute-start.15
  82.3 7.8 %shard_map.135 = bf16[4096,128]{1,0:T(8,128)(2,1)} custom-call(bf16[1024,256]{1,0:T(8,128)(2,1)S(1)} %get-tuple-element.59.coarse_ref, bf16[512,256]{1,0:T(8,128)(2,1)S(1)} %copy-done.3, bf16[4096,128]{1,0:T(8,128)(2,1)S(1)} %bitcast.7), custom_call_target="tpu_custom_call" | custom-call | flops 5000000000 | bytes 1835008 | tf_op jit(solution)/shard_map/pallas_call | solution.py:21
  90.1 0.8 shard_map.136
  90.9 0.1 broadcast_select_fusion.1
  91.1 1.2 %shard_map.137 = (f32[128,1024]{1,0:T(8,128)}, f32[512,256]{1,0:T(8,128)}) custom-call(bf16[256,1024]{1,0:T(8,128)(2,1)S(1)} %pad_maximum_fusion.sum_ref), custom_call_target="tpu_custom_call" | custom-call | bytes 524288 | tf_op jit(solution)/shard_map/pallas_call | solution.py:21
  (32 shorter events, 0.4 us)
Async XLA Ops:
  0.6 1.2 %copy-start = (bf16[2,64,32,128]{3,2,1,0:T(8,128)(2,1)S(1)}, bf16[2,64,32,128]{3,2,1,0:T(8,128)(2,1)}, u32[]{:S(2)}) copy-start(bf16[2,64,32,128]{3,2,1,0:T(8,128)(2,1)} %param.7) | copy-start | bytes 3145732
  1.9 0.9 %copy-start.2 = (bf16[512,256]{1,0:T(8,128)(2,1)S(1)}, bf16[512,256]{1,0:T(8,128)(2,1)}, u32[]{:S(2)}) copy-start(bf16[512,256]{1,0:T(8,128)(2,1)} %w_ref.3) | copy-start | bytes 786436
  7.6 5.1 %collective-permute-start = (bf16[96,256]{1,0:T(8,128)(2,1)S(1)}, bf16[96,256]{1,0:T(8,128)(2,1)S(1)}, u32[]{:S(2)}, u32[]{:S(2)}) collective-permute-start(bf16[96,256]{1,0:T(8,128)(2,1)S(1)} %broadcast_select_fusion.7), channel_id=1, source_target_pairs={{0,2},{2,0},{1,3},{3,1},{4,6},{6,4},{5,7},{7,5},{8,10},{10,8},{9,1... | collective-permute-start | bytes 147464 | tf_op jit(solution)/shard_map/ppermute | solution.py:436
  10.7 1.1 %copy-start.4 = (bf16[2,32,16,256]{3,2,1,0:T(8,128)(2,1)S(1)}, bf16[2,32,16,256]{3,2,1,0:T(8,128)(2,1)}, u32[]{:S(2)}) copy-start(bf16[2,32,16,256]{3,2,1,0:T(8,128)(2,1)} %param.8) | copy-start | bytes 1572868
  11.8 5.7 %copy-start.5 = (bf16[256,1024]{1,0:T(8,128)(2,1)S(1)}, bf16[256,1024]{1,0:T(8,128)(2,1)}, u32[]{:S(2)}) copy-start(bf16[256,1024]{1,0:T(8,128)(2,1)} %we_ref.3) | copy-start | bytes 1572868
  11.8 5.7 %copy-start.6 = (bf16[1024,256]{1,0:T(8,128)(2,1)S(1)}, bf16[1024,256]{1,0:T(8,128)(2,1)}, u32[]{:S(2)}) copy-start(bf16[1024,256]{1,0:T(8,128)(2,1)} %wc_ref.3) | copy-start | bytes 1572868
  11.8 5.7 %copy-start.7 = (f32[49,256]{1,0:T(8,128)S(1)}, f32[49,256]{1,0:T(8,128)}, u32[]{:S(2)}) copy-start(f32[49,256]{1,0:T(8,128)} %kern_ref.5) | copy-start | bytes 150532
  11.8 5.7 %copy-start.8 = (f32[256]{0:T(256)S(1)}, f32[256]{0:T(256)}, u32[]{:S(2)}) copy-start(f32[256]{0:T(256)} %param.10) | copy-start | bytes 3076
  13.2 13.1 %collective-permute-start.1 = (bf16[336,256]{1,0:T(8,128)(2,1)S(1)}, bf16[336,256]{1,0:T(8,128)(2,1)S(1)}, u32[]{:S(2)}, u32[]{:S(2)}) collective-permute-start(bf16[336,256]{1,0:T(8,128)(2,1)S(1)} %get-tuple-element.43), channel_id=1, source_target_pairs={{0,4},{4,8},{8,12},{12,0},{1,5},{5,9},{9,13},{13,1},{2,6},{6,10},{... | collective-permute-start | bytes 516104 | tf_op jit(solution)/shard_map/ppermute | solution.py:476
  15.4 10.9 %collective-permute-start.2 = (bf16[336,256]{1,0:T(8,128)(2,1)S(1)}, bf16[336,256]{1,0:T(8,128)(2,1)S(1)}, u32[]{:S(2)}, u32[]{:S(2)}) collective-permute-start(bf16[336,256]{1,0:T(8,128)(2,1)S(1)} %get-tuple-element.44), channel_id=1, source_target_pairs={{4,0},{8,4},{12,8},{0,12},{5,1},{9,5},{13,9},{1,13},{6,2},{10,6},{... | collective-permute-start | bytes 516104 | tf_op jit(solution)/shard_map/ppermute | solution.py:476
  33.1 9.4 %collective-permute-start.3 = (bf16[96,256]{1,0:T(8,128)(2,1)S(1)}, bf16[96,256]{1,0:T(8,128)(2,1)S(1)}, u32[]{:S(2)}, u32[]{:S(2)}) collective-permute-start(bf16[96,256]{1,0:T(8,128)(2,1)S(1)} %broadcast_select_fusion.6), channel_id=1, source_target_pairs={{0,2},{2,0},{1,3},{3,1},{4,6},{6,4},{5,7},{7,5},{8,10},{10,8},{9,1... | collective-permute-start | bytes 147464 | tf_op jit(solution)/shard_map/ppermute | solution.py:436
  34.8 12.1 %collective-permute-start.10 = (bf16[256,1024]{1,0:T(8,128)(2,1)S(1)}, bf16[256,1024]{1,0:T(8,128)(2,1)S(1)}, u32[]{:S(2)}, u32[]{:S(2)}) collective-permute-start(bf16[256,1024]{1,0:T(8,128)(2,1)S(1)} %get-tuple-element.65), channel_id=1, source_target_pairs={{0,1},{1,0},{2,3},{3,2},{4,5},{5,4},{6,7},{7,6},{8,9},{9,8},{10,11... | collective-permute-start | bytes 1572872 | tf_op jit(solution)/shard_map/ppermute | solution.py:436
  43.1 9.1 %collective-permute-start.4 = (bf16[336,256]{1,0:T(8,128)(2,1)S(1)}, bf16[336,256]{1,0:T(8,128)(2,1)S(1)}, u32[]{:S(2)}, u32[]{:S(2)}) collective-permute-start(bf16[336,256]{1,0:T(8,128)(2,1)S(1)} %get-tuple-element.54), channel_id=1, source_target_pairs={{0,4},{4,8},{8,12},{12,0},{1,5},{5,9},{9,13},{13,1},{2,6},{6,10},{... | collective-permute-start | bytes 516104 | tf_op jit(solution)/shard_map/ppermute | solution.py:476
  43.2 10.7 %collective-permute-start.5 = (bf16[336,256]{1,0:T(8,128)(2,1)S(1)}, bf16[336,256]{1,0:T(8,128)(2,1)S(1)}, u32[]{:S(2)}, u32[]{:S(2)}) collective-permute-start(bf16[336,256]{1,0:T(8,128)(2,1)S(1)} %get-tuple-element.55), channel_id=1, source_target_pairs={{4,0},{8,4},{12,8},{0,12},{5,1},{9,5},{13,9},{1,13},{6,2},{10,6},{... | collective-permute-start | bytes 516104 | tf_op jit(solution)/shard_map/ppermute | solution.py:476
  47.2 12.6 %collective-permute-start.11 = (bf16[128,1024]{1,0:T(8,128)(2,1)S(1)}, bf16[128,1024]{1,0:T(8,128)(2,1)S(1)}, u32[]{:S(2)}, u32[]{:S(2)}) collective-permute-start(bf16[128,1024]{1,0:T(8,128)(2,1)S(1)} %broadcast_select_fusion.2), channel_id=1, source_target_pairs={{0,2},{2,0},{1,3},{3,1},{4,6},{6,4},{5,7},{7,5},{8,10},{10,8},{9,1... | collective-permute-start | bytes 786440 | tf_op jit(solution)/shard_map/ppermute | solution.py:436
  59.7 1.4 %collective-permute-start.6 = (bf16[288,256]{1,0:T(8,128)(2,1)S(1)}, bf16[288,256]{1,0:T(8,128)(2,1)S(1)}, u32[]{:S(2)}, u32[]{:S(2)}) collective-permute-start(bf16[288,256]{1,0:T(8,128)(2,1)S(1)} %get-tuple-element.61), channel_id=1, source_target_pairs={{0,1},{1,0},{2,3},{3,2},{4,5},{5,4},{6,7},{7,6},{8,9},{9,8},{10,11... | collective-permute-start | bytes 442376 | tf_op jit(solution)/shard_map/ppermute | solution.py:436
  60.0 22.3 %copy-start.1 = (bf16[2,64,32,128]{3,2,1,0:T(8,128)(2,1)S(1)}, bf16[2,64,32,128]{3,2,1,0:T(8,128)(2,1)}, u32[]{:S(2)}) copy-start(bf16[2,64,32,128]{3,2,1,0:T(8,128)(2,1)} %param.7) | copy-start | bytes 3145732
  60.0 22.3 %copy-start.3 = (bf16[512,256]{1,0:T(8,128)(2,1)S(1)}, bf16[512,256]{1,0:T(8,128)(2,1)}, u32[]{:S(2)}) copy-start(bf16[512,256]{1,0:T(8,128)(2,1)} %w_ref.3) | copy-start | bytes 786436
  60.0 6.0 %collective-permute-start.12 = (bf16[64,1024]{1,0:T(8,128)(2,1)S(1)}, bf16[64,1024]{1,0:T(8,128)(2,1)S(1)}, u32[]{:S(2)}, u32[]{:S(2)}) collective-permute-start(bf16[64,1024]{1,0:T(8,128)(2,1)S(1)} %broadcast_select_fusion.5), channel_id=1, source_target_pairs={{0,4},{4,0},{8,12},{12,8},{1,5},{5,1},{9,13},{13,9},{2,6},{6,2},{1... | collective-permute-start | bytes 393224 | tf_op jit(solution)/shard_map/ppermute | solution.py:436
  61.2 7.0 %collective-permute-start.7 = (bf16[288,256]{1,0:T(8,128)(2,1)S(1)}, bf16[288,256]{1,0:T(8,128)(2,1)S(1)}, u32[]{:S(2)}, u32[]{:S(2)}) collective-permute-start(bf16[288,256]{1,0:T(8,128)(2,1)S(1)} %add_convert_fusion.5), channel_id=1, source_target_pairs={{0,2},{2,0},{1,3},{3,1},{4,6},{6,4},{5,7},{7,5},{8,10},{10,8},{9,1... | collective-permute-start | bytes 442376 | tf_op jit(solution)/shard_map/ppermute | solution.py:436
  66.0 9.0 %collective-permute-start.13 = (bf16[64,1024]{1,0:T(8,128)(2,1)S(1)}, bf16[64,1024]{1,0:T(8,128)(2,1)S(1)}, u32[]{:S(2)}, u32[]{:S(2)}) collective-permute-start(bf16[64,1024]{1,0:T(8,128)(2,1)S(1)} %add_convert_fusion.7), channel_id=1, source_target_pairs={{0,8},{4,12},{8,0},{12,4},{1,9},{5,13},{9,1},{13,5},{2,10},{6,14},... | collective-permute-start | bytes 393224 | tf_op jit(solution)/shard_map/ppermute | solution.py:436
  68.3 7.7 %collective-permute-start.8 = (bf16[288,256]{1,0:T(8,128)(2,1)S(1)}, bf16[288,256]{1,0:T(8,128)(2,1)S(1)}, u32[]{:S(2)}, u32[]{:S(2)}) collective-permute-start(bf16[288,256]{1,0:T(8,128)(2,1)S(1)} %add_convert_fusion.4), channel_id=1, source_target_pairs={{0,4},{4,0},{8,12},{12,8},{1,5},{5,1},{9,13},{13,9},{2,6},{6,2},{1... | collective-permute-start | bytes 442376 | tf_op jit(solution)/shard_map/ppermute | solution.py:436
  75.0 6.7 %collective-permute-start.14 = (bf16[64,1024]{1,0:T(8,128)(2,1)S(1)}, bf16[64,1024]{1,0:T(8,128)(2,1)S(1)}, u32[]{:S(2)}, u32[]{:S(2)}) collective-permute-start(bf16[64,1024]{1,0:T(8,128)(2,1)S(1)} %add_convert_fusion.6), channel_id=1, source_target_pairs={{0,4},{4,0},{8,12},{12,8},{1,5},{5,1},{9,13},{13,9},{2,6},{6,2},{1... | collective-permute-start | bytes 393224 | tf_op jit(solution)/shard_map/ppermute | solution.py:436
  76.0 14.0 %collective-permute-start.9 = (bf16[288,256]{1,0:T(8,128)(2,1)S(1)}, bf16[288,256]{1,0:T(8,128)(2,1)S(1)}, u32[]{:S(2)}, u32[]{:S(2)}) collective-permute-start(bf16[288,256]{1,0:T(8,128)(2,1)S(1)} %add_convert_fusion.3), channel_id=1, source_target_pairs={{0,8},{4,12},{8,0},{12,4},{1,9},{5,13},{9,1},{13,5},{2,10},{6,14},... | collective-permute-start | bytes 442376 | tf_op jit(solution)/shard_map/ppermute | solution.py:436
  81.8 9.1 %collective-permute-start.15 = (bf16[128,1024]{1,0:T(8,128)(2,1)S(1)}, bf16[128,1024]{1,0:T(8,128)(2,1)S(1)}, u32[]{:S(2)}, u32[]{:S(2)}) collective-permute-start(bf16[128,1024]{1,0:T(8,128)(2,1)S(1)} %pad_maximum_fusion.1), channel_id=1, source_target_pairs={{0,2},{2,0},{1,3},{3,1},{4,6},{6,4},{5,7},{7,5},{8,10},{10,8},{9,1... | collective-permute-start | bytes 786440 | tf_op jit(solution)/shard_map/ppermute | solution.py:436

commit v2 on v1

--- a/solution.py
+++ b/solution.py
@@ -16,23 +16,40 @@
 BF16 = jnp.bfloat16
 
 
-def kernel_call(fn, outs, args, scratch=(), flops=0):
+def kernel_call(fn, outs, args, scratch=(), flops=0, after=()):
+    outs = [*outs, ((SUB, LANE), F32)]
     whole = pl.BlockSpec(memory_space=pltpu.VMEM)
+    count = len(args)
+    held = sum(math.prod(s) * jnp.dtype(d).itemsize for s, d in scratch)
+
+    def run(*refs):
+        last = count + len(after) + len(outs) - 1
+        refs[last][...] = jnp.zeros((SUB, LANE), F32)
+        fn(*refs[:count], *refs[count + len(after) : last], *refs[last + 1 :])
+
     return pl.pallas_call(
-        fn,
+        run,
         out_shape=[jax.ShapeDtypeStruct(s, d) for s, d in outs],
-        in_specs=[whole] * len(args),
+        in_specs=[whole] * count + [whole] * len(after),
         out_specs=[whole] * len(outs),
         scratch_shapes=[pltpu.VMEM(s, d) for s, d in scratch],
-        compiler_params=pltpu.CompilerParams(vmem_limit_bytes=40 * 2**20),
+        compiler_params=pltpu.CompilerParams(vmem_limit_bytes=held + 8 * 2**20),
         cost_estimate=pl.CostEstimate(
             flops=flops, bytes_accessed=sum(a.size * a.dtype.itemsize for a in args), transcendentals=0
         ),
-    )(*args)
+    )(*args, *after)
 
 
 def rows(start, size):
-    return pl.ds(start if isinstance(start, int) else pl.multiple_of(start, size & -size), size)
+    return pl.ds(start if isinstance(start, int) else pl.multiple_of(start, SUB), size)
+
+
+def lanes_at(start, size):
+    return pl.ds(pl.multiple_of(start, LANE), size)
+
+
+def rows16(start, size):
+    return pl.ds(start if isinstance(start, int) else pl.multiple_of(start, 2 * SUB), size)
 
 
 def dot(a, b):
@@ -59,7 +76,8 @@
         self.pad_col = self.pad_rows * SUB
         self.cells = self.cols * self.col
         self.fine = 4 * self.cells
-        self.fine_stride = 2 * self.block_rows * fine_cols
+        self.fine_block = 2 * self.block_rows * fine_cols
+        self.fine_stride = self.fine_block + SUB
         self.fine_cols = fine_cols
         self.halves = self.channels // LANE
 
@@ -75,8 +93,9 @@
     return pl.ds((2 * i + p) * z.fine_cols + 2 * j + q, SUB, stride=z.fine_stride)
 
 
-def edge_rows(z, scratch, before_ref, after_ref):
-    for ref, first_row, block in ((after_ref, 0, 0), (before_ref, z.block_rows - M, z.blocks - 1)):
+def edge_rows(z, scratch, edge_refs):
+    sides = []
+    for first_row, block in ((z.block_rows - M, z.blocks - 1), (0, 0)):
         parts = []
         for r in range(M):
             for s in range(z.samples):
@@ -86,16 +105,24 @@
                         [scratch[h, pl.ds(start, z.cols, stride=z.col), :] for h in range(z.halves)], axis=1
                     )
                 )
-        ref[...] = jnp.concatenate(parts, axis=0).astype(BF16)
-
-
-def merge_kernel(z, fine_ref, w_ref, patches_ref, coarse_ref, last_ref, first_ref, unit_s, split_s):
+        sides.append(jnp.concatenate(parts, axis=0))
+    if len(edge_refs) == 1:
+        edge_refs[0][...] = jnp.where(lax.axis_index("lat") == 0, sides[0], sides[1]).astype(BF16)
+    else:
+        for ref, side in zip(edge_refs, sides):
+            ref[...] = side.astype(BF16)
+
+
+def merge_kernel(z, fine_ref, w_ref, patches_ref, coarse_ref, inv_ref, *rest):
+    *edge_refs, unit_s, split_s = rest
     def norm_step(t, _):
-        at = rows(t * 512, 512)
-        unit_s[at, :] = fine_stats(z, fine_ref[at, :])[0]
-        return 0
-
-    lax.fori_loop(0, z.fine // 512, norm_step, 0)
+        at = rows16(t * z.fine_block, z.fine_block)
+        unit, inverse = fine_stats(z, fine_ref[at, :])
+        unit_s[rows(t * z.fine_stride, z.fine_block), :] = unit
+        inv_ref[at, :] = inverse
+        return 0
+
+    lax.fori_loop(0, SUB, norm_step, 0)
     group = 4
 
     def step(g, _):
@@ -109,8 +136,8 @@
                             [unit_s[fine_rows_of(z, j, i, p, q), :] for i in range(z.block_rows)], axis=0
                         ).astype(BF16)
                     )
-            patches_ref[rows(j * z.col, z.col), :] = jnp.concatenate(quarters, axis=1)
-        at = rows(g * group * z.col, group * z.col)
+            patches_ref[rows16(j * z.col, z.col), :] = jnp.concatenate(quarters, axis=1)
+        at = rows16(g * group * z.col, group * z.col)
         low = dot(patches_ref[at, :], w_ref[...]).astype(BF16)
         coarse_ref[at, :] = low
         for h in range(z.halves):
@@ -118,10 +145,20 @@
         return 0
 
     lax.fori_loop(0, z.cols // group, step, 0)
-    edge_rows(z, split_s, last_ref, first_ref)
-
-
-def weighted_kernel(z, grad_ref, cos_ref, out_ref, split_s):
+    edge_rows(z, split_s, edge_refs)
+
+
+def weighted_kernel(z, lats, grad_ref, w_ref, out_ref, centered_ref, split_s):
+    for t in range(4):
+        at = slice(t * z.narrow, (t + 1) * z.narrow)
+        w = w_ref[at, :].astype(F32)
+        w = w - jnp.sum(w, axis=0, keepdims=True) * (1.0 / z.narrow)
+        high = w.astype(BF16)
+        centered_ref[at, 0 : z.channels] = high
+        centered_ref[at, z.channels :] = (w - high.astype(F32)).astype(BF16)
+    place = lax.broadcasted_iota(jnp.int32, (z.col, LANE), 0)
+    row = lax.axis_index("lat") * z.lat_rows + (place % SUB) % z.blocks * z.block_rows + place // SUB
+    cosine = jnp.cos(math.pi * ((row.astype(F32) + 0.5) / (z.lat_rows * lats) - 0.5))
     for h in range(z.halves):
         split_s[h, :, :] = grad_ref[:, h * LANE : (h + 1) * LANE].astype(F32)
 
@@ -134,7 +171,7 @@
                 ],
                 axis=0,
             )
-            out_ref[rows(j * z.col, z.col), h * LANE : (h + 1) * LANE] = (col * cos_ref[...]).astype(BF16)
+            out_ref[rows16(j * z.col, z.col), h * LANE : (h + 1) * LANE] = (col * cosine).astype(BF16)
         return 0
 
     lax.fori_loop(0, z.cols, step, 0)
@@ -154,7 +191,7 @@
         return inner
 
     def step(j, _):
-        own = own_ref[rows(j * z.col, z.col), :].astype(F32)
+        own = own_ref[rows16(j * z.col, z.col), :].astype(F32)
         pad_ref[rows(j * z.pad_col + M * SUB, SUB * z.block_rows), :] = own
         for r in range(M):
             i = z.block_rows - M + r
@@ -210,7 +247,7 @@
 
     def step(j, _):
         parts = [taps(z, pad, taps_s, sources(j), h, False) for h in range(z.halves)]
-        at = rows(j * z.col, z.col)
+        at = rows16(j * z.col, z.col)
         mean = sum(jnp.sum(p, axis=-1, keepdims=True) for p in parts) * (1.0 / z.channels)
         parts = [p - mean for p in parts]
         var = sum(jnp.sum(p * p, axis=-1, keepdims=True) for p in parts) * (1.0 / z.channels)
@@ -268,9 +305,10 @@
 def outer_kernel(
     z, pad_ref, left_ref, right_ref, kern_ref, gain_ref, we_ref, wc_ref, coarse_ref, weighted_ref,
     expand_ref, contract_ref, gain_sum_ref, inner_mixed_ref,
-    section_ref, mixed_ref, mine_ref, other_ref, low_ref, last_ref, first_ref, gain_out_ref,
-    taps_s, edge_s, sum_s, split_s, *scratch,
+    section_ref, mixed_ref, mine_ref, other_ref, low_ref, gain_out_ref, *rest,
 ):
+    *edge_refs, taps_s, edge_s, sum_s, split_s = rest[:-6]
+    scratch = rest[-6:]
     spread_taps(z, kern_ref, taps_s)
     edge, near = M * z.pad_col, 2 * M * z.pad_col
     edge_s[0:edge, :] = left_ref[...].astype(F32)
@@ -290,9 +328,9 @@
     own = lax.axis_index("dp")
     half, cut = z.channels // 2, z.wide // 2
     for ref, owner in ((mine_ref, own), (other_ref, 1 - own)):
-        ref[0:half, :] = sum_s[0, rows(owner * half, half), :].astype(BF16)
+        ref[0:half, :] = sum_s[0, rows16(owner * half, half), :].astype(BF16)
         for t in range(2):
-            ref[half:, t * cut : (t + 1) * cut] = sum_s[1, t * half : (t + 1) * half, rows(owner * cut, cut)].astype(
+            ref[half:, t * cut : (t + 1) * cut] = sum_s[1, t * half : (t + 1) * half, lanes_at(owner * cut, cut)].astype(
                 BF16
             )
     low_ref[0:size, :] = mixed_ref[0:size, :].astype(BF16)
@@ -300,7 +338,7 @@
     low_ref[z.cells - size :, :] = mixed_ref[size:, :].astype(BF16)
     for h in range(z.halves):
         split_s[h, :, :] = low_ref[:, h * LANE : (h + 1) * LANE].astype(F32)
-    edge_rows(z, split_s, last_ref, first_ref)
+    edge_rows(z, split_s, edge_refs)
 
 
 def terms_kernel(z, pad_ref, left_ref, right_ref, inner_ref, outer_ref, gain_ref, out_ref, full_s, mixed_s):
@@ -342,7 +380,7 @@
     full_s[edge + z.cols * z.pad_col :, :] = right_ref[...].astype(F32)
 
     def step(j, _):
-        at = rows(j * z.col, z.col)
+        at = rows16(j * z.col, z.col)
         for h in range(z.halves):
             lanes = slice(h * LANE, (h + 1) * LANE)
             spread = taps(z, full_s, taps_s, j, h, True)
@@ -355,43 +393,63 @@
     cut, depth = 2 * z.narrow, aux_ref.shape[0] // 2
     half = z.channels // 2
     for ref, owner in ((mine_ref, own), (other_ref, 1 - own)):
-        ref[0 : z.channels, :] = sum_s[:, rows(owner * cut, cut)].astype(BF16)
+        ref[0 : z.channels, :] = sum_s[:, lanes_at(owner * cut, cut)].astype(BF16)
         for t in range(2):
             ref[z.channels :, t * half : (t + 1) * half] = aux_ref[
-                t * depth : (t + 1) * depth, rows(owner * half, half)
+                t * depth : (t + 1) * depth, lanes_at(owner * half, half)
             ].astype(BF16)
 
 
-def fine_kernel(z, coarse_ref, w_ref, fine_ref, out_ref, back_s):
+def unfold_kernel(z, coarse_ref, centered_ref, patches_ref, back_ref):
     group = 4
+    ones = jnp.full((z.narrow, z.narrow), 1.0 / z.narrow, BF16)
 
     def step(g, _):
-        back = dot_nt(coarse_ref[rows(g * group * z.col, group * z.col), :], w_ref[...])
-        for jj in range(group):
-            j = g * group + jj
-            for p in range(2):
-                for q in range(2):
-                    lanes = slice((p * 2 + q) * z.narrow, (p * 2 + q + 1) * z.narrow)
+        at = rows16(g * group * z.col, group * z.col)
+        low = coarse_ref[at, :]
+        back = dot_nt(jnp.concatenate([low, low], axis=1), centered_ref[...])
+        for p in range(2):
+            for q in range(2):
+                lanes = slice((p * 2 + q) * z.narrow, (p * 2 + q + 1) * z.narrow)
+                unit = patches_ref[at, lanes].astype(F32)
+                up = back[:, lanes]
+                up = up - unit * dot((up * unit).astype(BF16), ones)
+                for jj in range(group):
                     for i in range(z.block_rows):
                         first = jj * z.col + i * SUB
-                        back_s[fine_rows_of(z, j, i, p, q), :] = back[first : first + SUB, lanes]
+                        back_ref[fine_rows_of(z, g * group + jj, i, p, q), :] = up[first : first + SUB]
         return 0
 
     lax.fori_loop(0, z.cols // group, step, 0)
-    ones = jnp.full((z.narrow, z.narrow), 1.0 / z.narrow, BF16)
-
-    def mean(x):
-        high = x.astype(BF16)
-        return dot(high, ones) + dot((x - high.astype(F32)).astype(BF16), ones)
-
-    def norm_step(t, _):
-        at = rows(t * 512, 512)
-        unit, inverse = fine_stats(z, fine_ref[at, :])
-        back = back_s[at, :]
-        out_ref[at, :] = (inverse * (back - mean(back) - unit * mean(back * unit))).astype(BF16)
-        return 0
-
-    lax.fori_loop(0, z.fine // 512, norm_step, 0)
+
+
+def fine_kernel(z, back_ref, inv_ref, out_ref):
+    def step(t, _):
+        at = rows16(t * z.fine_block, z.fine_block)
+        out_ref[at, :] = (inv_ref[at, :] * back_ref[rows(t * z.fine_stride, z.fine_block), :]).astype(BF16)
+        return 0
+
+    lax.fori_loop(0, SUB, step, 0)
+
+
+def second(axis, distance):
+    return lax.axis_index(axis) // distance % 2
+
+
+def add_kernel(step, mine_ref, got_ref, *out_refs):
+    if step is None:
+        out_refs[0][...] = (mine_ref[...].astype(F32) + got_ref[...].astype(F32)).astype(BF16)
+        return
+    half, side = mine_ref.shape[0] // 2, second(*step)
+    for ref, which in zip(out_refs, (side, 1 - side)):
+        at = rows16(which * half, half)
+        ref[...] = (mine_ref[at, :].astype(F32) + got_ref[at, :].astype(F32)).astype(BF16)
+
+
+def join_kernel(step, mine_ref, got_ref, out_ref):
+    half, side = mine_ref.shape[0], second(*step)
+    out_ref[rows16(side * half, half), :] = mine_ref[...]
+    out_ref[rows16((1 - side) * half, half), :] = got_ref[...]
 
 
 def section_kernel(z, inner_ref, outer_ref, out_ref, all_s, split_s):
@@ -413,7 +471,8 @@
         out_ref[:, h * LANE : (h + 1) * LANE] = split_s[h, :, :].astype(BF16)
 
 
-def final_wide_kernel(z, factor, sum_ref, expand_ref, contract_ref):
+def final_wide_kernel(z, factor, step, mine_ref, got_ref, expand_ref, contract_ref, sum_ref):
+    join_kernel(step, mine_ref, got_ref, sum_ref)
     half, cut = z.channels // 2, z.wide // 2
     expand_ref[...] = sum_ref[0:half, :].astype(F32) * factor
     for t in range(2):
@@ -436,37 +495,35 @@
     return lax.ppermute(x, axis, [(i, i ^ distance) for i in range(size)])
 
 
-def reduce_rows(x, halving):
+def add(mine, got, after=(), halve=None):
+    count, width = mine.shape
+    outs = [((count, width), BF16)] if halve is None else [((count // 2, width), BF16)] * 2
+    return kernel_call(functools.partial(add_kernel, halve), outs, (mine, got), after=after)
+
+
+def join(x, step):
+    got = swap(x, *step)
+    return kernel_call(functools.partial(join_kernel, step), [((2 * x.shape[0], x.shape[1]), BF16)], (x, got))[0]
+
+
+def sum_steps(count):
     steps = []
     for axis in ("lat", "lon"):
         distance = 1
         while distance < lax.axis_size(axis):
             steps.append((axis, distance))
             distance *= 2
-    done = []
-    for n, (axis, distance) in enumerate(steps):
-        if halving and n < len(steps) - 1:
-            low = ((lax.axis_index(axis) // distance) % 2) == 0
-            half = x.shape[0] // 2
-            mine = jnp.where(low, x[:half], x[half:])
-            send = jnp.where(low, x[half:], x[:half])
-            got = swap(send, axis, distance)
-            done.append((axis, distance, low))
-        else:
-            mine, got = x, swap(x, axis, distance)
-        x = (mine.astype(F32) + got.astype(F32)).astype(BF16)
-    for axis, distance, low in reversed(done):
-        got = swap(x, axis, distance)
-        x = jnp.concatenate([jnp.where(low, x, got), jnp.where(low, got, x)], axis=0)
-    return x
-
-
-def lat_margins(last, first):
-    lats = lax.axis_size("lat")
-    if lats == 2:
-        got = swap(jnp.where(lax.axis_index("lat") == 0, last, first), "lat", 1)
+    halvings = 0
+    while halvings < len(steps) - 1 and count >> (halvings + 1) >= 2 * SUB:
+        halvings += 1
+    return steps, halvings
+
+
+def lat_margins(last, first=None):
+    if first is None:
+        got = swap(last, "lat", 1)
         return got, got
-    up = [(i, i + 1) for i in range(lats - 1)]
+    up = [(i, i + 1) for i in range(lax.axis_size("lat") - 1)]
     return lax.ppermute(last, "lat", up), lax.ppermute(first, "lat", [(j, i) for i, j in up])
 
 
@@ -478,36 +535,31 @@
 
 def body(fine_field, grad_out, conv_kernel, norm_gain, w_expand, w_contract, w_merge):
     z = Sizes(fine_field, w_merge, w_expand)
-    ch, wide, lats = z.channels, z.wide, lax.axis_size("lat")
+    ch, ff, lats = z.channels, z.wide, lax.axis_size("lat")
     fine = fine_field.reshape(z.fine, z.narrow)
     gain = norm_gain.reshape(1, ch)
-    total_rows = z.lat_rows * lats
-    place = jnp.arange(z.col, dtype=jnp.int32)
-    row = lax.axis_index("lat") * z.lat_rows + (place % SUB) % z.blocks * z.block_rows + place // SUB
-    latitude = math.pi * ((row.astype(F32) + 0.5) / total_rows - 0.5)
-    cosine = jnp.broadcast_to(jnp.cos(latitude)[:, None], (z.col, LANE))
 
     part = functools.partial
     split = ((z.halves, z.cells, LANE), F32)
-    edge = ((z.samples * M * z.cols, ch), BF16)
-    patches, coarse, last, first = kernel_call(
+    edges = [((z.samples * M * z.cols, ch), BF16)] * (1 if lats == 2 else 2)
+    patches, coarse, fine_inv, *send, _ = kernel_call(
         part(merge_kernel, z),
-        [((z.cells, 4 * z.narrow), BF16), ((z.cells, ch), BF16), edge, edge],
+        [((z.cells, 4 * z.narrow), BF16), ((z.cells, ch), BF16), ((z.fine, z.narrow), F32), *edges],
         (fine, w_merge),
-        [((z.fine, z.narrow), F32), split],
-    )
-    before, after = lat_margins(last, first)
-    (weighted,) = kernel_call(
-        part(weighted_kernel, z),
-        [((z.cells, ch), BF16)],
-        (grad_out.reshape(z.cells, ch), cosine),
+        [((SUB * z.fine_stride, z.narrow), F32), split],
+    )
+    before, after = lat_margins(*send)
+    weighted, w_centered, _ = kernel_call(
+        part(weighted_kernel, z, lats),
+        [((z.cells, ch), BF16), ((4 * z.narrow, 2 * ch), BF16)],
+        (grad_out.reshape(z.cells, ch), w_merge),
         [split],
         flops=2_000_000_000,
     )
     slab = ((M * z.pad_col, ch), BF16)
     padded = ((z.cols * z.pad_col, ch), F32)
     pad_scratch = [((2 * z.samples * M * z.cols, ch), F32)]
-    pad, left, right = kernel_call(part(pad_kernel, z, lats), [padded, slab, slab], (coarse, before, after), pad_scratch)
+    pad, left, right, _ = kernel_call(part(pad_kernel, z, lats), [padded, slab, slab], (coarse, before, after), pad_scratch)
     left, right = lon_margins(left, right)
 
     taps_s = ((KS * KS * SUB, ch), F32)
@@ -517,82 +569,104 @@
             ((count, ch), F32),
             ((count, LANE), F32),
             ((count, ch), BF16),
-            ((count, wide), BF16),
-            ((count, wide), BF16),
+            ((count, ff), BF16),
+            ((count, ff), BF16),
             ((count, ch), BF16),
         ]
 
     outer = 2 * M * z.col
     inner = z.cells - outer
-    section_in, mixed_in, expand, contract, gain_sum = kernel_call(
+    section_in, mixed_in, expand, contract, gain_sum, _ = kernel_call(
         part(inner_kernel, z),
-        [((inner, ch), BF16), ((inner, ch), F32), ((ch, wide), F32), ((ch, wide), F32), ((SUB, ch), F32)],
+        [((inner, ch), BF16), ((inner, ch), F32), ((ch, ff), F32), ((ch, ff), F32), ((SUB, ch), F32)],
         (pad, conv_kernel, gain, w_expand, w_contract, coarse, weighted),
         [taps_s] + section_scratch(inner),
         flops=8_000_000_000,
     )
-    section_out, mixed_out, mine, other, low, last, first, gain_sum = kernel_call(
+    section_out, mixed_out, mine, other, low, gain_sum, *send, _ = kernel_call(
         part(outer_kernel, z),
         [
             ((outer, ch), BF16),
             ((outer, ch), F32),
-            ((ch, wide), BF16),
-            ((ch, wide), BF16),
+            ((ch, ff), BF16),
+            ((ch, ff), BF16),
             ((z.cells, ch), BF16),
-            edge,
-            edge,
             ((SUB, ch), F32),
+            *edges,
         ],
         (pad, left, right, conv_kernel, gain, w_expand, w_contract, coarse, weighted)
         + (expand, contract, gain_sum, mixed_in),
-        [taps_s, ((6 * M * z.pad_col, ch), F32), ((2, ch, wide), F32), split] + section_scratch(outer),
+        [taps_s, ((6 * M * z.pad_col, ch), F32), ((2, ch, ff), F32), split] + section_scratch(outer),
         flops=8_000_000_000,
     )
-    before, after = lat_margins(last, first)
-    got = swap(other, "dp", 1)
-    (section_all,) = kernel_call(
+    before, after = lat_margins(*send)
+    steps, halvings = sum_steps(ch)
+    wide, away, token = add(mine, swap(other, "dp", 1), halve=steps[0])
+    pad_low, edge_left, edge_right, token = kernel_call(
+        part(pad_kernel, z, lats), [padded, slab, slab], (low, before, after), pad_scratch, after=(token,)
+    )
+    left_low, right_low = lon_margins(edge_left, edge_right)
+    full = (((z.cols + 2 * M) * z.pad_col, ch), F32)
+    aux, token = kernel_call(
+        part(terms_kernel, z),
+        [((64, ch), F32)],
+        (pad, left, right, mixed_in, mixed_out, gain_sum),
+        [full, ((z.cells, ch), F32)],
+        flops=5_000_000_000,
+        after=(token,),
+    )
+    wide, away, token = add(wide, swap(away, *steps[0]), after=(token,), halve=steps[1])
+    small = ((ch + 32, ch), BF16)
+    back_coarse, mine, other, token = kernel_call(
+        part(back_kernel, z),
+        [((z.cells, ch), BF16), small, small],
+        (pad_low, left_low, right_low, conv_kernel, weighted, patches, aux),
+        [taps_s, full, ((ch, 4 * z.narrow), F32)],
+        flops=5_000_000_000,
+        after=(token,),
+    )
+    for n in range(1, halvings - 1):
+        wide, away, token = add(wide, swap(away, *steps[n]), after=(token,), halve=steps[n + 1])
+    wide, token = add(wide, swap(away, *steps[halvings - 1]), after=(token,))
+    back_fine, token = kernel_call(
+        part(unfold_kernel, z),
+        [((SUB * z.fine_stride, z.narrow), F32)],
+        (back_coarse, w_centered, patches),
+        flops=3_000_000_000,
+        after=(token,),
+    )
+    small_sum, token = add(mine, swap(other, "dp", 1), after=(token,))
+    grad_fine, token = kernel_call(
+        part(fine_kernel, z),
+        [((z.fine, z.narrow), BF16)],
+        (back_fine, fine_inv),
+        flops=2_000_000_000,
+        after=(token,),
+    )
+    section_all, token = kernel_call(
         part(section_kernel, z),
         [((z.cells, ch), BF16)],
         (section_in, section_out),
         [((z.cells, ch), F32), split],
         flops=2_000_000_000,
-    )
-    pad_low, left_low, right_low = kernel_call(
-        part(pad_kernel, z, lats), [padded, slab, slab], (low, before, after), pad_scratch
-    )
-    left_low, right_low = lon_margins(left_low, right_low)
-    full = (((z.cols + 2 * M) * z.pad_col, ch), F32)
-    (aux,) = kernel_call(
-        part(terms_kernel, z),
-        [((64, ch), F32)],
-        (pad, left, right, mixed_in, mixed_out, gain_sum),
-        [full, ((z.cells, ch), F32)],
-        flops=5_000_000_000,
-    )
-    wide_sum = reduce_rows((mine.astype(F32) + got.astype(F32)).astype(BF16), True)
-    small = ((ch + 32, ch), BF16)
-    back_coarse, mine, other = kernel_call(
-        part(back_kernel, z),
-        [((z.cells, ch), BF16), small, small],
-        (pad_low, left_low, right_low, conv_kernel, weighted, patches, aux),
-        [taps_s, full, ((ch, 4 * z.narrow), F32)],
-        flops=5_000_000_000,
-    )
-    got = swap(other, "dp", 1)
-    (grad_fine,) = kernel_call(
-        part(fine_kernel, z),
-        [((z.fine, z.narrow), BF16)],
-        (back_coarse, w_merge, fine),
-        [((z.fine, z.narrow), F32)],
-        flops=5_000_000_000,
-    )
-    small_sum = reduce_rows((mine.astype(F32) + got.astype(F32)).astype(BF16), False)
-    all_cells = z.samples * lax.axis_size("dp") * total_rows * z.cols * lax.axis_size("lon")
+        after=(token,),
+    )
+    small_sum, token = add(small_sum, swap(small_sum, *steps[0]), after=(token,))
+    for step in steps[halvings:]:
+        wide, token = add(wide, swap(wide, *step), after=(token,))
+    for step in steps[1:]:
+        small_sum, token = add(small_sum, swap(small_sum, *step))
+    for step in reversed(steps[1:halvings]):
+        wide = join(wide, step)
+    all_cells = z.samples * lax.axis_size("dp") * z.lat_rows * lats * z.cols * lax.axis_size("lon")
     factor = 1.0 / math.sqrt(all_cells)
-    grad_expand, grad_contract = kernel_call(
-        part(final_wide_kernel, z, factor), [((ch // 2, wide), F32), ((wide // 2, ch), F32)], (wide_sum,)
-    )
-    grad_merge, grad_kernel, grad_gain = kernel_call(
+    grad_expand, grad_contract, _ = kernel_call(
+        part(final_wide_kernel, z, factor, steps[0]),
+        [((ch // 2, ff), F32), ((ff // 2, ch), F32)],
+        (wide, swap(wide, *steps[0])),
+        [((ch, ff), BF16)],
+    )
+    grad_merge, grad_kernel, grad_gain, _ = kernel_call(
         part(final_small_kernel, z, factor),
         [((2 * z.narrow, ch), F32), ((KS * KS, ch // 2), F32), ((1, ch // 2), F32)],
         (small_sum,),

time: 92.5 us -> 87.1 us (0.942)
  waiting for transfers between devices: 22.1 us -> 14.5 us
  starting transfers between devices: 19.5 us -> 22.4 us
    ppermute x2, waiting for transfers between devices: 4.51 us -> 0.01 us  [lon_margins(): lax.ppermute(right, 'lon', up)]
    ppermute x12, starting transfers between devices: 11.4 us -> 14.7 us  [swap(): return lax.ppermute(x, axis, [(i, i ^ distance) for i in range(size)])]
    ppermute x2, waiting for transfers between devices: 1.7 us -> 0.09 us  [lon_margins(): lax.ppermute(left, 'lon', [(j, i) for i, j in up])]
    ppermute x12, waiting for transfers between devices: 15.9 us -> 14.4 us  [swap(): return lax.ppermute(x, axis, [(i, i ^ distance) for i in range(size)])]
    pallas_call x12 -> x22, Pallas kernels: 45.6 us -> 45.9 us  [kernel_call(): pl.pallas_call(run, out_shape=[jax.ShapeDtypeStruct(s, d) for s, d in out...]
    unnamed x18 -> x14, local copies, waits for them, and re-layouts: 3.25 us -> 3.22 us
  transfers between devices with their start and end apart: 16 -> 16, of which waited for: 7 -> 6; matrix products, arithmetic and copies ran while one was open for 1% -> 0% of each run, Pallas kernels for 35% -> 36%
where the time goes in v2:
time: 87.1 us; the launch traced here: 86.9 us
  Pallas kernels  45.9 us (53%)
  starting transfers between devices  22.4 us (26%)
  waiting for transfers between devices  14.5 us (17%)
  local copies, waits for them, and re-layouts  3.22 us (4%)
    pallas_call x22, Pallas kernels, kernel_call(): pl.pallas_call(run, out_shape=[jax.ShapeDtypeStruct(s, d) for s, d in out...  45.9 us
    ppermute x12, starting transfers between devices, swap(): return lax.ppermute(x, axis, [(i, i ^ distance) for i in range(size)])  14.7 us
    ppermute x12, waiting for transfers between devices, swap(): return lax.ppermute(x, axis, [(i, i ^ distance) for i in range(size)])  14.4 us
    ppermute x2, starting transfers between devices, lon_margins(): lax.ppermute(left, 'lon', [(j, i) for i, j in up])  6.06 us
    unnamed x14, local copies, waits for them, and re-layouts  3.22 us
  transfers between devices with their start and end apart: 16, of which 6 were waited for; matrix products, arithmetic and copies ran while one was open for 0% of the time, Pallas kernels for 36%

profile of v2, /device:TPU:0, one launch (start us, length us, event | category | flops | bytes accessed | tf_op | source)
XLA Modules:
  0.0 86.9 jit_solution(11312147341758808526)
XLA Ops:
  0.6 1.2 %copy-done = bf16[2,64,32,128]{3,2,1,0:T(8,128)(2,1)S(1)} copy-done((bf16[2,64,32,128]{3,2,1,0:T(8,128)(2,1)S(1)}, bf16[2,64,32,128]{3,2,1,0:T(8,128)(2,1)}, u32[]{:S(2)}) %copy-start) | copy-done | bytes 1048600
  1.9 0.9 %copy-done.1 = bf16[512,256]{1,0:T(8,128)(2,1)S(1)} copy-done((bf16[512,256]{1,0:T(8,128)(2,1)S(1)}, bf16[512,256]{1,0:T(8,128)(2,1)}, u32[]{:S(2)}) %copy-start.1) | copy-done | bytes 262168
  2.8 4.4 %shard_map.126 = (bf16[1024,512]{1,0:T(8,128)(2,1)S(1)}, bf16[1024,256]{1,0:T(8,128)(2,1)S(1)}, f32[4096,128]{1,0:T(8,128)S(1)}, bf16[96,256]{1,0:T(8,128)(2,1)S(1)}, f32[8,128]{1,0:T(8,128)}) custom-call(bf16[4096,128]{1,0:T(8,128)(2,1)S(1)} %bitcast.6, bf16[512,256]{1,0:T(8,128)(2,1)S(1)} %copy-done.1), custom_call_target="tpu_custom_call" | custom-call | bytes 1310720 | tf_op jit(solution)/shard_map/pallas_call | solution.py:30
  7.2 2.9 %collective-permute-start = (bf16[96,256]{1,0:T(8,128)(2,1)S(1)}, bf16[96,256]{1,0:T(8,128)(2,1)S(1)}, u32[]{:S(2)}, u32[]{:S(2)}) collective-permute-start(bf16[96,256]{1,0:T(8,128)(2,1)S(1)} %get-tuple-element.66), channel_id=1, source_target_pairs={{0,2},{2,0},{1,3},{3,1},{4,6},{6,4},{5,7},{7,5},{8,10},{10,8},{9,1... | collective-permute-start | bytes 147464 | tf_op jit(solution)/shard_map/ppermute | solution.py:495
  10.2 1.0 %copy-done.2 = bf16[2,32,16,256]{3,2,1,0:T(8,128)(2,1)S(1)} copy-done((bf16[2,32,16,256]{3,2,1,0:T(8,128)(2,1)S(1)}, bf16[2,32,16,256]{3,2,1,0:T(8,128)(2,1)}, u32[]{:S(2)}) %copy-start.2) | copy-done | bytes 524312
  11.2 1.6 %shard_map.128 = (bf16[1024,256]{1,0:T(8,128)(2,1)S(1)}, bf16[512,512]{1,0:T(8,128)(2,1)S(1)}, f32[8,128]{1,0:T(8,128)}) custom-call(bf16[1024,256]{1,0:T(8,128)(2,1)S(1)} %bitcast.7, bf16[512,256]{1,0:T(8,128)(2,1)S(1)} %copy-done.1), custom_call_target="tpu_custom_call" | custom-call | flops 2000000000 | bytes 786432 | tf_op jit(solution)/shard_map/pallas_call | solution.py:30
  12.8 0.0 collective-permute-done.refs_1_.refs_2_
  12.8 1.2 %shard_map.127 = (f32[1792,256]{1,0:T(8,128)S(1)}, bf16[336,256]{1,0:T(8,128)(2,1)S(1)}, bf16[336,256]{1,0:T(8,128)(2,1)S(1)}, f32[8,128]{1,0:T(8,128)}) custom-call(bf16[1024,256]{1,0:T(8,128)(2,1)S(1)} %get-tuple-element.65.refs_0_.refs_5_.refs_7_, bf16[96,256]{1,0:T(8,128)(2,1)S(1)} %collective-permute-done.refs_1_.refs_2_, ...), custom_call_target="tpu_custom_call" | custom-call | bytes 622592 | tf_op jit(solution)/shard_map/pallas_call | solution.py:30
  14.0 1.6 %collective-permute-start.1 = (bf16[336,256]{1,0:T(8,128)(2,1)S(1)}, bf16[336,256]{1,0:T(8,128)(2,1)S(1)}, u32[]{:S(2)}, u32[]{:S(2)}) collective-permute-start(bf16[336,256]{1,0:T(8,128)(2,1)S(1)} %get-tuple-element.70), channel_id=1, source_target_pairs={{0,4},{4,8},{8,12},{12,0},{1,5},{5,9},{9,13},{13,1},{2,6},{6,10},{... | collective-permute-start | bytes 516104 | tf_op jit(solution)/shard_map/ppermute | solution.py:533
  15.6 2.2 %collective-permute-start.2 = (bf16[336,256]{1,0:T(8,128)(2,1)S(1)}, bf16[336,256]{1,0:T(8,128)(2,1)S(1)}, u32[]{:S(2)}, u32[]{:S(2)}) collective-permute-start(bf16[336,256]{1,0:T(8,128)(2,1)S(1)} %get-tuple-element.71), channel_id=1, source_target_pairs={{4,0},{8,4},{12,8},{0,12},{5,1},{9,5},{13,9},{1,13},{6,2},{10,6},{... | collective-permute-start | bytes 516104 | tf_op jit(solution)/shard_map/ppermute | solution.py:533
  17.8 9.5 %shard_map.129 = (bf16[640,256]{1,0:T(8,128)(2,1)S(1)}, f32[640,256]{1,0:T(8,128)S(1)}, f32[256,1024]{1,0:T(8,128)S(1)}, f32[256,1024]{1,0:T(8,128)S(1)}, f32[8,256]{1,0:T(8,128)S(1)}, /*index=5*/f32[8,128]{1,0:T(8,128)}) custom-call(f32[1792,256]{1,0:T(8,128)S(1)} %get-tuple-element.67.refs_0_, f32[49,256]{1,0:T(8,128)S(1)} %copy-done.5, ...), custom_call_target="tpu_custom_call" | custom-call | flops 8000000000 | bytes 3983360 | tf_op jit(solution)/shard_map/pallas_call | solution.py:30
  27.3 0.0 collective-permute-done.2.refs_2_
  27.4 7.1 %shard_map.130 = (bf16[384,256]{1,0:T(8,128)(2,1)S(1)}, f32[384,256]{1,0:T(8,128)S(1)}, bf16[256,1024]{1,0:T(8,128)(2,1)S(1)}, bf16[256,1024]{1,0:T(8,128)(2,1)S...) custom-call(f32[1792,256]{1,0:T(8,128)S(1)} %get-tuple-element.67.re, ...), custom_call_target="tpu_custom_call" | custom-call | flops 8000000000 | bytes 7088128 | tf_op jit(solution)/shard_map/pallas_call | solution.py:30
  34.5 0.0 collective-permute-start.4
  34.5 1.4 %collective-permute-start.3 = (bf16[96,256]{1,0:T(8,128)(2,1)S(1)}, bf16[96,256]{1,0:T(8,128)(2,1)S(1)}, u32[]{:S(2)}, u32[]{:S(2)}) collective-permute-start(bf16[96,256]{1,0:T(8,128)(2,1)S(1)} %get-tuple-element.78), channel_id=1, source_target_pairs={{0,2},{2,0},{1,3},{3,1},{4,6},{6,4},{5,7},{7,5},{8,10},{10,8},{9,1... | collective-permute-start | bytes 147464 | tf_op jit(solution)/shard_map/ppermute | solution.py:495
  35.9 0.5 collective-permute-done.4.refs_1_
  36.4 0.1 shard_map.131
  36.5 1.5 %collective-permute-start.7 = (bf16[128,1024]{1,0:T(8,128)(2,1)S(1)}, bf16[128,1024]{1,0:T(8,128)(2,1)S(1)}, u32[]{:S(2)}, u32[]{:S(2)}) collective-permute-start(bf16[128,1024]{1,0:T(8,128)(2,1)S(1)} %get-tuple-element.91), channel_id=1, source_target_pairs={{0,2},{2,0},{1,3},{3,1},{4,6},{6,4},{5,7},{7,5},{8,10},{10,8},{9,1... | collective-permute-start | bytes 786440 | tf_op jit(solution)/shard_map/ppermute | solution.py:495
  38.0 0.6 collective-permute-done.3.refs_1_.refs_2_
  38.6 0.6 shard_map.132
  39.2 0.1 collective-permute-start.5
  39.3 3.8 %collective-permute-start.6 = (bf16[336,256]{1,0:T(8,128)(2,1)S(1)}, bf16[336,256]{1,0:T(8,128)(2,1)S(1)}, u32[]{:S(2)}, u32[]{:S(2)}) collective-permute-start(bf16[336,256]{1,0:T(8,128)(2,1)S(1)} %get-tuple-element.84), channel_id=1, source_target_pairs={{4,0},{8,4},{12,8},{0,12},{5,1},{9,5},{13,9},{1,13},{6,2},{10,6},{... | collective-permute-start | bytes 516104 | tf_op jit(solution)/shard_map/ppermute | solution.py:533
  43.1 5.8 %shard_map.133 = (f32[64,256]{1,0:T(8,128)S(1)}, f32[8,128]{1,0:T(8,128)S(1)}) custom-call(f32[1792,256]{1,0:T(8,128)S(1)} %get-tuple-element.67.refs_0_, bf16[336,256]{1,0:T(8,128)(2,1)S(1)} %collective-permute-done.1.refs_1_, bf16[336,256]{1,0:T(8,128)(2,1)S(1)} %collective-permute-done.2.refs_2_, f32[640,256]{1,0:T(8,128)S(1)} %get-tuple-element.75.refs_12_.refs_3_, ...), custom_call_target="tpu_custom_call" | custom-call | flops 5000000000 | bytes 3235840 | tf_op jit(solution)/shard_map/pallas_call | solution.py:30
  48.9 0.1 shard_map.134
  49.0 0.1 collective-permute-start.8
  49.1 0.0 collective-permute-done.5.refs_1_
  49.1 0.1 collective-permute-done.6.refs_2_
  49.2 5.8 %shard_map.135 = (bf16[1024,256]{1,0:T(8,128)(2,1)S(1)}, bf16[288,256]{1,0:T(8,128)(2,1)S(1)}, bf16[288,256]{1,0:T(8,128)(2,1)S(1)}, f32[8,128]{1,0:T(8,128)S(1)}) custom-call(f32[1792,256]{1,0:T(8,128)S(1)} %get-tuple-element.82.refs_0_, bf16[336,256]{1,0:T(8,128)(2,1)S(1)} %collective-permute-done.5.refs_1_, ...), custom_call_target="tpu_custom_call" | custom-call | flops 5000000000 | bytes 3867648 | tf_op jit(solution)/shard_map/pallas_call | solution.py:30
  55.1 0.1 collective-permute-start.9
  55.1 0.0 collective-permute-done.8.refs_1_
  55.2 3.5 %collective-permute-start.13 = (bf16[64,1024]{1,0:T(8,128)(2,1)S(1)}, bf16[64,1024]{1,0:T(8,128)(2,1)S(1)}, u32[]{:S(2)}, u32[]{:S(2)}) collective-permute-start(bf16[64,1024]{1,0:T(8,128)(2,1)S(1)} %get-tuple-element.116.refs_0_), channel_id=1, source_target_pairs={{0,8},{4,12},{8,0},{12,4},{1,9},{5,13},{9,1},{13,5},{2,10},{6,14},... | collective-permute-start | bytes 393224 | tf_op jit(solution)/shard_map/ppermute | solution.py:495
  58.6 2.1 %shard_map.137 = (f32[4160,128]{1,0:T(8,128)S(1)}, f32[8,128]{1,0:T(8,128)S(1)}) custom-call(bf16[1024,256]{1,0:T(8,128)(2,1)S(1)} %get-tuple-element.94.refs_0_, bf16[512,512]{1,0:T(8,128)(2,1)S(1)} %get-tuple-element.95.refs_1_, bf16[1024,512]{1,0:T(8,128)(2,1)S(1)} %get-tuple-element.85.refs_5_.refs_2_, f32[8,128]{1,0:T(8,128)S(1)} %get-tuple-element.99.refs_3_), custom_call_target="tpu_custom_call" | custom-call | flops 3000000000 | bytes 2097152 | tf_op jit(solution)/shard_map/pallas_call | solution.py:30
  60.7 0.0 collective-permute-done.9.refs_1_
  60.8 1.5 %collective-permute-start.10 = (bf16[288,256]{1,0:T(8,128)(2,1)S(1)}, bf16[288,256]{1,0:T(8,128)(2,1)S(1)}, u32[]{:S(2)}, u32[]{:S(2)}) collective-permute-start(bf16[288,256]{1,0:T(8,128)(2,1)S(1)} %get-tuple-element.109.refs_0_), channel_id=1, source_target_pairs={{0,2},{2,0},{1,3},{3,1},{4,6},{6,4},{5,7},{7,5},{8,10},{10,8},{9,1... | collective-permute-start | bytes 442376 | tf_op jit(solution)/shard_map/ppermute | solution.py:495
  62.3 1.3 %shard_map.139 = (bf16[4096,128]{1,0:T(8,128)(2,1)}, f32[8,128]{1,0:T(8,128)S(1)}) custom-call(f32[4160,128]{1,0:T(8,128)S(1)} %get-tuple-element.100.refs_0_, f32[4096,128]{1,0:T(8,128)S(1)} %get-tuple-element.101.refs_1_, f32[8,128]{1,0:T(8,128)S(1)} %get-tuple-element.105.refs_2_), custom_call_target="tpu_custom_call" | custom-call | flops 2000000000 | bytes 4227072 | tf_op jit(solution)/shard_map/pallas_call | solution.py:30
  63.5 1.8 %shard_map.140 = (bf16[1024,256]{1,0:T(8,128)(2,1)}, f32[8,128]{1,0:T(8,128)S(1)}) custom-call(bf16[640,256]{1,0:T(8,128)(2,1)S(1)} %get-tuple-element.69.refs_0_, bf16[384,256]{1,0:T(8,128)(2,1)S(1)} %get-tuple-element.76.refs_1_, f32[8,128]{1,0:T(8,128)S(1)} %get-tuple-element.106.refs_2_), custom_call_target="tpu_custom_call" | custom-call | flops 2000000000 | bytes 524288 | tf_op jit(solution)/shard_map/pallas_call | solution.py:30
  65.3 1.4 %collective-permute-done.10.refs_1_ = bf16[288,256]{1,0:T(8,128)(2,1)S(1)} collective-permute-done((bf16[288,256]{1,0:T(8,128)(2,1)S(1)}, bf16[288,256]{1,0:T(8,128)(2,1)S(1)}, u32[]{:S(2)}, u32[]{:S(2)}) %collective-permute-start.10) | collective-permute-done | bytes 147488 | tf_op jit(solution)/shard_map/ppermute | solution.py:495
  66.8 0.6 shard_map.145
  67.4 2.0 %collective-permute-start.11 = (bf16[288,256]{1,0:T(8,128)(2,1)S(1)}, bf16[288,256]{1,0:T(8,128)(2,1)S(1)}, u32[]{:S(2)}, u32[]{:S(2)}) collective-permute-start(bf16[288,256]{1,0:T(8,128)(2,1)S(1)} %get-tuple-element.111.refs_0_), channel_id=1, source_target_pairs={{0,4},{4,0},{8,12},{12,8},{1,5},{5,1},{9,13},{13,9},{2,6},{6,2},{1... | collective-permute-start | bytes 442376 | tf_op jit(solution)/shard_map/ppermute | solution.py:495
  69.5 4.3 %collective-permute-done.14.refs_1_ = bf16[64,1024]{1,0:T(8,128)(2,1)S(1)} collective-permute-done((bf16[64,1024]{1,0:T(8,128)(2,1)S(1)}, bf16[64,1024]{1,0:T(8,128)(2,1)S(1)}, u32[]{:S(2)}, u32[]{:S(2)}) %collective-permute-start.14) | collective-permute-done | bytes 131104 | tf_op jit(solution)/shard_map/ppermute | solution.py:495
  73.8 0.6 shard_map.146
  74.4 1.4 %collective-permute-start.15 = (bf16[128,1024]{1,0:T(8,128)(2,1)S(1)}, bf16[128,1024]{1,0:T(8,128)(2,1)S(1)}, u32[]{:S(2)}, u32[]{:S(2)}) collective-permute-start(bf16[128,1024]{1,0:T(8,128)(2,1)S(1)} %get-tuple-element.119.refs_0_), channel_id=1, source_target_pairs={{0,2},{2,0},{1,3},{3,1},{4,6},{6,4},{5,7},{7,5},{8,10},{10,8},{9,1... | collective-permute-start | bytes 786440 | tf_op jit(solution)/shard_map/ppermute | solution.py:495
  75.8 0.6 shard_map.142
  76.4 0.3 collective-permute-start.12
  76.8 7.5 %collective-permute-done.12.refs_1_ = bf16[288,256]{1,0:T(8,128)(2,1)S(1)} collective-permute-done((bf16[288,256]{1,0:T(8,128)(2,1)S(1)}, bf16[288,256]{1,0:T(8,128)(2,1)S(1)}, u32[]{:S(2)}, u32[]{:S(2)}) %collective-permute-start.12) | collective-permute-done | bytes 147488 | tf_op jit(solution)/shard_map/ppermute | solution.py:495
  84.3 0.6 shard_map.143
  84.9 0.8 shard_map.144
  85.7 1.2 %shard_map.147 = (f32[128,1024]{1,0:T(8,128)}, f32[512,256]{1,0:T(8,128)}, f32[8,128]{1,0:T(8,128)}) custom-call(bf16[128,1024]{1,0:T(8,128)(2,1)S(1)} %get-tuple-element.119.refs_0_, bf16[128,1024]{1,0:T(8,128)(2,1)S(1)} %collective-permute-done.15.refs_1_), custom_call_target="tpu_custom_call" | custom-call | bytes 524288 | tf_op jit(solution)/shard_map/pallas_call | solution.py:30
  (20 shorter events, 0.2 us)
Async XLA Ops:
  0.6 1.2 %copy-start = (bf16[2,64,32,128]{3,2,1,0:T(8,128)(2,1)S(1)}, bf16[2,64,32,128]{3,2,1,0:T(8,128)(2,1)}, u32[]{:S(2)}) copy-start(bf16[2,64,32,128]{3,2,1,0:T(8,128)(2,1)} %param.7) | copy-start | bytes 3145732
  1.9 0.9 %copy-start.1 = (bf16[512,256]{1,0:T(8,128)(2,1)S(1)}, bf16[512,256]{1,0:T(8,128)(2,1)}, u32[]{:S(2)}) copy-start(bf16[512,256]{1,0:T(8,128)(2,1)} %refs_1_.4) | copy-start | bytes 786436
  7.2 5.6 %collective-permute-start = (bf16[96,256]{1,0:T(8,128)(2,1)S(1)}, bf16[96,256]{1,0:T(8,128)(2,1)S(1)}, u32[]{:S(2)}, u32[]{:S(2)}) collective-permute-start(bf16[96,256]{1,0:T(8,128)(2,1)S(1)} %get-tuple-element.66), channel_id=1, source_target_pairs={{0,2},{2,0},{1,3},{3,1},{4,6},{6,4},{5,7},{7,5},{8,10},{10,8},{9,1... | collective-permute-start | bytes 147464 | tf_op jit(solution)/shard_map/ppermute | solution.py:495
  10.2 1.0 %copy-start.2 = (bf16[2,32,16,256]{3,2,1,0:T(8,128)(2,1)S(1)}, bf16[2,32,16,256]{3,2,1,0:T(8,128)(2,1)}, u32[]{:S(2)}) copy-start(bf16[2,32,16,256]{3,2,1,0:T(8,128)(2,1)} %param.8) | copy-start | bytes 1572868
  11.2 6.6 %copy-start.3 = (bf16[256,1024]{1,0:T(8,128)(2,1)S(1)}, bf16[256,1024]{1,0:T(8,128)(2,1)}, u32[]{:S(2)}) copy-start(bf16[256,1024]{1,0:T(8,128)(2,1)} %refs_5_.1) | copy-start | bytes 1572868
  11.2 6.6 %copy-start.4 = (bf16[1024,256]{1,0:T(8,128)(2,1)S(1)}, bf16[1024,256]{1,0:T(8,128)(2,1)}, u32[]{:S(2)}) copy-start(bf16[1024,256]{1,0:T(8,128)(2,1)} %refs_6_.1) | copy-start | bytes 1572868
  11.2 6.6 %copy-start.5 = (f32[49,256]{1,0:T(8,128)S(1)}, f32[49,256]{1,0:T(8,128)}, u32[]{:S(2)}) copy-start(f32[49,256]{1,0:T(8,128)} %refs_3_.5) | copy-start | bytes 150532
  11.2 6.6 %copy-start.6 = (f32[256]{0:T(256)S(1)}, f32[256]{0:T(256)}, u32[]{:S(2)}) copy-start(f32[256]{0:T(256)} %param.10) | copy-start | bytes 3076
  14.0 13.4 %collective-permute-start.1 = (bf16[336,256]{1,0:T(8,128)(2,1)S(1)}, bf16[336,256]{1,0:T(8,128)(2,1)S(1)}, u32[]{:S(2)}, u32[]{:S(2)}) collective-permute-start(bf16[336,256]{1,0:T(8,128)(2,1)S(1)} %get-tuple-element.70), channel_id=1, source_target_pairs={{0,4},{4,8},{8,12},{12,0},{1,5},{5,9},{9,13},{13,1},{2,6},{6,10},{... | collective-permute-start | bytes 516104 | tf_op jit(solution)/shard_map/ppermute | solution.py:533
  15.6 11.8 %collective-permute-start.2 = (bf16[336,256]{1,0:T(8,128)(2,1)S(1)}, bf16[336,256]{1,0:T(8,128)(2,1)S(1)}, u32[]{:S(2)}, u32[]{:S(2)}) collective-permute-start(bf16[336,256]{1,0:T(8,128)(2,1)S(1)} %get-tuple-element.71), channel_id=1, source_target_pairs={{4,0},{8,4},{12,8},{0,12},{5,1},{9,5},{13,9},{1,13},{6,2},{10,6},{... | collective-permute-start | bytes 516104 | tf_op jit(solution)/shard_map/ppermute | solution.py:533
  34.5 1.9 %collective-permute-start.4 = (bf16[256,1024]{1,0:T(8,128)(2,1)S(1)}, bf16[256,1024]{1,0:T(8,128)(2,1)S(1)}, u32[]{:S(2)}, u32[]{:S(2)}) collective-permute-start(bf16[256,1024]{1,0:T(8,128)(2,1)S(1)} %get-tuple-element.80), channel_id=1, source_target_pairs={{0,1},{1,0},{2,3},{3,2},{4,5},{5,4},{6,7},{7,6},{8,9},{9,8},{10,11... | collective-permute-start | bytes 1572872 | tf_op jit(solution)/shard_map/ppermute | solution.py:495
  34.5 4.2 %collective-permute-start.3 = (bf16[96,256]{1,0:T(8,128)(2,1)S(1)}, bf16[96,256]{1,0:T(8,128)(2,1)S(1)}, u32[]{:S(2)}, u32[]{:S(2)}) collective-permute-start(bf16[96,256]{1,0:T(8,128)(2,1)S(1)} %get-tuple-element.78), channel_id=1, source_target_pairs={{0,2},{2,0},{1,3},{3,1},{4,6},{6,4},{5,7},{7,5},{8,10},{10,8},{9,1... | collective-permute-start | bytes 147464 | tf_op jit(solution)/shard_map/ppermute | solution.py:495
  36.5 12.4 %collective-permute-start.7 = (bf16[128,1024]{1,0:T(8,128)(2,1)S(1)}, bf16[128,1024]{1,0:T(8,128)(2,1)S(1)}, u32[]{:S(2)}, u32[]{:S(2)}) collective-permute-start(bf16[128,1024]{1,0:T(8,128)(2,1)S(1)} %get-tuple-element.91), channel_id=1, source_target_pairs={{0,2},{2,0},{1,3},{3,1},{4,6},{6,4},{5,7},{7,5},{8,10},{10,8},{9,1... | collective-permute-start | bytes 786440 | tf_op jit(solution)/shard_map/ppermute | solution.py:495
  39.2 9.9 %collective-permute-start.5 = (bf16[336,256]{1,0:T(8,128)(2,1)S(1)}, bf16[336,256]{1,0:T(8,128)(2,1)S(1)}, u32[]{:S(2)}, u32[]{:S(2)}) collective-permute-start(bf16[336,256]{1,0:T(8,128)(2,1)S(1)} %get-tuple-element.83), channel_id=1, source_target_pairs={{0,4},{4,8},{8,12},{12,0},{1,5},{5,9},{9,13},{13,1},{2,6},{6,10},{... | collective-permute-start | bytes 516104 | tf_op jit(solution)/shard_map/ppermute | solution.py:533
  39.3 9.9 %collective-permute-start.6 = (bf16[336,256]{1,0:T(8,128)(2,1)S(1)}, bf16[336,256]{1,0:T(8,128)(2,1)S(1)}, u32[]{:S(2)}, u32[]{:S(2)}) collective-permute-start(bf16[336,256]{1,0:T(8,128)(2,1)S(1)} %get-tuple-element.84), channel_id=1, source_target_pairs={{4,0},{8,4},{12,8},{0,12},{5,1},{9,5},{13,9},{1,13},{6,2},{10,6},{... | collective-permute-start | bytes 516104 | tf_op jit(solution)/shard_map/ppermute | solution.py:533
  49.0 6.1 %collective-permute-start.8 = (bf16[64,1024]{1,0:T(8,128)(2,1)S(1)}, bf16[64,1024]{1,0:T(8,128)(2,1)S(1)}, u32[]{:S(2)}, u32[]{:S(2)}) collective-permute-start(bf16[64,1024]{1,0:T(8,128)(2,1)S(1)} %get-tuple-element.97), channel_id=1, source_target_pairs={{0,4},{4,0},{8,12},{12,8},{1,5},{5,1},{9,13},{13,9},{2,6},{6,2},{1... | collective-permute-start | bytes 393224 | tf_op jit(solution)/shard_map/ppermute | solution.py:495
  55.1 5.7 %collective-permute-start.9 = (bf16[288,256]{1,0:T(8,128)(2,1)S(1)}, bf16[288,256]{1,0:T(8,128)(2,1)S(1)}, u32[]{:S(2)}, u32[]{:S(2)}) collective-permute-start(bf16[288,256]{1,0:T(8,128)(2,1)S(1)} %get-tuple-element.103), channel_id=1, source_target_pairs={{0,1},{1,0},{2,3},{3,2},{4,5},{5,4},{6,7},{7,6},{8,9},{9,8},{10,11... | collective-permute-start | bytes 442376 | tf_op jit(solution)/shard_map/ppermute | solution.py:495
  55.2 11.6 %collective-permute-start.13 = (bf16[64,1024]{1,0:T(8,128)(2,1)S(1)}, bf16[64,1024]{1,0:T(8,128)(2,1)S(1)}, u32[]{:S(2)}, u32[]{:S(2)}) collective-permute-start(bf16[64,1024]{1,0:T(8,128)(2,1)S(1)} %get-tuple-element.116.refs_0_), channel_id=1, source_target_pairs={{0,8},{4,12},{8,0},{12,4},{1,9},{5,13},{9,1},{13,5},{2,10},{6,14},... | collective-permute-start | bytes 393224 | tf_op jit(solution)/shard_map/ppermute | solution.py:495
  60.8 6.0 %collective-permute-start.10 = (bf16[288,256]{1,0:T(8,128)(2,1)S(1)}, bf16[288,256]{1,0:T(8,128)(2,1)S(1)}, u32[]{:S(2)}, u32[]{:S(2)}) collective-permute-start(bf16[288,256]{1,0:T(8,128)(2,1)S(1)} %get-tuple-element.109.refs_0_), channel_id=1, source_target_pairs={{0,2},{2,0},{1,3},{3,1},{4,6},{6,4},{5,7},{7,5},{8,10},{10,8},{9,1... | collective-permute-start | bytes 442376 | tf_op jit(solution)/shard_map/ppermute | solution.py:495
  67.4 6.4 %collective-permute-start.14 = (bf16[64,1024]{1,0:T(8,128)(2,1)S(1)}, bf16[64,1024]{1,0:T(8,128)(2,1)S(1)}, u32[]{:S(2)}, u32[]{:S(2)}) collective-permute-start(bf16[64,1024]{1,0:T(8,128)(2,1)S(1)} %get-tuple-element.118.refs_0_), channel_id=1, source_target_pairs={{0,4},{4,0},{8,12},{12,8},{1,5},{5,1},{9,13},{13,9},{2,6},{6,2},{1... | collective-permute-start | bytes 393224 | tf_op jit(solution)/shard_map/ppermute | solution.py:495
  67.4 8.4 %collective-permute-start.11 = (bf16[288,256]{1,0:T(8,128)(2,1)S(1)}, bf16[288,256]{1,0:T(8,128)(2,1)S(1)}, u32[]{:S(2)}, u32[]{:S(2)}) collective-permute-start(bf16[288,256]{1,0:T(8,128)(2,1)S(1)} %get-tuple-element.111.refs_0_), channel_id=1, source_target_pairs={{0,4},{4,0},{8,12},{12,8},{1,5},{5,1},{9,13},{13,9},{2,6},{6,2},{1... | collective-permute-start | bytes 442376 | tf_op jit(solution)/shard_map/ppermute | solution.py:495
  74.4 11.3 %collective-permute-start.15 = (bf16[128,1024]{1,0:T(8,128)(2,1)S(1)}, bf16[128,1024]{1,0:T(8,128)(2,1)S(1)}, u32[]{:S(2)}, u32[]{:S(2)}) collective-permute-start(bf16[128,1024]{1,0:T(8,128)(2,1)S(1)} %get-tuple-element.119.refs_0_), channel_id=1, source_target_pairs={{0,2},{2,0},{1,3},{3,1},{4,6},{6,4},{5,7},{7,5},{8,10},{10,8},{9,1... | collective-permute-start | bytes 786440 | tf_op jit(solution)/shard_map/ppermute | solution.py:495
  76.4 7.8 %collective-permute-start.12 = (bf16[288,256]{1,0:T(8,128)(2,1)S(1)}, bf16[288,256]{1,0:T(8,128)(2,1)S(1)}, u32[]{:S(2)}, u32[]{:S(2)}) collective-permute-start(bf16[288,256]{1,0:T(8,128)(2,1)S(1)} %get-tuple-element.112.refs_0_), channel_id=1, source_target_pairs={{0,8},{4,12},{8,0},{12,4},{1,9},{5,13},{9,1},{13,5},{2,10},{6,14},... | collective-permute-start | bytes 442376 | tf_op jit(solution)/shard_map/ppermute | solution.py:495

commit v3 on v2

--- a/solution.py
+++ b/solution.py
@@ -30,7 +30,7 @@
     return pl.pallas_call(
         run,
         out_shape=[jax.ShapeDtypeStruct(s, d) for s, d in outs],
-        in_specs=[whole] * count + [whole] * len(after),
+        in_specs=[whole] * (count + len(after)),
         out_specs=[whole] * len(outs),
         scratch_shapes=[pltpu.VMEM(s, d) for s, d in scratch],
         compiler_params=pltpu.CompilerParams(vmem_limit_bytes=held + 8 * 2**20),
@@ -115,14 +115,11 @@
 
 def merge_kernel(z, fine_ref, w_ref, patches_ref, coarse_ref, inv_ref, *rest):
     *edge_refs, unit_s, split_s = rest
-    def norm_step(t, _):
-        at = rows16(t * z.fine_block, z.fine_block)
+    for t in range(SUB):
+        at = slice(t * z.fine_block, (t + 1) * z.fine_block)
         unit, inverse = fine_stats(z, fine_ref[at, :])
-        unit_s[rows(t * z.fine_stride, z.fine_block), :] = unit
+        unit_s[t * z.fine_stride : t * z.fine_stride + z.fine_block, :] = unit
         inv_ref[at, :] = inverse
-        return 0
-
-    lax.fori_loop(0, SUB, norm_step, 0)
     group = 4
 
     def step(g, _):
@@ -144,7 +141,7 @@
             split_s[h, at, :] = low[:, h * LANE : (h + 1) * LANE].astype(F32)
         return 0
 
-    lax.fori_loop(0, z.cols // group, step, 0)
+    lax.fori_loop(0, z.cols // group, step, 0, unroll=True)
     edge_rows(z, split_s, edge_refs)
 
 
@@ -174,39 +171,50 @@
             out_ref[rows16(j * z.col, z.col), h * LANE : (h + 1) * LANE] = (col * cosine).astype(BF16)
         return 0
 
-    lax.fori_loop(0, z.cols, step, 0)
-
-
-def pad_kernel(z, lats, own_ref, before_ref, after_ref, pad_ref, left_ref, right_ref, halo_s):
+    lax.fori_loop(0, z.cols, step, 0, unroll=8)
+
+
+def pad_column(z, own, line, ref, start):
+    place = lax.broadcasted_iota(jnp.int32, (SUB, z.channels), 0)
+    ref[rows(start + M * SUB, z.col), :] = own
+    for r in range(M):
+        i = z.block_rows - M + r
+        top = pltpu.roll(own[i * SUB : (i + 1) * SUB], 1, 0)
+        low = pltpu.roll(own[r * SUB : (r + 1) * SUB], SUB - 1, 0)
+        for s in range(z.samples):
+            top = jnp.where(place == s * z.blocks, line(0, r, s), top)
+            low = jnp.where(place == (s + 1) * z.blocks - 1, line(1, r, s), low)
+        ref[rows(start + r * SUB, SUB), :] = top
+        ref[rows(start + (M + z.block_rows + r) * SUB, SUB), :] = low
+
+
+def pad_kernel(z, lats, own_ref, before_ref, after_ref, pad_ref, left_ref, right_ref, halo_s, slab_s):
     lat = lax.axis_index("lat")
     near = z.samples * M * z.cols
     halo_s[0:near, :] = jnp.where(lat > 0, before_ref[...].astype(F32), 0.0)
     halo_s[near : 2 * near, :] = jnp.where(lat < lats - 1, after_ref[...].astype(F32), 0.0)
-    place = lax.broadcasted_iota(jnp.int32, (SUB, z.channels), 0)
-
-    def halo(base, r, j, block, inner):
-        for s in range(z.samples):
-            line = halo_s[pl.ds(base + (r * z.samples + s) * z.cols + j, 1), :]
-            inner = jnp.where(place == s * z.blocks + block, line, inner)
-        return inner
 
     def step(j, _):
         own = own_ref[rows16(j * z.col, z.col), :].astype(F32)
-        pad_ref[rows(j * z.pad_col + M * SUB, SUB * z.block_rows), :] = own
-        for r in range(M):
-            i = z.block_rows - M + r
-            up = pltpu.roll(own[i * SUB : (i + 1) * SUB], 1, 0)
-            down = pltpu.roll(own[r * SUB : (r + 1) * SUB], SUB - 1, 0)
-            pad_ref[rows(j * z.pad_col + r * SUB, SUB), :] = halo(0, r, j, 0, up)
-            pad_ref[rows(j * z.pad_col + (M + z.block_rows + r) * SUB, SUB), :] = halo(
-                near, r, j, z.blocks - 1, down
-            )
-        return 0
-
-    lax.fori_loop(0, z.cols, step, 0)
-    edge = M * z.pad_col
-    left_ref[...] = pad_ref[0:edge, :].astype(BF16)
-    right_ref[...] = pad_ref[z.cols * z.pad_col - edge :, :].astype(BF16)
+        line = lambda side, r, s: halo_s[pl.ds(side * near + (r * z.samples + s) * z.cols + j, 1), :]
+        pad_column(z, own, line, pad_ref, j * z.pad_col)
+        return 0
+
+    lax.fori_loop(0, z.cols, step, 0, unroll=4)
+    own = M * z.col
+    slab_s[own:, :] = jnp.zeros_like(slab_s[own:, :])
+    for ref, first in ((left_ref, 0), (right_ref, z.cols - M)):
+        for t in range(2 * M * z.samples):
+            slab_s[own + t * M : own + (t + 1) * M, :] = halo_s[t * z.cols + first : t * z.cols + first + M, :]
+        ref[0:own, :] = own_ref[first * z.col : (first + M) * z.col, :]
+        ref[own:, :] = slab_s[own:, :].astype(BF16)
+
+
+def unpack_slab(z, slab_ref, slab_s, ref, start):
+    slab_s[...] = slab_ref[...].astype(F32)
+    for c in range(M):
+        line = lambda side, r, s: slab_s[pl.ds(M * z.col + ((side * M + r) * z.samples + s) * M + c, 1), :]
+        pad_column(z, slab_s[c * z.col : (c + 1) * z.col, :], line, ref, start + c * z.pad_col)
 
 
 def taps(z, pad, taps_s, start, h, flipped):
@@ -260,7 +268,7 @@
             normed_s[at, lanes] = (unit * gain_ref[:, lanes]).astype(BF16)
         return 0
 
-    lax.fori_loop(0, count // z.col, step, 0)
+    lax.fori_loop(0, count // z.col, step, 0, unroll=2)
     for low, full, size in groups:
         weighted_s[low : low + size, :] = weighted_ref[full : full + size, :]
     gain_sum = jnp.zeros((SUB, z.channels), F32)
@@ -305,16 +313,14 @@
 def outer_kernel(
     z, pad_ref, left_ref, right_ref, kern_ref, gain_ref, we_ref, wc_ref, coarse_ref, weighted_ref,
     expand_ref, contract_ref, gain_sum_ref, inner_mixed_ref,
-    section_ref, mixed_ref, mine_ref, other_ref, low_ref, gain_out_ref, *rest,
+    section_ref, mixed_ref, mine_ref, other_ref, low_ref, gain_out_ref, left_out_ref, right_out_ref, *rest,
 ):
-    *edge_refs, taps_s, edge_s, sum_s, split_s = rest[:-6]
+    *edge_refs, taps_s, edge_s, sum_s, split_s, slab_s = rest[:-6]
     scratch = rest[-6:]
     spread_taps(z, kern_ref, taps_s)
-    edge, near = M * z.pad_col, 2 * M * z.pad_col
-    edge_s[0:edge, :] = left_ref[...].astype(F32)
-    edge_s[edge : edge + near, :] = pad_ref[0:near, :]
-    edge_s[edge + near : edge + 2 * near, :] = pad_ref[z.cols * z.pad_col - near :, :]
-    edge_s[edge + 2 * near :, :] = right_ref[...].astype(F32)
+    edge_columns(z, left_ref, pad_ref, right_ref, edge_s, slab_s)
+    left_out_ref[...] = edge_s[0 : M * z.pad_col, :]
+    right_out_ref[...] = edge_s[5 * M * z.pad_col :, :]
     size = M * z.col
     refs = (gain_ref, we_ref, wc_ref, coarse_ref, weighted_ref)
     groups = [(0, 0, size), (size, z.cells - size, size)]
@@ -341,57 +347,80 @@
     edge_rows(z, split_s, edge_refs)
 
 
-def terms_kernel(z, pad_ref, left_ref, right_ref, inner_ref, outer_ref, gain_ref, out_ref, full_s, mixed_s):
-    edge = M * z.pad_col
-    full_s[0:edge, :] = left_ref[...].astype(F32)
-    full_s[edge : edge + z.cols * z.pad_col, :] = pad_ref[...]
-    full_s[edge + z.cols * z.pad_col :, :] = right_ref[...].astype(F32)
-    size = M * z.col
-    mixed_s[0:size, :] = outer_ref[0:size, :]
-    mixed_s[size : z.cells - size, :] = inner_ref[...]
-    mixed_s[z.cells - size :, :] = outer_ref[size:, :]
-    out_ref[...] = jnp.zeros_like(out_ref)
+def terms_kernel(
+    z, pad_ref, left_ref, right_ref, inner_ref, outer_ref, gain_ref, aux_s, full_s, mixed_s
+):
+    edge, size = M * z.pad_col, M * z.col
+    aux_s[...] = jnp.zeros_like(aux_s)
     for h in range(z.halves):
         lanes = slice(h * LANE, (h + 1) * LANE)
+        full_s[0:edge, :] = left_ref[:, lanes]
+        full_s[edge : edge + z.cols * z.pad_col, :] = pad_ref[:, lanes]
+        full_s[edge + z.cols * z.pad_col :, :] = right_ref[:, lanes]
+        mixed_s[0:size, :] = outer_ref[0:size, lanes]
+        mixed_s[size : z.cells - size, :] = inner_ref[:, lanes]
+        mixed_s[z.cells - size :, :] = outer_ref[size:, lanes]
         for e in range(KS):
 
             def step(j, sums):
-                column = full_s[rows((j + e) * z.pad_col, z.pad_col), lanes].reshape(z.pad_rows, SUB, LANE)
-                back = mixed_s[rows(j * z.col, z.col), lanes].reshape(z.block_rows, SUB, LANE)
-                return tuple(
-                    sums[a] + jnp.sum(column[a : a + z.block_rows] * back, axis=0) for a in range(KS)
-                )
-
-            sums = lax.fori_loop(0, z.cols, step, tuple(jnp.zeros((SUB, LANE), F32) for _ in range(KS)))
+                column = full_s[rows((j + e) * z.pad_col, z.pad_col), :].reshape(z.pad_rows, SUB, LANE)
+                back = mixed_s[rows(j * z.col, z.col), :].reshape(z.block_rows, SUB, LANE)
+                return tuple(sums[a] + jnp.sum(column[a : a + z.block_rows] * back, axis=0) for a in range(KS))
+
+            zeros = tuple(jnp.zeros((SUB, LANE), F32) for _ in range(KS))
+            sums = lax.fori_loop(0, z.cols, step, zeros, unroll=2)
             for a in range(KS):
                 t = a * KS + e
-                out_ref[t : t + 1, lanes] = jnp.sum(sums[a], axis=0, keepdims=True)
-    out_ref[KS * KS : KS * KS + 1, :] = jnp.sum(gain_ref[...], axis=0, keepdims=True)
-
-
-def back_kernel(
-    z, pad_ref, left_ref, right_ref, kern_ref, weighted_ref, patches_ref, aux_ref,
-    coarse_ref, mine_ref, other_ref, taps_s, full_s, sum_s,
+                aux_s[t : t + 1, lanes] = jnp.sum(sums[a], axis=0, keepdims=True)
+    aux_s[KS * KS : KS * KS + 1, :] = jnp.sum(gain_ref[...], axis=0, keepdims=True)
+
+
+def spread(z, pad, taps_s, source, at, low, weighted_ref, out_ref):
+    for h in range(z.halves):
+        lanes = slice(h * LANE, (h + 1) * LANE)
+        total = taps(z, pad, taps_s, source, h, True)
+        out_ref[low, lanes] = (weighted_ref[at, lanes].astype(F32) + total).astype(BF16)
+
+
+def back_inner_kernel(z, pad_ref, kern_ref, weighted_ref, coarse_ref, taps_s):
+    spread_taps(z, kern_ref, taps_s)
+
+    def step(j, _):
+        spread(
+            z, pad_ref, taps_s, j, rows16((j + M) * z.col, z.col), rows16(j * z.col, z.col), weighted_ref, coarse_ref
+        )
+        return 0
+
+    lax.fori_loop(0, z.cols - 2 * M, step, 0, unroll=2)
+
+
+def edge_columns(z, left_ref, pad_ref, right_ref, edge_s, slab_s):
+    edge, near = M * z.pad_col, 2 * M * z.pad_col
+    unpack_slab(z, left_ref, slab_s, edge_s, 0)
+    edge_s[edge : edge + near, :] = pad_ref[0:near, :]
+    edge_s[edge + near : edge + 2 * near, :] = pad_ref[z.cols * z.pad_col - near :, :]
+    unpack_slab(z, right_ref, slab_s, edge_s, edge + 2 * near)
+
+
+def back_outer_kernel(
+    z, pad_ref, left_ref, right_ref, kern_ref, weighted_ref, patches_ref, inner_ref, aux_ref,
+    coarse_ref, mine_ref, other_ref, taps_s, edge_s, sum_s, slab_s,
 ):
     spread_taps(z, kern_ref, taps_s)
-    edge = M * z.pad_col
-    full_s[0:edge, :] = left_ref[...].astype(F32)
-    full_s[edge : edge + z.cols * z.pad_col, :] = pad_ref[...]
-    full_s[edge + z.cols * z.pad_col :, :] = right_ref[...].astype(F32)
+    edge_columns(z, left_ref, pad_ref, right_ref, edge_s, slab_s)
 
     def step(j, _):
-        at = rows16(j * z.col, z.col)
-        for h in range(z.halves):
-            lanes = slice(h * LANE, (h + 1) * LANE)
-            spread = taps(z, full_s, taps_s, j, h, True)
-            coarse_ref[at, lanes] = (weighted_ref[at, lanes].astype(F32) + spread).astype(BF16)
-        return 0
-
-    lax.fori_loop(0, z.cols, step, 0)
+        for first, source in ((0, 0), (z.cols - M, 3 * M)):
+            at = rows16((first + j) * z.col, z.col)
+            spread(z, edge_s, taps_s, source + j, at, at, weighted_ref, coarse_ref)
+        return 0
+
+    lax.fori_loop(0, M, step, 0)
+    size = M * z.col
+    coarse_ref[size : z.cells - size, :] = inner_ref[...]
     sum_s[...] = dot_tn(coarse_ref[...], patches_ref[...])
-    own = lax.axis_index("dp")
-    cut, depth = 2 * z.narrow, aux_ref.shape[0] // 2
-    half = z.channels // 2
+    own, cut = lax.axis_index("dp"), 2 * z.narrow
+    depth, half = aux_ref.shape[0] // 2, z.channels // 2
     for ref, owner in ((mine_ref, own), (other_ref, 1 - own)):
         ref[0 : z.channels, :] = sum_s[:, lanes_at(owner * cut, cut)].astype(BF16)
         for t in range(2):
@@ -420,7 +449,7 @@
                         back_ref[fine_rows_of(z, g * group + jj, i, p, q), :] = up[first : first + SUB]
         return 0
 
-    lax.fori_loop(0, z.cols // group, step, 0)
+    lax.fori_loop(0, z.cols // group, step, 0, unroll=True)
 
 
 def fine_kernel(z, back_ref, inv_ref, out_ref):
@@ -429,7 +458,7 @@
         out_ref[at, :] = (inv_ref[at, :] * back_ref[rows(t * z.fine_stride, z.fine_block), :]).astype(BF16)
         return 0
 
-    lax.fori_loop(0, SUB, step, 0)
+    lax.fori_loop(0, SUB, step, 0, unroll=2)
 
 
 def second(axis, distance):
@@ -466,7 +495,7 @@
                 ]
         return 0
 
-    lax.fori_loop(0, z.cols, step, 0)
+    lax.fori_loop(0, z.cols, step, 0, unroll=8)
     for h in range(z.halves):
         out_ref[:, h * LANE : (h + 1) * LANE] = split_s[h, :, :].astype(BF16)
 
@@ -480,10 +509,11 @@
         contract_ref[:, t * half : (t + 1) * half] = part.T
 
 
-def final_small_kernel(z, factor, sum_ref, merge_ref, kernel_ref, gain_ref):
-    merge_ref[...] = (sum_ref[0 : z.channels, :].astype(F32) * factor).T
+def final_small_kernel(z, factor, mine_ref, got_ref, merge_ref, kernel_ref, gain_ref):
+    total = (mine_ref[...].astype(F32) + got_ref[...].astype(F32)) * factor
+    merge_ref[...] = total[0 : z.channels].T
     half = z.channels // 2
-    tail = sum_ref[z.channels :, :].astype(F32) * factor
+    tail = total[z.channels :]
     depth = tail.shape[0]
     kernel_ref[0:depth, :] = tail[:, :half]
     kernel_ref[depth:, :] = tail[: KS * KS - depth, half:]
@@ -501,9 +531,9 @@
     return kernel_call(functools.partial(add_kernel, halve), outs, (mine, got), after=after)
 
 
-def join(x, step):
-    got = swap(x, *step)
-    return kernel_call(functools.partial(join_kernel, step), [((2 * x.shape[0], x.shape[1]), BF16)], (x, got))[0]
+def join(x, step, after):
+    outs = [((2 * x.shape[0], x.shape[1]), BF16)]
+    return kernel_call(functools.partial(join_kernel, step), outs, (x, swap(x, *step)), after=after)
 
 
 def sum_steps(count):
@@ -556,9 +586,10 @@
         [split],
         flops=2_000_000_000,
     )
-    slab = ((M * z.pad_col, ch), BF16)
+    slab_rows = -(-(M * z.col + 2 * M * z.samples * M) // (2 * SUB)) * 2 * SUB
+    slab, slab_s = ((slab_rows, ch), BF16), ((slab_rows, ch), F32)
     padded = ((z.cols * z.pad_col, ch), F32)
-    pad_scratch = [((2 * z.samples * M * z.cols, ch), F32)]
+    pad_scratch = [((2 * z.samples * M * z.cols, ch), F32), slab_s]
     pad, left, right, _ = kernel_call(part(pad_kernel, z, lats), [padded, slab, slab], (coarse, before, after), pad_scratch)
     left, right = lon_margins(left, right)
 
@@ -583,7 +614,7 @@
         [taps_s] + section_scratch(inner),
         flops=8_000_000_000,
     )
-    section_out, mixed_out, mine, other, low, gain_sum, *send, _ = kernel_call(
+    section_out, mixed_out, mine, other, low, gain_sum, left, right, *send, _ = kernel_call(
         part(outer_kernel, z),
         [
             ((outer, ch), BF16),
@@ -592,11 +623,13 @@
             ((ch, ff), BF16),
             ((z.cells, ch), BF16),
             ((SUB, ch), F32),
+            ((M * z.pad_col, ch), F32),
+            ((M * z.pad_col, ch), F32),
             *edges,
         ],
         (pad, left, right, conv_kernel, gain, w_expand, w_contract, coarse, weighted)
         + (expand, contract, gain_sum, mixed_in),
-        [taps_s, ((6 * M * z.pad_col, ch), F32), ((2, ch, ff), F32), split] + section_scratch(outer),
+        [taps_s, ((6 * M * z.pad_col, ch), F32), ((2, ch, ff), F32), split, slab_s] + section_scratch(outer),
         flops=8_000_000_000,
     )
     before, after = lat_margins(*send)
@@ -606,70 +639,72 @@
         part(pad_kernel, z, lats), [padded, slab, slab], (low, before, after), pad_scratch, after=(token,)
     )
     left_low, right_low = lon_margins(edge_left, edge_right)
-    full = (((z.cols + 2 * M) * z.pad_col, ch), F32)
+    bf = lambda count, width: ((count, width), BF16)
     aux, token = kernel_call(
         part(terms_kernel, z),
         [((64, ch), F32)],
         (pad, left, right, mixed_in, mixed_out, gain_sum),
-        [full, ((z.cells, ch), F32)],
-        flops=5_000_000_000,
-        after=(token,),
+        [(((z.cols + 2 * M) * z.pad_col, LANE), F32), ((z.cells, LANE), F32)],
+        5_000_000_000,
+        (token,),
     )
     wide, away, token = add(wide, swap(away, *steps[0]), after=(token,), halve=steps[1])
-    small = ((ch + 32, ch), BF16)
-    back_coarse, mine, other, token = kernel_call(
-        part(back_kernel, z),
-        [((z.cells, ch), BF16), small, small],
-        (pad_low, left_low, right_low, conv_kernel, weighted, patches, aux),
-        [taps_s, full, ((ch, 4 * z.narrow), F32)],
-        flops=5_000_000_000,
-        after=(token,),
+    back_inner, token = kernel_call(
+        part(back_inner_kernel, z), [bf(inner, ch)], (pad_low, conv_kernel, weighted), [taps_s], 4_000_000_000, (token,)
     )
     for n in range(1, halvings - 1):
         wide, away, token = add(wide, swap(away, *steps[n]), after=(token,), halve=steps[n + 1])
-    wide, token = add(wide, swap(away, *steps[halvings - 1]), after=(token,))
+    back_coarse, mine, other, token = kernel_call(
+        part(back_outer_kernel, z),
+        [bf(z.cells, ch), bf(ch + 32, 2 * z.narrow), bf(ch + 32, 2 * z.narrow)],
+        (pad_low, left_low, right_low, conv_kernel, weighted, patches, back_inner, aux),
+        [taps_s, ((6 * M * z.pad_col, ch), F32), ((ch, 4 * z.narrow), F32), slab_s],
+        4_000_000_000,
+        (token,),
+    )
+    small, token = add(mine, swap(other, "dp", 1))
     back_fine, token = kernel_call(
         part(unfold_kernel, z),
         [((SUB * z.fine_stride, z.narrow), F32)],
         (back_coarse, w_centered, patches),
-        flops=3_000_000_000,
-        after=(token,),
-    )
-    small_sum, token = add(mine, swap(other, "dp", 1), after=(token,))
+        (),
+        3_000_000_000,
+        (token,),
+    )
+    wide, token = add(wide, swap(away, *steps[halvings - 1]), after=(token,))
     grad_fine, token = kernel_call(
-        part(fine_kernel, z),
-        [((z.fine, z.narrow), BF16)],
-        (back_fine, fine_inv),
-        flops=2_000_000_000,
-        after=(token,),
-    )
+        part(fine_kernel, z), [bf(z.fine, z.narrow)], (back_fine, fine_inv), (), 2_000_000_000, (token,)
+    )
+    small, token = add(small, swap(small, *steps[0]), after=(token,))
     section_all, token = kernel_call(
         part(section_kernel, z),
-        [((z.cells, ch), BF16)],
+        [bf(z.cells, ch)],
         (section_in, section_out),
         [((z.cells, ch), F32), split],
-        flops=2_000_000_000,
-        after=(token,),
-    )
-    small_sum, token = add(small_sum, swap(small_sum, *steps[0]), after=(token,))
+        2_000_000_000,
+        (token,),
+    )
     for step in steps[halvings:]:
         wide, token = add(wide, swap(wide, *step), after=(token,))
-    for step in steps[1:]:
-        small_sum, token = add(small_sum, swap(small_sum, *step))
+    for step in steps[1:-1]:
+        small, token = add(small, swap(small, *step), after=(token,))
+    small_got = swap(small, *steps[-1])
     for step in reversed(steps[1:halvings]):
-        wide = join(wide, step)
+        wide, token = join(wide, step, (token,))
     all_cells = z.samples * lax.axis_size("dp") * z.lat_rows * lats * z.cols * lax.axis_size("lon")
     factor = 1.0 / math.sqrt(all_cells)
-    grad_expand, grad_contract, _ = kernel_call(
+    grad_expand, grad_contract, token = kernel_call(
         part(final_wide_kernel, z, factor, steps[0]),
         [((ch // 2, ff), F32), ((ff // 2, ch), F32)],
         (wide, swap(wide, *steps[0])),
         [((ch, ff), BF16)],
+        after=(token,),
     )
     grad_merge, grad_kernel, grad_gain, _ = kernel_call(
         part(final_small_kernel, z, factor),
         [((2 * z.narrow, ch), F32), ((KS * KS, ch // 2), F32), ((1, ch // 2), F32)],
-        (small_sum,),
+        (small, small_got),
+        after=(token,),
     )
     return (
         section_all.reshape(z.samples, z.lat_rows, z.cols, ch),

time: 87.1 us -> 80.5 us (0.924)
  Pallas kernels: 45.9 us -> 37.3 us
  waiting for transfers between devices: 14.5 us -> 18.9 us
  starting transfers between devices: 22.4 us -> 20.2 us
    pallas_call x22, Pallas kernels: 45.9 us -> 37.3 us  [kernel_call(): pl.pallas_call(run, out_shape=[jax.ShapeDtypeStruct(s, d) for s, d in out...]
    ppermute x12, waiting for transfers between devices: 14.4 us -> 18.8 us  [swap(): return lax.ppermute(x, axis, [(i, i ^ distance) for i in range(size)])]
    ppermute x12, starting transfers between devices: 14.7 us -> 12.5 us  [swap(): return lax.ppermute(x, axis, [(i, i ^ distance) for i in range(size)])]
  transfers between devices with their start and end apart: 16 -> 16, of which waited for: 6 -> 10; matrix products, arithmetic and copies ran while one was open for 0% -> 0% of each run, Pallas kernels for 36% -> 30%
where the time goes in v3:
time: 80.5 us; the launch traced here: 80.3 us
  Pallas kernels  37.3 us (46%)
  starting transfers between devices  20.2 us (25%)
  waiting for transfers between devices  18.9 us (23%)
  local copies, waits for them, and re-layouts  3.22 us (4%)
    pallas_call x22, Pallas kernels, kernel_call(): pl.pallas_call(run, out_shape=[jax.ShapeDtypeStruct(s, d) for s, d in out...  37.3 us
    ppermute x12, waiting for transfers between devices, swap(): return lax.ppermute(x, axis, [(i, i ^ distance) for i in range(size)])  18.8 us
    ppermute x12, starting transfers between devices, swap(): return lax.ppermute(x, axis, [(i, i ^ distance) for i in range(size)])  12.5 us
    ppermute x2, starting transfers between devices, lon_margins(): lax.ppermute(left, 'lon', [(j, i) for i, j in up])  5.9 us
    unnamed x14, local copies, waits for them, and re-layouts  3.22 us
    ppermute x2, starting transfers between devices, lon_margins(): lax.ppermute(right, 'lon', up)  1.79 us
  transfers between devices with their start and end apart: 16, of which 10 were waited for; matrix products, arithmetic and copies ran while one was open for 0% of the time, Pallas kernels for 30%

profile of v3, /device:TPU:0, one launch (start us, length us, event | category | flops | bytes accessed | tf_op | source)
XLA Modules:
  0.0 80.3 jit_solution(16944889115573980285)
XLA Ops:
  0.6 1.2 %copy-done = bf16[2,64,32,128]{3,2,1,0:T(8,128)(2,1)S(1)} copy-done((bf16[2,64,32,128]{3,2,1,0:T(8,128)(2,1)S(1)}, bf16[2,64,32,128]{3,2,1,0:T(8,128)(2,1)}, u32[]{:S(2)}) %copy-start) | copy-done | bytes 1048600
  1.9 0.9 %copy-done.1 = bf16[512,256]{1,0:T(8,128)(2,1)S(1)} copy-done((bf16[512,256]{1,0:T(8,128)(2,1)S(1)}, bf16[512,256]{1,0:T(8,128)(2,1)}, u32[]{:S(2)}) %copy-start.1) | copy-done | bytes 262168
  2.8 2.0 %shard_map.126 = (bf16[1024,512]{1,0:T(8,128)(2,1)S(1)}, bf16[1024,256]{1,0:T(8,128)(2,1)S(1)}, f32[4096,128]{1,0:T(8,128)S(1)}, bf16[96,256]{1,0:T(8,128)(2,1)S(1)}, f32[8,128]{1,0:T(8,128)}) custom-call(bf16[4096,128]{1,0:T(8,128)(2,1)S(1)} %bitcast.6, bf16[512,256]{1,0:T(8,128)(2,1)S(1)} %copy-done.1), custom_call_target="tpu_custom_call" | custom-call | bytes 1310720 | tf_op jit(solution)/shard_map/pallas_call | solution.py:30
  4.8 2.9 %collective-permute-start = (bf16[96,256]{1,0:T(8,128)(2,1)S(1)}, bf16[96,256]{1,0:T(8,128)(2,1)S(1)}, u32[]{:S(2)}, u32[]{:S(2)}) collective-permute-start(bf16[96,256]{1,0:T(8,128)(2,1)S(1)} %get-tuple-element.72), channel_id=1, source_target_pairs={{0,2},{2,0},{1,3},{3,1},{4,6},{6,4},{5,7},{7,5},{8,10},{10,8},{9,1... | collective-permute-start | bytes 147464 | tf_op jit(solution)/shard_map/ppermute | solution.py:525
  7.7 1.0 %copy-done.2 = bf16[2,32,16,256]{3,2,1,0:T(8,128)(2,1)S(1)} copy-done((bf16[2,32,16,256]{3,2,1,0:T(8,128)(2,1)S(1)}, bf16[2,32,16,256]{3,2,1,0:T(8,128)(2,1)}, u32[]{:S(2)}) %copy-start.2) | copy-done | bytes 524312
  8.8 1.4 %shard_map.128 = (bf16[1024,256]{1,0:T(8,128)(2,1)S(1)}, bf16[512,512]{1,0:T(8,128)(2,1)S(1)}, f32[8,128]{1,0:T(8,128)}) custom-call(bf16[1024,256]{1,0:T(8,128)(2,1)S(1)} %bitcast.7, bf16[512,256]{1,0:T(8,128)(2,1)S(1)} %copy-done.1), custom_call_target="tpu_custom_call" | custom-call | flops 2000000000 | bytes 786432 | tf_op jit(solution)/shard_map/pallas_call | solution.py:30
  10.1 1.1 %shard_map.127 = (f32[1792,256]{1,0:T(8,128)S(1)}, bf16[240,256]{1,0:T(8,128)(2,1)S(1)}, bf16[240,256]{1,0:T(8,128)(2,1)S(1)}, f32[8,128]{1,0:T(8,128)}) custom-call(bf16[1024,256]{1,0:T(8,128)(2,1)S(1)} %get-tuple-element.71.refs_0_.refs_5_.refs_7_, bf16[96,256]{1,0:T(8,128)(2,1)S(1)} %collective-permute-done.refs_1_.refs_2_, ...), custom_call_target="tpu_custom_call" | custom-call | bytes 622592 | tf_op jit(solution)/shard_map/pallas_call | solution.py:30
  11.3 1.7 %collective-permute-start.1 = (bf16[240,256]{1,0:T(8,128)(2,1)S(1)}, bf16[240,256]{1,0:T(8,128)(2,1)S(1)}, u32[]{:S(2)}, u32[]{:S(2)}) collective-permute-start(bf16[240,256]{1,0:T(8,128)(2,1)S(1)} %get-tuple-element.76), channel_id=1, source_target_pairs={{0,4},{4,8},{8,12},{12,0},{1,5},{5,9},{9,13},{13,1},{2,6},{6,10},{... | collective-permute-start | bytes 368648 | tf_op jit(solution)/shard_map/ppermute | solution.py:563
  13.0 2.1 %collective-permute-start.2 = (bf16[240,256]{1,0:T(8,128)(2,1)S(1)}, bf16[240,256]{1,0:T(8,128)(2,1)S(1)}, u32[]{:S(2)}, u32[]{:S(2)}) collective-permute-start(bf16[240,256]{1,0:T(8,128)(2,1)S(1)} %get-tuple-element.77), channel_id=1, source_target_pairs={{4,0},{8,4},{12,8},{0,12},{5,1},{9,5},{13,9},{1,13},{6,2},{10,6},{... | collective-permute-start | bytes 368648 | tf_op jit(solution)/shard_map/ppermute | solution.py:563
  15.1 8.5 %shard_map.129 = (bf16[640,256]{1,0:T(8,128)(2,1)S(1)}, f32[640,256]{1,0:T(8,128)S(1)}, f32[256,1024]{1,0:T(8,128)S(1)}, f32[256,1024]{1,0:T(8,128)S(1)}, f32[8,256]{1,0:T(8,128)S(1)}, /*index=5*/f32[8,128]{1,0:T(8,128)}) custom-call(f32[1792,256]{1,0:T(8,128)S(1)} %get-tuple-element.73.refs_0_, f32[49,256]{1,0:T(8,128)S(1)} %copy-done.5, ...), custom_call_target="tpu_custom_call" | custom-call | flops 8000000000 | bytes 3983360 | tf_op jit(solution)/shard_map/pallas_call | solution.py:30
  23.6 0.0 collective-permute-done.1.refs_1_
  23.6 6.6 %shard_map.130 = (bf16[384,256]{1,0:T(8,128)(2,1)S(1)}, f32[384,256]{1,0:T(8,128)S(1)}, bf16[256,1024]{1,0:T(8,128)(2,1)S(1)}, bf16[256,1024]{1,0:T(8,128)(2,1)S...) custom-call(f32[1792,256]{1,0:T(8,128)S(1)} %get-tuple-element.73.re, ...), custom_call_target="tpu_custom_call" | custom-call | flops 8000000000 | bytes 6989824 | tf_op jit(solution)/shard_map/pallas_call | solution.py:30
  30.2 0.0 collective-permute-start.4
  30.2 1.6 %collective-permute-start.3 = (bf16[96,256]{1,0:T(8,128)(2,1)S(1)}, bf16[96,256]{1,0:T(8,128)(2,1)S(1)}, u32[]{:S(2)}, u32[]{:S(2)}) collective-permute-start(bf16[96,256]{1,0:T(8,128)(2,1)S(1)} %get-tuple-element.84), channel_id=1, source_target_pairs={{0,2},{2,0},{1,3},{3,1},{4,6},{6,4},{5,7},{7,5},{8,10},{10,8},{9,1... | collective-permute-start | bytes 147464 | tf_op jit(solution)/shard_map/ppermute | solution.py:525
  31.8 0.3 collective-permute-done.4.refs_1_
  32.1 0.1 shard_map.131
  32.2 1.7 %collective-permute-start.7 = (bf16[128,1024]{1,0:T(8,128)(2,1)S(1)}, bf16[128,1024]{1,0:T(8,128)(2,1)S(1)}, u32[]{:S(2)}, u32[]{:S(2)}) collective-permute-start(bf16[128,1024]{1,0:T(8,128)(2,1)S(1)} %get-tuple-element.93), channel_id=1, source_target_pairs={{0,2},{2,0},{1,3},{3,1},{4,6},{6,4},{5,7},{7,5},{8,10},{10,8},{9,1... | collective-permute-start | bytes 786440 | tf_op jit(solution)/shard_map/ppermute | solution.py:525
  33.9 0.4 collective-permute-done.3.refs_1_.refs_2_
  34.3 0.6 shard_map.132
  34.9 0.1 collective-permute-start.5
  35.0 3.8 %collective-permute-start.6 = (bf16[240,256]{1,0:T(8,128)(2,1)S(1)}, bf16[240,256]{1,0:T(8,128)(2,1)S(1)}, u32[]{:S(2)}, u32[]{:S(2)}) collective-permute-start(bf16[240,256]{1,0:T(8,128)(2,1)S(1)} %get-tuple-element.90), channel_id=1, source_target_pairs={{4,0},{8,4},{12,8},{0,12},{5,1},{9,5},{13,9},{1,13},{6,2},{10,6},{... | collective-permute-start | bytes 368648 | tf_op jit(solution)/shard_map/ppermute | solution.py:563
  38.8 4.5 %shard_map.133 = (f32[64,256]{1,0:T(8,128)S(1)}, f32[8,128]{1,0:T(8,128)S(1)}) custom-call(f32[1792,256]{1,0:T(8,128)S(1)} %get-tuple-element.73.refs_0_, f32[336,256]{1,0:T(8,128)S(1)} %get-tuple-element.94.refs_1_, f32[336,256]{1,0:T(8,128)S(1)} %get-tuple-element.95.refs_2_, f32[640,256]{1,0:T(8,128)S(1)} %get-tuple-element.81.refs_12_.refs_3_, ...), custom_call_target="tpu_custom_call" | custom-call | flops 5000000000 | bytes 3579904 | tf_op jit(solution)/shard_map/pallas_call | solution.py:30
  43.2 0.0 collective-permute-done.7.refs_1_
  43.2 0.1 shard_map.134
  43.3 2.9 %shard_map.135 = (bf16[640,256]{1,0:T(8,128)(2,1)S(1)}, f32[8,128]{1,0:T(8,128)S(1)}) custom-call(f32[1792,256]{1,0:T(8,128)S(1)} %get-tuple-element.88.refs_0_, f32[49,256]{1,0:T(8,128)S(1)} %copy-done.5, bf16[1024,256]{1,0:T(8,128)(2,1)S(1)} %get-tuple-element.74.refs_6_.refs_8_.refs_2_.refs_4_, f32[8,128]{1,0:T(8,128)S(1)} %get-tuple-element.100.refs_3_), custom_call_target="tpu_custom_call" | custom-call | flops 4000000000 | bytes 2409472 | tf_op jit(solution)/shard_map/pallas_call | solution.py:30
  46.3 0.0 collective-permute-done.5.refs_1_
  46.3 0.0 collective-permute-done.6.refs_2_
  46.3 2.7 %shard_map.136 = (bf16[1024,256]{1,0:T(8,128)(2,1)S(1)}, bf16[288,256]{1,0:T(8,128)(2,1)S(1)}, bf16[288,256]{1,0:T(8,128)(2,1)S(1)}, f32[8,128]{1,0:T(8,128)}) custom-call(f32[1792,256]{1,0:T(8,128)S(1)} %get-tuple-element.88.refs_0_, bf16[240,256]{1,0:T(8,128)(2,1)S(1)} %collective-permute-done.5.refs_1_, ...), custom_call_target="tpu_custom_call" | custom-call | flops 4000000000 | bytes 4097024 | tf_op jit(solution)/shard_map/pallas_call | solution.py:30
  49.0 0.0 collective-permute-start.8
  49.0 1.4 %collective-permute-done.8.refs_1_ = bf16[288,256]{1,0:T(8,128)(2,1)S(1)} collective-permute-done((bf16[288,256]{1,0:T(8,128)(2,1)S(1)}, bf16[288,256]{1,0:T(8,128)(2,1)S(1)}, u32[]{:S(2)}, u32[]{:S(2)}) %collective-permute-start.8) | collective-permute-done | bytes 147488 | tf_op jit(solution)/shard_map/ppermute | solution.py:525
  50.4 1.7 %shard_map.138 = (f32[4160,128]{1,0:T(8,128)S(1)}, f32[8,128]{1,0:T(8,128)S(1)}) custom-call(bf16[1024,256]{1,0:T(8,128)(2,1)S(1)} %get-tuple-element.107.refs_0_, bf16[512,512]{1,0:T(8,128)(2,1)S(1)} %get-tuple-element.108.refs_1_, bf16[1024,512]{1,0:T(8,128)(2,1)S(1)} %get-tuple-element.91.refs_5_.refs_2_, f32[8,128]{1,0:T(8,128)S(1)} %get-tuple-element.109.refs_3_), custom_call_target="tpu_custom_call" | custom-call | flops 3000000000 | bytes 2097152 | tf_op jit(solution)/shard_map/pallas_call | solution.py:30
  52.0 2.8 %collective-permute-done.10.refs_1_ = bf16[64,1024]{1,0:T(8,128)(2,1)S(1)} collective-permute-done((bf16[64,1024]{1,0:T(8,128)(2,1)S(1)}, bf16[64,1024]{1,0:T(8,128)(2,1)S(1)}, u32[]{:S(2)}, u32[]{:S(2)}) %collective-permute-start.10) | collective-permute-done | bytes 131104 | tf_op jit(solution)/shard_map/ppermute | solution.py:525
  54.9 0.1 collective-permute-start.12
  55.0 1.7 %collective-permute-start.9 = (bf16[288,256]{1,0:T(8,128)(2,1)S(1)}, bf16[288,256]{1,0:T(8,128)(2,1)S(1)}, u32[]{:S(2)}, u32[]{:S(2)}) collective-permute-start(bf16[288,256]{1,0:T(8,128)(2,1)S(1)} %get-tuple-element.106.refs_0_), channel_id=1, source_target_pairs={{0,2},{2,0},{1,3},{3,1},{4,6},{6,4},{5,7},{7,5},{8,10},{10,8},{9,1... | collective-permute-start | bytes 442376 | tf_op jit(solution)/shard_map/ppermute | solution.py:525
  56.7 1.2 %shard_map.140 = (bf16[4096,128]{1,0:T(8,128)(2,1)}, f32[8,128]{1,0:T(8,128)S(1)}) custom-call(f32[4160,128]{1,0:T(8,128)S(1)} %get-tuple-element.110.refs_0_, f32[4096,128]{1,0:T(8,128)S(1)} %get-tuple-element.111.refs_1_, f32[8,128]{1,0:T(8,128)S(1)} %get-tuple-element.115.refs_2_), custom_call_target="tpu_custom_call" | custom-call | flops 2000000000 | bytes 4227072 | tf_op jit(solution)/shard_map/pallas_call | solution.py:30
  57.9 2.6 %collective-permute-done.9.refs_1_ = bf16[288,256]{1,0:T(8,128)(2,1)S(1)} collective-permute-done((bf16[288,256]{1,0:T(8,128)(2,1)S(1)}, bf16[288,256]{1,0:T(8,128)(2,1)S(1)}, u32[]{:S(2)}, u32[]{:S(2)}) %collective-permute-start.9) | collective-permute-done | bytes 147488 | tf_op jit(solution)/shard_map/ppermute | solution.py:525
  60.6 0.6 collective-permute-start.11
  61.1 1.8 %shard_map.142 = (bf16[1024,256]{1,0:T(8,128)(2,1)}, f32[8,128]{1,0:T(8,128)S(1)}) custom-call(bf16[640,256]{1,0:T(8,128)(2,1)S(1)} %get-tuple-element.75.refs_0_, bf16[384,256]{1,0:T(8,128)(2,1)S(1)} %get-tuple-element.82.refs_1_, f32[8,128]{1,0:T(8,128)S(1)} %get-tuple-element.117.refs_2_), custom_call_target="tpu_custom_call" | custom-call | flops 2000000000 | bytes 524288 | tf_op jit(solution)/shard_map/pallas_call | solution.py:30
  63.0 0.9 %collective-permute-done.12.refs_1_ = bf16[64,1024]{1,0:T(8,128)(2,1)S(1)} collective-permute-done((bf16[64,1024]{1,0:T(8,128)(2,1)S(1)}, bf16[64,1024]{1,0:T(8,128)(2,1)S(1)}, u32[]{:S(2)}, u32[]{:S(2)}) %collective-permute-start.12) | collective-permute-done | bytes 131104 | tf_op jit(solution)/shard_map/ppermute | solution.py:525
  63.9 0.7 collective-permute-start.14
  64.6 2.6 %collective-permute-done.11.refs_1_ = bf16[288,256]{1,0:T(8,128)(2,1)S(1)} collective-permute-done((bf16[288,256]{1,0:T(8,128)(2,1)S(1)}, bf16[288,256]{1,0:T(8,128)(2,1)S(1)}, u32[]{:S(2)}, u32[]{:S(2)}) %collective-permute-start.11) | collective-permute-done | bytes 147488 | tf_op jit(solution)/shard_map/ppermute | solution.py:525
  67.3 2.4 %collective-permute-done.14.refs_1_ = bf16[64,1024]{1,0:T(8,128)(2,1)S(1)} collective-permute-done((bf16[64,1024]{1,0:T(8,128)(2,1)S(1)}, bf16[64,1024]{1,0:T(8,128)(2,1)S(1)}, u32[]{:S(2)}, u32[]{:S(2)}) %collective-permute-start.14) | collective-permute-done | bytes 131104 | tf_op jit(solution)/shard_map/ppermute | solution.py:525
  69.7 1.7 %collective-permute-start.15 = (bf16[128,1024]{1,0:T(8,128)(2,1)S(1)}, bf16[128,1024]{1,0:T(8,128)(2,1)S(1)}, u32[]{:S(2)}, u32[]{:S(2)}) collective-permute-start(bf16[128,1024]{1,0:T(8,128)(2,1)S(1)} %get-tuple-element.127.refs_0_), channel_id=1, source_target_pairs={{0,2},{2,0},{1,3},{3,1},{4,6},{6,4},{5,7},{7,5},{8,10},{10,8},{9,1... | collective-permute-start | bytes 786440 | tf_op jit(solution)/shard_map/ppermute | solution.py:525
  71.5 1.4 %collective-permute-start.13 = (bf16[288,256]{1,0:T(8,128)(2,1)S(1)}, bf16[288,256]{1,0:T(8,128)(2,1)S(1)}, u32[]{:S(2)}, u32[]{:S(2)}) collective-permute-start(bf16[288,256]{1,0:T(8,128)(2,1)S(1)} %get-tuple-element.124.refs_0_), channel_id=1, source_target_pairs={{0,8},{4,12},{8,0},{12,4},{1,9},{5,13},{9,1},{13,5},{2,10},{6,14},... | collective-permute-start | bytes 442376 | tf_op jit(solution)/shard_map/ppermute | solution.py:525
  72.8 4.7 %collective-permute-done.15.refs_1_ = bf16[128,1024]{1,0:T(8,128)(2,1)S(1)} collective-permute-done((bf16[128,1024]{1,0:T(8,128)(2,1)S(1)}, bf16[128,1024]{1,0:T(8,128)(2,1)S(1)}, u32[]{:S(2)}, u32[]{:S(2)}) %collective-permute-start.15) | collective-permute-done | bytes 262176 | tf_op jit(solution)/shard_map/ppermute | solution.py:525
  77.5 1.2 %shard_map.146 = (f32[128,1024]{1,0:T(8,128)}, f32[512,256]{1,0:T(8,128)}, f32[8,128]{1,0:T(8,128)S(1)}) custom-call(bf16[128,1024]{1,0:T(8,128)(2,1)S(1)} %get-tuple-element.127.refs_0_, bf16[128,1024]{1,0:T(8,128)(2,1)S(1)} %collective-permute-done.15.refs_1_, f32[8,128]{1,0:T(8,128)S(1)} %get-tuple-element.128.refs_2_), custom_call_target="tpu_custom_call" | custom-call | bytes 524288 | tf_op jit(solution)/shard_map/pallas_call | solution.py:30
  78.7 0.8 collective-permute-done.13.refs_1_
  79.5 0.8 %shard_map.147 = (f32[256,256]{1,0:T(8,128)}, f32[49,128]{1,0:T(8,128)}, f32[1,128]{1,0:T(1,128)}, f32[8,128]{1,0:T(8,128)}) custom-call(bf16[288,256]{1,0:T(8,128)(2,1)S(1)} %get-tuple-element.124.refs_0_, bf16[288,256]{1,0:T(8,128)(2,1)S(1)} %collective-permute-done.13.refs_1_, f32[8,128]{1,0:T(8,128)S(1)} %get-tuple-element.129.refs_2_), custom_call_target="tpu_custom_call" | custom-call | bytes 294912 | tf_op jit(solution)/shard_map/pallas_call | solution.py:30
  (20 shorter events, 0.2 us)
Async XLA Ops:
  0.6 1.2 %copy-start = (bf16[2,64,32,128]{3,2,1,0:T(8,128)(2,1)S(1)}, bf16[2,64,32,128]{3,2,1,0:T(8,128)(2,1)}, u32[]{:S(2)}) copy-start(bf16[2,64,32,128]{3,2,1,0:T(8,128)(2,1)} %param.7) | copy-start | bytes 3145732
  1.9 0.9 %copy-start.1 = (bf16[512,256]{1,0:T(8,128)(2,1)S(1)}, bf16[512,256]{1,0:T(8,128)(2,1)}, u32[]{:S(2)}) copy-start(bf16[512,256]{1,0:T(8,128)(2,1)} %refs_1_.5) | copy-start | bytes 786436
  4.8 5.4 %collective-permute-start = (bf16[96,256]{1,0:T(8,128)(2,1)S(1)}, bf16[96,256]{1,0:T(8,128)(2,1)S(1)}, u32[]{:S(2)}, u32[]{:S(2)}) collective-permute-start(bf16[96,256]{1,0:T(8,128)(2,1)S(1)} %get-tuple-element.72), channel_id=1, source_target_pairs={{0,2},{2,0},{1,3},{3,1},{4,6},{6,4},{5,7},{7,5},{8,10},{10,8},{9,1... | collective-permute-start | bytes 147464 | tf_op jit(solution)/shard_map/ppermute | solution.py:525
  7.7 1.0 %copy-start.2 = (bf16[2,32,16,256]{3,2,1,0:T(8,128)(2,1)S(1)}, bf16[2,32,16,256]{3,2,1,0:T(8,128)(2,1)}, u32[]{:S(2)}) copy-start(bf16[2,32,16,256]{3,2,1,0:T(8,128)(2,1)} %param.8) | copy-start | bytes 1572868
  8.7 6.3 %copy-start.3 = (bf16[256,1024]{1,0:T(8,128)(2,1)S(1)}, bf16[256,1024]{1,0:T(8,128)(2,1)}, u32[]{:S(2)}) copy-start(bf16[256,1024]{1,0:T(8,128)(2,1)} %refs_5_.1) | copy-start | bytes 1572868
  8.7 6.3 %copy-start.4 = (bf16[1024,256]{1,0:T(8,128)(2,1)S(1)}, bf16[1024,256]{1,0:T(8,128)(2,1)}, u32[]{:S(2)}) copy-start(bf16[1024,256]{1,0:T(8,128)(2,1)} %refs_6_.1) | copy-start | bytes 1572868
  8.7 6.3 %copy-start.5 = (f32[49,256]{1,0:T(8,128)S(1)}, f32[49,256]{1,0:T(8,128)}, u32[]{:S(2)}) copy-start(f32[49,256]{1,0:T(8,128)} %refs_3_.5) | copy-start | bytes 150532
  8.7 6.3 %copy-start.6 = (f32[256]{0:T(256)S(1)}, f32[256]{0:T(256)}, u32[]{:S(2)}) copy-start(f32[256]{0:T(256)} %param.10) | copy-start | bytes 3076
  11.3 12.3 %collective-permute-start.1 = (bf16[240,256]{1,0:T(8,128)(2,1)S(1)}, bf16[240,256]{1,0:T(8,128)(2,1)S(1)}, u32[]{:S(2)}, u32[]{:S(2)}) collective-permute-start(bf16[240,256]{1,0:T(8,128)(2,1)S(1)} %get-tuple-element.76), channel_id=1, source_target_pairs={{0,4},{4,8},{8,12},{12,0},{1,5},{5,9},{9,13},{13,1},{2,6},{6,10},{... | collective-permute-start | bytes 368648 | tf_op jit(solution)/shard_map/ppermute | solution.py:563
  13.0 10.6 %collective-permute-start.2 = (bf16[240,256]{1,0:T(8,128)(2,1)S(1)}, bf16[240,256]{1,0:T(8,128)(2,1)S(1)}, u32[]{:S(2)}, u32[]{:S(2)}) collective-permute-start(bf16[240,256]{1,0:T(8,128)(2,1)S(1)} %get-tuple-element.77), channel_id=1, source_target_pairs={{4,0},{8,4},{12,8},{0,12},{5,1},{9,5},{13,9},{1,13},{6,2},{10,6},{... | collective-permute-start | bytes 368648 | tf_op jit(solution)/shard_map/ppermute | solution.py:563
  30.2 1.9 %collective-permute-start.4 = (bf16[256,1024]{1,0:T(8,128)(2,1)S(1)}, bf16[256,1024]{1,0:T(8,128)(2,1)S(1)}, u32[]{:S(2)}, u32[]{:S(2)}) collective-permute-start(bf16[256,1024]{1,0:T(8,128)(2,1)S(1)} %get-tuple-element.86), channel_id=1, source_target_pairs={{0,1},{1,0},{2,3},{3,2},{4,5},{5,4},{6,7},{7,6},{8,9},{9,8},{10,11... | collective-permute-start | bytes 1572872 | tf_op jit(solution)/shard_map/ppermute | solution.py:525
  30.2 4.2 %collective-permute-start.3 = (bf16[96,256]{1,0:T(8,128)(2,1)S(1)}, bf16[96,256]{1,0:T(8,128)(2,1)S(1)}, u32[]{:S(2)}, u32[]{:S(2)}) collective-permute-start(bf16[96,256]{1,0:T(8,128)(2,1)S(1)} %get-tuple-element.84), channel_id=1, source_target_pairs={{0,2},{2,0},{1,3},{3,1},{4,6},{6,4},{5,7},{7,5},{8,10},{10,8},{9,1... | collective-permute-start | bytes 147464 | tf_op jit(solution)/shard_map/ppermute | solution.py:525
  32.2 11.0 %collective-permute-start.7 = (bf16[128,1024]{1,0:T(8,128)(2,1)S(1)}, bf16[128,1024]{1,0:T(8,128)(2,1)S(1)}, u32[]{:S(2)}, u32[]{:S(2)}) collective-permute-start(bf16[128,1024]{1,0:T(8,128)(2,1)S(1)} %get-tuple-element.93), channel_id=1, source_target_pairs={{0,2},{2,0},{1,3},{3,1},{4,6},{6,4},{5,7},{7,5},{8,10},{10,8},{9,1... | collective-permute-start | bytes 786440 | tf_op jit(solution)/shard_map/ppermute | solution.py:525
  34.9 11.4 %collective-permute-start.5 = (bf16[240,256]{1,0:T(8,128)(2,1)S(1)}, bf16[240,256]{1,0:T(8,128)(2,1)S(1)}, u32[]{:S(2)}, u32[]{:S(2)}) collective-permute-start(bf16[240,256]{1,0:T(8,128)(2,1)S(1)} %get-tuple-element.89), channel_id=1, source_target_pairs={{0,4},{4,8},{8,12},{12,0},{1,5},{5,9},{9,13},{13,1},{2,6},{6,10},{... | collective-permute-start | bytes 368648 | tf_op jit(solution)/shard_map/ppermute | solution.py:563
  35.0 11.3 %collective-permute-start.6 = (bf16[240,256]{1,0:T(8,128)(2,1)S(1)}, bf16[240,256]{1,0:T(8,128)(2,1)S(1)}, u32[]{:S(2)}, u32[]{:S(2)}) collective-permute-start(bf16[240,256]{1,0:T(8,128)(2,1)S(1)} %get-tuple-element.90), channel_id=1, source_target_pairs={{4,0},{8,4},{12,8},{0,12},{5,1},{9,5},{13,9},{1,13},{6,2},{10,6},{... | collective-permute-start | bytes 368648 | tf_op jit(solution)/shard_map/ppermute | solution.py:563
  49.0 1.4 %collective-permute-start.8 = (bf16[288,256]{1,0:T(8,128)(2,1)S(1)}, bf16[288,256]{1,0:T(8,128)(2,1)S(1)}, u32[]{:S(2)}, u32[]{:S(2)}) collective-permute-start(bf16[288,256]{1,0:T(8,128)(2,1)S(1)} %get-tuple-element.105), channel_id=1, source_target_pairs={{0,1},{1,0},{2,3},{3,2},{4,5},{5,4},{6,7},{7,6},{8,9},{9,8},{10,11... | collective-permute-start | bytes 442376 | tf_op jit(solution)/shard_map/ppermute | solution.py:525
  49.0 5.9 %collective-permute-start.10 = (bf16[64,1024]{1,0:T(8,128)(2,1)S(1)}, bf16[64,1024]{1,0:T(8,128)(2,1)S(1)}, u32[]{:S(2)}, u32[]{:S(2)}) collective-permute-start(bf16[64,1024]{1,0:T(8,128)(2,1)S(1)} %get-tuple-element.113), channel_id=1, source_target_pairs={{0,4},{4,0},{8,12},{12,8},{1,5},{5,1},{9,13},{13,9},{2,6},{6,2},{1... | collective-permute-start | bytes 393224 | tf_op jit(solution)/shard_map/ppermute | solution.py:525
  54.9 8.9 %collective-permute-start.12 = (bf16[64,1024]{1,0:T(8,128)(2,1)S(1)}, bf16[64,1024]{1,0:T(8,128)(2,1)S(1)}, u32[]{:S(2)}, u32[]{:S(2)}) collective-permute-start(bf16[64,1024]{1,0:T(8,128)(2,1)S(1)} %get-tuple-element.121.refs_0_), channel_id=1, source_target_pairs={{0,8},{4,12},{8,0},{12,4},{1,9},{5,13},{9,1},{13,5},{2,10},{6,14},... | collective-permute-start | bytes 393224 | tf_op jit(solution)/shard_map/ppermute | solution.py:525
  55.0 5.5 %collective-permute-start.9 = (bf16[288,256]{1,0:T(8,128)(2,1)S(1)}, bf16[288,256]{1,0:T(8,128)(2,1)S(1)}, u32[]{:S(2)}, u32[]{:S(2)}) collective-permute-start(bf16[288,256]{1,0:T(8,128)(2,1)S(1)} %get-tuple-element.106.refs_0_), channel_id=1, source_target_pairs={{0,2},{2,0},{1,3},{3,1},{4,6},{6,4},{5,7},{7,5},{8,10},{10,8},{9,1... | collective-permute-start | bytes 442376 | tf_op jit(solution)/shard_map/ppermute | solution.py:525
  60.6 6.7 %collective-permute-start.11 = (bf16[288,256]{1,0:T(8,128)(2,1)S(1)}, bf16[288,256]{1,0:T(8,128)(2,1)S(1)}, u32[]{:S(2)}, u32[]{:S(2)}) collective-permute-start(bf16[288,256]{1,0:T(8,128)(2,1)S(1)} %get-tuple-element.120.refs_0_), channel_id=1, source_target_pairs={{0,4},{4,0},{8,12},{12,8},{1,5},{5,1},{9,13},{13,9},{2,6},{6,2},{1... | collective-permute-start | bytes 442376 | tf_op jit(solution)/shard_map/ppermute | solution.py:525
  63.9 5.8 %collective-permute-start.14 = (bf16[64,1024]{1,0:T(8,128)(2,1)S(1)}, bf16[64,1024]{1,0:T(8,128)(2,1)S(1)}, u32[]{:S(2)}, u32[]{:S(2)}) collective-permute-start(bf16[64,1024]{1,0:T(8,128)(2,1)S(1)} %get-tuple-element.125.refs_0_), channel_id=1, source_target_pairs={{0,4},{4,0},{8,12},{12,8},{1,5},{5,1},{9,13},{13,9},{2,6},{6,2},{1... | collective-permute-start | bytes 393224 | tf_op jit(solution)/shard_map/ppermute | solution.py:525
  69.7 7.8 %collective-permute-start.15 = (bf16[128,1024]{1,0:T(8,128)(2,1)S(1)}, bf16[128,1024]{1,0:T(8,128)(2,1)S(1)}, u32[]{:S(2)}, u32[]{:S(2)}) collective-permute-start(bf16[128,1024]{1,0:T(8,128)(2,1)S(1)} %get-tuple-element.127.refs_0_), channel_id=1, source_target_pairs={{0,2},{2,0},{1,3},{3,1},{4,6},{6,4},{5,7},{7,5},{8,10},{10,8},{9,1... | collective-permute-start | bytes 786440 | tf_op jit(solution)/shard_map/ppermute | solution.py:525
  71.5 8.0 %collective-permute-start.13 = (bf16[288,256]{1,0:T(8,128)(2,1)S(1)}, bf16[288,256]{1,0:T(8,128)(2,1)S(1)}, u32[]{:S(2)}, u32[]{:S(2)}) collective-permute-start(bf16[288,256]{1,0:T(8,128)(2,1)S(1)} %get-tuple-element.124.refs_0_), channel_id=1, source_target_pairs={{0,8},{4,12},{8,0},{12,4},{1,9},{5,13},{9,1},{13,5},{2,10},{6,14},... | collective-permute-start | bytes 442376 | tf_op jit(solution)/shard_map/ppermute | solution.py:525

commit v4 on v3

--- a/solution.py
+++ b/solution.py
@@ -347,32 +347,29 @@
     edge_rows(z, split_s, edge_refs)
 
 
-def terms_kernel(
-    z, pad_ref, left_ref, right_ref, inner_ref, outer_ref, gain_ref, aux_s, full_s, mixed_s
-):
+def terms_kernel(z, h, pad_ref, left_ref, right_ref, inner_ref, outer_ref, gain_ref, out_ref, full_s, mixed_s):
     edge, size = M * z.pad_col, M * z.col
-    aux_s[...] = jnp.zeros_like(aux_s)
-    for h in range(z.halves):
-        lanes = slice(h * LANE, (h + 1) * LANE)
-        full_s[0:edge, :] = left_ref[:, lanes]
-        full_s[edge : edge + z.cols * z.pad_col, :] = pad_ref[:, lanes]
-        full_s[edge + z.cols * z.pad_col :, :] = right_ref[:, lanes]
-        mixed_s[0:size, :] = outer_ref[0:size, lanes]
-        mixed_s[size : z.cells - size, :] = inner_ref[:, lanes]
-        mixed_s[z.cells - size :, :] = outer_ref[size:, lanes]
-        for e in range(KS):
-
-            def step(j, sums):
-                column = full_s[rows((j + e) * z.pad_col, z.pad_col), :].reshape(z.pad_rows, SUB, LANE)
-                back = mixed_s[rows(j * z.col, z.col), :].reshape(z.block_rows, SUB, LANE)
-                return tuple(sums[a] + jnp.sum(column[a : a + z.block_rows] * back, axis=0) for a in range(KS))
-
-            zeros = tuple(jnp.zeros((SUB, LANE), F32) for _ in range(KS))
-            sums = lax.fori_loop(0, z.cols, step, zeros, unroll=2)
-            for a in range(KS):
-                t = a * KS + e
-                aux_s[t : t + 1, lanes] = jnp.sum(sums[a], axis=0, keepdims=True)
-    aux_s[KS * KS : KS * KS + 1, :] = jnp.sum(gain_ref[...], axis=0, keepdims=True)
+    lanes = slice(h * LANE, (h + 1) * LANE)
+    full_s[0:edge, :] = left_ref[:, lanes]
+    full_s[edge : edge + z.cols * z.pad_col, :] = pad_ref[:, lanes]
+    full_s[edge + z.cols * z.pad_col :, :] = right_ref[:, lanes]
+    mixed_s[0:size, :] = outer_ref[0:size, lanes]
+    mixed_s[size : z.cells - size, :] = inner_ref[:, lanes]
+    mixed_s[z.cells - size :, :] = outer_ref[size:, lanes]
+    out_ref[...] = jnp.zeros_like(out_ref)
+    for e in range(KS):
+
+        def step(j, sums):
+            column = full_s[rows((j + e) * z.pad_col, z.pad_col), :].reshape(z.pad_rows, SUB, LANE)
+            back = mixed_s[rows(j * z.col, z.col), :].reshape(z.block_rows, SUB, LANE)
+            return tuple(sums[a] + jnp.sum(column[a : a + z.block_rows] * back, axis=0) for a in range(KS))
+
+        zeros = tuple(jnp.zeros((SUB, LANE), F32) for _ in range(KS))
+        sums = lax.fori_loop(0, z.cols, step, zeros, unroll=2)
+        for a in range(KS):
+            t = a * KS + e
+            out_ref[t : t + 1, :] = jnp.sum(sums[a], axis=0, keepdims=True)
+    out_ref[KS * KS : KS * KS + 1, :] = jnp.sum(gain_ref[:, lanes], axis=0, keepdims=True)
 
 
 def spread(z, pad, taps_s, source, at, low, weighted_ref, out_ref):
@@ -403,7 +400,7 @@
 
 
 def back_outer_kernel(
-    z, pad_ref, left_ref, right_ref, kern_ref, weighted_ref, patches_ref, inner_ref, aux_ref,
+    z, pad_ref, left_ref, right_ref, kern_ref, weighted_ref, patches_ref, inner_ref, low_aux_ref, high_aux_ref,
     coarse_ref, mine_ref, other_ref, taps_s, edge_s, sum_s, slab_s,
 ):
     spread_taps(z, kern_ref, taps_s)
@@ -420,13 +417,13 @@
     coarse_ref[size : z.cells - size, :] = inner_ref[...]
     sum_s[...] = dot_tn(coarse_ref[...], patches_ref[...])
     own, cut = lax.axis_index("dp"), 2 * z.narrow
-    depth, half = aux_ref.shape[0] // 2, z.channels // 2
+    depth, half = low_aux_ref.shape[0] // 2, z.channels // 2
     for ref, owner in ((mine_ref, own), (other_ref, 1 - own)):
         ref[0 : z.channels, :] = sum_s[:, lanes_at(owner * cut, cut)].astype(BF16)
         for t in range(2):
-            ref[z.channels :, t * half : (t + 1) * half] = aux_ref[
-                t * depth : (t + 1) * depth, lanes_at(owner * half, half)
-            ].astype(BF16)
+            at = slice(t * depth, (t + 1) * depth)
+            aux = jnp.where(owner == 0, low_aux_ref[at, :], high_aux_ref[at, :])
+            ref[z.channels :, t * half : (t + 1) * half] = aux.astype(BF16)
 
 
 def unfold_kernel(z, coarse_ref, centered_ref, patches_ref, back_ref):
@@ -640,29 +637,34 @@
     )
     left_low, right_low = lon_margins(edge_left, edge_right)
     bf = lambda count, width: ((count, width), BF16)
-    aux, token = kernel_call(
-        part(terms_kernel, z),
-        [((64, ch), F32)],
-        (pad, left, right, mixed_in, mixed_out, gain_sum),
-        [(((z.cols + 2 * M) * z.pad_col, LANE), F32), ((z.cells, LANE), F32)],
-        5_000_000_000,
-        (token,),
-    )
+
+    def terms(h, token):
+        return kernel_call(
+            part(terms_kernel, z, h),
+            [((64, LANE), F32)],
+            (pad, left, right, mixed_in, mixed_out, gain_sum),
+            [(((z.cols + 2 * M) * z.pad_col, LANE), F32), ((z.cells, LANE), F32)],
+            3_000_000_000,
+            (token,),
+        )
+
+    low_aux, token = terms(0, token)
     wide, away, token = add(wide, swap(away, *steps[0]), after=(token,), halve=steps[1])
+    high_aux, token = terms(1, token)
     back_inner, token = kernel_call(
         part(back_inner_kernel, z), [bf(inner, ch)], (pad_low, conv_kernel, weighted), [taps_s], 4_000_000_000, (token,)
     )
     for n in range(1, halvings - 1):
         wide, away, token = add(wide, swap(away, *steps[n]), after=(token,), halve=steps[n + 1])
+    wide, token = add(wide, swap(away, *steps[halvings - 1]), after=(token,))
     back_coarse, mine, other, token = kernel_call(
         part(back_outer_kernel, z),
         [bf(z.cells, ch), bf(ch + 32, 2 * z.narrow), bf(ch + 32, 2 * z.narrow)],
-        (pad_low, left_low, right_low, conv_kernel, weighted, patches, back_inner, aux),
+        (pad_low, left_low, right_low, conv_kernel, weighted, patches, back_inner, low_aux, high_aux),
         [taps_s, ((6 * M * z.pad_col, ch), F32), ((ch, 4 * z.narrow), F32), slab_s],
         4_000_000_000,
         (token,),
     )
-    small, token = add(mine, swap(other, "dp", 1))
     back_fine, token = kernel_call(
         part(unfold_kernel, z),
         [((SUB * z.fine_stride, z.narrow), F32)],
@@ -671,10 +673,12 @@
         3_000_000_000,
         (token,),
     )
-    wide, token = add(wide, swap(away, *steps[halvings - 1]), after=(token,))
+    small, token = add(mine, swap(other, "dp", 1), after=(token,))
     grad_fine, token = kernel_call(
         part(fine_kernel, z), [bf(z.fine, z.narrow)], (back_fine, fine_inv), (), 2_000_000_000, (token,)
     )
+    for step in steps[halvings:]:
+        wide, token = add(wide, swap(wide, *step), after=(token,))
     small, token = add(small, swap(small, *steps[0]), after=(token,))
     section_all, token = kernel_call(
         part(section_kernel, z),
@@ -684,13 +688,11 @@
         2_000_000_000,
         (token,),
     )
-    for step in steps[halvings:]:
-        wide, token = add(wide, swap(wide, *step), after=(token,))
+    for step in reversed(steps[1:halvings]):
+        wide, token = join(wide, step, (token,))
     for step in steps[1:-1]:
         small, token = add(small, swap(small, *step), after=(token,))
     small_got = swap(small, *steps[-1])
-    for step in reversed(steps[1:halvings]):
-        wide, token = join(wide, step, (token,))
     all_cells = z.samples * lax.axis_size("dp") * z.lat_rows * lats * z.cols * lax.axis_size("lon")
     factor = 1.0 / math.sqrt(all_cells)
     grad_expand, grad_contract, token = kernel_call(

time: 80.5 us -> 75 us (0.932)
  waiting for transfers between devices: 18.9 us -> 10.1 us
  starting transfers between devices: 20.2 us -> 23.6 us
    ppermute x12, waiting for transfers between devices: 18.8 us -> 10.1 us  [swap(): return lax.ppermute(x, axis, [(i, i ^ distance) for i in range(size)])]
    ppermute x12, starting transfers between devices: 12.5 us -> 15.9 us  [swap(): return lax.ppermute(x, axis, [(i, i ^ distance) for i in range(size)])]
    pallas_call x22 -> x23, Pallas kernels: 37.3 us -> 37 us  [kernel_call(): pl.pallas_call(run, out_shape=[jax.ShapeDtypeStruct(s, d) for s, d in out...]
  transfers between devices with their start and end apart: 16 -> 16, of which waited for: 10 -> 7; matrix products, arithmetic and copies ran while one was open for 0% -> 0% of each run, Pallas kernels for 30% -> 36%
where the time goes in v4:
time: 75 us; the launch traced here: 74.7 us
  Pallas kernels  37 us (49%)
  starting transfers between devices  23.6 us (31%)
  waiting for transfers between devices  10.1 us (13%)
  local copies, waits for them, and re-layouts  3.22 us (4%)
  between operations  0.8 us (1%)
    pallas_call x23, Pallas kernels, kernel_call(): pl.pallas_call(run, out_shape=[jax.ShapeDtypeStruct(s, d) for s, d in out...  37 us
    ppermute x12, starting transfers between devices, swap(): return lax.ppermute(x, axis, [(i, i ^ distance) for i in range(size)])  15.9 us
    ppermute x12, waiting for transfers between devices, swap(): return lax.ppermute(x, axis, [(i, i ^ distance) for i in range(size)])  10.1 us
    ppermute x2, starting transfers between devices, lon_margins(): lax.ppermute(left, 'lon', [(j, i) for i, j in up])  5.9 us
    unnamed x14, local copies, waits for them, and re-layouts  3.22 us
    ppermute x2, starting transfers between devices, lon_margins(): lax.ppermute(right, 'lon', up)  1.79 us
  transfers between devices with their start and end apart: 16, of which 7 were waited for; matrix products, arithmetic and copies ran while one was open for 0% of the time, Pallas kernels for 36%

profile of v4, /device:TPU:0, one launch (start us, length us, event | category | flops | bytes accessed | tf_op | source)
XLA Modules:
  0.0 74.7 jit_solution(11977038436192376763)
XLA Ops:
  0.6 1.2 %copy-done = bf16[2,64,32,128]{3,2,1,0:T(8,128)(2,1)S(1)} copy-done((bf16[2,64,32,128]{3,2,1,0:T(8,128)(2,1)S(1)}, bf16[2,64,32,128]{3,2,1,0:T(8,128)(2,1)}, u32[]{:S(2)}) %copy-start) | copy-done | bytes 1048600
  1.9 0.9 %copy-done.1 = bf16[512,256]{1,0:T(8,128)(2,1)S(1)} copy-done((bf16[512,256]{1,0:T(8,128)(2,1)S(1)}, bf16[512,256]{1,0:T(8,128)(2,1)}, u32[]{:S(2)}) %copy-start.1) | copy-done | bytes 262168
  2.8 2.0 %shard_map.126 = (bf16[1024,512]{1,0:T(8,128)(2,1)S(1)}, bf16[1024,256]{1,0:T(8,128)(2,1)S(1)}, f32[4096,128]{1,0:T(8,128)S(1)}, bf16[96,256]{1,0:T(8,128)(2,1)S(1)}, f32[8,128]{1,0:T(8,128)}) custom-call(bf16[4096,128]{1,0:T(8,128)(2,1)S(1)} %bitcast.6, bf16[512,256]{1,0:T(8,128)(2,1)S(1)} %copy-done.1), custom_call_target="tpu_custom_call" | custom-call | bytes 1310720 | tf_op jit(solution)/shard_map/pallas_call | solution.py:30
  4.8 2.9 %collective-permute-start = (bf16[96,256]{1,0:T(8,128)(2,1)S(1)}, bf16[96,256]{1,0:T(8,128)(2,1)S(1)}, u32[]{:S(2)}, u32[]{:S(2)}) collective-permute-start(bf16[96,256]{1,0:T(8,128)(2,1)S(1)} %get-tuple-element.75), channel_id=1, source_target_pairs={{0,2},{2,0},{1,3},{3,1},{4,6},{6,4},{5,7},{7,5},{8,10},{10,8},{9,1... | collective-permute-start | bytes 147464 | tf_op jit(solution)/shard_map/ppermute | solution.py:522
  7.7 1.0 %copy-done.2 = bf16[2,32,16,256]{3,2,1,0:T(8,128)(2,1)S(1)} copy-done((bf16[2,32,16,256]{3,2,1,0:T(8,128)(2,1)S(1)}, bf16[2,32,16,256]{3,2,1,0:T(8,128)(2,1)}, u32[]{:S(2)}) %copy-start.2) | copy-done | bytes 524312
  8.8 1.4 %shard_map.128 = (bf16[1024,256]{1,0:T(8,128)(2,1)S(1)}, bf16[512,512]{1,0:T(8,128)(2,1)S(1)}, f32[8,128]{1,0:T(8,128)}) custom-call(bf16[1024,256]{1,0:T(8,128)(2,1)S(1)} %bitcast.7, bf16[512,256]{1,0:T(8,128)(2,1)S(1)} %copy-done.1), custom_call_target="tpu_custom_call" | custom-call | flops 2000000000 | bytes 786432 | tf_op jit(solution)/shard_map/pallas_call | solution.py:30
  10.1 0.0 collective-permute-done.refs_1_.refs_2_
  10.1 1.1 %shard_map.127 = (f32[1792,256]{1,0:T(8,128)S(1)}, bf16[240,256]{1,0:T(8,128)(2,1)S(1)}, bf16[240,256]{1,0:T(8,128)(2,1)S(1)}, f32[8,128]{1,0:T(8,128)}) custom-call(bf16[1024,256]{1,0:T(8,128)(2,1)S(1)} %get-tuple-element.74.refs_0_.refs_5_.refs_7_, bf16[96,256]{1,0:T(8,128)(2,1)S(1)} %collective-permute-done.refs_1_.refs_2_, ...), custom_call_target="tpu_custom_call" | custom-call | bytes 622592 | tf_op jit(solution)/shard_map/pallas_call | solution.py:30
  11.3 1.7 %collective-permute-start.1 = (bf16[240,256]{1,0:T(8,128)(2,1)S(1)}, bf16[240,256]{1,0:T(8,128)(2,1)S(1)}, u32[]{:S(2)}, u32[]{:S(2)}) collective-permute-start(bf16[240,256]{1,0:T(8,128)(2,1)S(1)} %get-tuple-element.79), channel_id=1, source_target_pairs={{0,4},{4,8},{8,12},{12,0},{1,5},{5,9},{9,13},{13,1},{2,6},{6,10},{... | collective-permute-start | bytes 368648 | tf_op jit(solution)/shard_map/ppermute | solution.py:560
  13.0 2.1 %collective-permute-start.2 = (bf16[240,256]{1,0:T(8,128)(2,1)S(1)}, bf16[240,256]{1,0:T(8,128)(2,1)S(1)}, u32[]{:S(2)}, u32[]{:S(2)}) collective-permute-start(bf16[240,256]{1,0:T(8,128)(2,1)S(1)} %get-tuple-element.80), channel_id=1, source_target_pairs={{4,0},{8,4},{12,8},{0,12},{5,1},{9,5},{13,9},{1,13},{6,2},{10,6},{... | collective-permute-start | bytes 368648 | tf_op jit(solution)/shard_map/ppermute | solution.py:560
  15.1 8.5 %shard_map.129 = (bf16[640,256]{1,0:T(8,128)(2,1)S(1)}, f32[640,256]{1,0:T(8,128)S(1)}, f32[256,1024]{1,0:T(8,128)S(1)}, f32[256,1024]{1,0:T(8,128)S(1)}, f32[8,256]{1,0:T(8,128)S(1)}, /*index=5*/f32[8,128]{1,0:T(8,128)}) custom-call(f32[1792,256]{1,0:T(8,128)S(1)} %get-tuple-element.76.refs_0_, f32[49,256]{1,0:T(8,128)S(1)} %copy-done.5, ...), custom_call_target="tpu_custom_call" | custom-call | flops 8000000000 | bytes 3983360 | tf_op jit(solution)/shard_map/pallas_call | solution.py:30
  23.6 0.0 collective-permute-done.1.refs_1_
  23.6 0.0 collective-permute-done.2.refs_2_
  23.6 6.6 %shard_map.130 = (bf16[384,256]{1,0:T(8,128)(2,1)S(1)}, f32[384,256]{1,0:T(8,128)S(1)}, bf16[256,1024]{1,0:T(8,128)(2,1)S(1)}, bf16[256,1024]{1,0:T(8,128)(2,1)S...) custom-call(f32[1792,256]{1,0:T(8,128)S(1)} %get-tuple-element.76.re, ...), custom_call_target="tpu_custom_call" | custom-call | flops 8000000000 | bytes 6989824 | tf_op jit(solution)/shard_map/pallas_call | solution.py:30
  30.2 0.0 collective-permute-start.4
  30.2 1.6 %collective-permute-start.3 = (bf16[96,256]{1,0:T(8,128)(2,1)S(1)}, bf16[96,256]{1,0:T(8,128)(2,1)S(1)}, u32[]{:S(2)}, u32[]{:S(2)}) collective-permute-start(bf16[96,256]{1,0:T(8,128)(2,1)S(1)} %get-tuple-element.87), channel_id=1, source_target_pairs={{0,2},{2,0},{1,3},{3,1},{4,6},{6,4},{5,7},{7,5},{8,10},{10,8},{9,1... | collective-permute-start | bytes 147464 | tf_op jit(solution)/shard_map/ppermute | solution.py:522
  31.8 0.3 collective-permute-done.4.refs_1_
  32.1 0.1 shard_map.131
  32.2 1.7 %collective-permute-start.7 = (bf16[128,1024]{1,0:T(8,128)(2,1)S(1)}, bf16[128,1024]{1,0:T(8,128)(2,1)S(1)}, u32[]{:S(2)}, u32[]{:S(2)}) collective-permute-start(bf16[128,1024]{1,0:T(8,128)(2,1)S(1)} %get-tuple-element.100), channel_id=1, source_target_pairs={{0,2},{2,0},{1,3},{3,1},{4,6},{6,4},{5,7},{7,5},{8,10},{10,8},{9,1... | collective-permute-start | bytes 786440 | tf_op jit(solution)/shard_map/ppermute | solution.py:522
  33.9 0.4 collective-permute-done.3.refs_1_.refs_2_
  34.3 0.6 shard_map.132
  34.9 0.1 collective-permute-start.5
  35.0 3.8 %collective-permute-start.6 = (bf16[240,256]{1,0:T(8,128)(2,1)S(1)}, bf16[240,256]{1,0:T(8,128)(2,1)S(1)}, u32[]{:S(2)}, u32[]{:S(2)}) collective-permute-start(bf16[240,256]{1,0:T(8,128)(2,1)S(1)} %get-tuple-element.93), channel_id=1, source_target_pairs={{4,0},{8,4},{12,8},{0,12},{5,1},{9,5},{13,9},{1,13},{6,2},{10,6},{... | collective-permute-start | bytes 368648 | tf_op jit(solution)/shard_map/ppermute | solution.py:560
  38.8 2.2 %shard_map.133 = (f32[64,128]{1,0:T(8,128)S(1)}, f32[8,128]{1,0:T(8,128)S(1)}) custom-call(f32[1792,256]{1,0:T(8,128)S(1)} %get-tuple-element.76.refs_0_, f32[336,256]{1,0:T(8,128)S(1)} %get-tuple-element.95.refs_1_, f32[336,256]{1,0:T(8,128)S(1)} %get-tuple-element.96.refs_2_, f32[640,256]{1,0:T(8,128)S(1)} %get-tuple-element.84.refs_12_.refs_3_, ...), custom_call_target="tpu_custom_call" | custom-call | flops 3000000000 | bytes 3579904 | tf_op jit(solution)/shard_map/pallas_call | solution.py:30
  41.0 0.0 collective-permute-done.7.refs_1_
  41.0 0.1 shard_map.134
  41.1 2.2 %shard_map.135 = (f32[64,128]{1,0:T(8,128)S(1)}, f32[8,128]{1,0:T(8,128)S(1)}) custom-call(f32[1792,256]{1,0:T(8,128)S(1)} %get-tuple-element.76.refs_0_, f32[336,256]{1,0:T(8,128)S(1)} %get-tuple-element.95.refs_1_, f32[336,256]{1,0:T(8,128)S(1)} %get-tuple-element.96.refs_2_, f32[640,256]{1,0:T(8,128)S(1)} %get-tuple-element.84.refs_12_.refs_3_, ...), custom_call_target="tpu_custom_call" | custom-call | flops 3000000000 | bytes 3579904 | tf_op jit(solution)/shard_map/pallas_call | solution.py:30
  43.3 0.1 collective-permute-start.8
  43.4 2.9 %shard_map.136 = (bf16[640,256]{1,0:T(8,128)(2,1)S(1)}, f32[8,128]{1,0:T(8,128)S(1)}) custom-call(f32[1792,256]{1,0:T(8,128)S(1)} %get-tuple-element.91.refs_0_, f32[49,256]{1,0:T(8,128)S(1)} %copy-done.5, bf16[1024,256]{1,0:T(8,128)(2,1)S(1)} %get-tuple-element.77.refs_6_.refs_8_.refs_2_.refs_4_, f32[8,128]{1,0:T(8,128)S(1)} %get-tuple-element.104.refs_3_), custom_call_target="tpu_custom_call" | custom-call | flops 4000000000 | bytes 2409472 | tf_op jit(solution)/shard_map/pallas_call | solution.py:30
  46.4 2.0 %collective-permute-done.8.refs_1_ = bf16[64,1024]{1,0:T(8,128)(2,1)S(1)} collective-permute-done((bf16[64,1024]{1,0:T(8,128)(2,1)S(1)}, bf16[64,1024]{1,0:T(8,128)(2,1)S(1)}, u32[]{:S(2)}, u32[]{:S(2)}) %collective-permute-start.8) | collective-permute-done | bytes 131104 | tf_op jit(solution)/shard_map/ppermute | solution.py:522
  48.4 0.6 collective-permute-start.11
  49.0 2.4 %shard_map.138 = (bf16[1024,256]{1,0:T(8,128)(2,1)S(1)}, bf16[288,256]{1,0:T(8,128)(2,1)S(1)}, bf16[288,256]{1,0:T(8,128)(2,1)S(1)}, f32[8,128]{1,0:T(8,128)S(1)}) custom-call(f32[1792,256]{1,0:T(8,128)S(1)} %get-tuple-element.91.refs_0_, bf16[240,256]{1,0:T(8,128)(2,1)S(1)} %collective-permute-done.5.refs_1_, ...), custom_call_target="tpu_custom_call" | custom-call | flops 4000000000 | bytes 4097024 | tf_op jit(solution)/shard_map/pallas_call | solution.py:30
  51.4 0.1 collective-permute-start.9
  51.5 1.7 %shard_map.139 = (f32[4160,128]{1,0:T(8,128)S(1)}, f32[8,128]{1,0:T(8,128)S(1)}) custom-call(bf16[1024,256]{1,0:T(8,128)(2,1)S(1)} %get-tuple-element.114.refs_0_, bf16[512,512]{1,0:T(8,128)(2,1)S(1)} %get-tuple-element.115.refs_1_, bf16[1024,512]{1,0:T(8,128)(2,1)S(1)} %get-tuple-element.94.refs_5_.refs_2_, f32[8,128]{1,0:T(8,128)S(1)} %get-tuple-element.116.refs_3_), custom_call_target="tpu_custom_call" | custom-call | flops 3000000000 | bytes 2097152 | tf_op jit(solution)/shard_map/pallas_call | solution.py:30
  53.2 1.6 %collective-permute-start.10 = (bf16[288,256]{1,0:T(8,128)(2,1)S(1)}, bf16[288,256]{1,0:T(8,128)(2,1)S(1)}, u32[]{:S(2)}, u32[]{:S(2)}) collective-permute-start(bf16[288,256]{1,0:T(8,128)(2,1)S(1)} %get-tuple-element.118.refs_0_), channel_id=1, source_target_pairs={{0,2},{2,0},{1,3},{3,1},{4,6},{6,4},{5,7},{7,5},{8,10},{10,8},{9,1... | collective-permute-start | bytes 442376 | tf_op jit(solution)/shard_map/ppermute | solution.py:522
  54.8 1.2 %shard_map.141 = (bf16[4096,128]{1,0:T(8,128)(2,1)}, f32[8,128]{1,0:T(8,128)S(1)}) custom-call(f32[4160,128]{1,0:T(8,128)S(1)} %get-tuple-element.120.refs_0_, f32[4096,128]{1,0:T(8,128)S(1)} %get-tuple-element.121.refs_1_, f32[8,128]{1,0:T(8,128)S(1)} %get-tuple-element.122.refs_2_), custom_call_target="tpu_custom_call" | custom-call | flops 2000000000 | bytes 4227072 | tf_op jit(solution)/shard_map/pallas_call | solution.py:30
  56.0 0.0 collective-permute-done.11.refs_1_
  56.1 1.6 %collective-permute-start.13 = (bf16[64,1024]{1,0:T(8,128)(2,1)S(1)}, bf16[64,1024]{1,0:T(8,128)(2,1)S(1)}, u32[]{:S(2)}, u32[]{:S(2)}) collective-permute-start(bf16[64,1024]{1,0:T(8,128)(2,1)S(1)} %get-tuple-element.129.refs_0_), channel_id=1, source_target_pairs={{0,4},{4,0},{8,12},{12,8},{1,5},{5,1},{9,13},{13,9},{2,6},{6,2},{1... | collective-permute-start | bytes 393224 | tf_op jit(solution)/shard_map/ppermute | solution.py:522
  57.7 1.9 %collective-permute-done.10.refs_1_ = bf16[288,256]{1,0:T(8,128)(2,1)S(1)} collective-permute-done((bf16[288,256]{1,0:T(8,128)(2,1)S(1)}, bf16[288,256]{1,0:T(8,128)(2,1)S(1)}, u32[]{:S(2)}, u32[]{:S(2)}) %collective-permute-start.10) | collective-permute-done | bytes 147488 | tf_op jit(solution)/shard_map/ppermute | solution.py:522
  59.6 1.6 %collective-permute-start.12 = (bf16[288,256]{1,0:T(8,128)(2,1)S(1)}, bf16[288,256]{1,0:T(8,128)(2,1)S(1)}, u32[]{:S(2)}, u32[]{:S(2)}) collective-permute-start(bf16[288,256]{1,0:T(8,128)(2,1)S(1)} %get-tuple-element.128.refs_0_), channel_id=1, source_target_pairs={{0,4},{4,0},{8,12},{12,8},{1,5},{5,1},{9,13},{13,9},{2,6},{6,2},{1... | collective-permute-start | bytes 442376 | tf_op jit(solution)/shard_map/ppermute | solution.py:522
  61.2 1.8 %shard_map.144 = (bf16[1024,256]{1,0:T(8,128)(2,1)}, f32[8,128]{1,0:T(8,128)S(1)}) custom-call(bf16[640,256]{1,0:T(8,128)(2,1)S(1)} %get-tuple-element.78.refs_0_, bf16[384,256]{1,0:T(8,128)(2,1)S(1)} %get-tuple-element.85.refs_1_, f32[8,128]{1,0:T(8,128)S(1)} %get-tuple-element.125.refs_2_), custom_call_target="tpu_custom_call" | custom-call | flops 2000000000 | bytes 524288 | tf_op jit(solution)/shard_map/pallas_call | solution.py:30
  63.1 1.6 %collective-permute-start.15 = (bf16[128,1024]{1,0:T(8,128)(2,1)S(1)}, bf16[128,1024]{1,0:T(8,128)(2,1)S(1)}, u32[]{:S(2)}, u32[]{:S(2)}) collective-permute-start(bf16[128,1024]{1,0:T(8,128)(2,1)S(1)} %get-tuple-element.133.refs_0_), channel_id=1, source_target_pairs={{0,2},{2,0},{1,3},{3,1},{4,6},{6,4},{5,7},{7,5},{8,10},{10,8},{9,1... | collective-permute-start | bytes 786440 | tf_op jit(solution)/shard_map/ppermute | solution.py:522
  64.7 0.5 collective-permute-done.12.refs_1_
  65.2 2.4 %collective-permute-start.14 = (bf16[288,256]{1,0:T(8,128)(2,1)S(1)}, bf16[288,256]{1,0:T(8,128)(2,1)S(1)}, u32[]{:S(2)}, u32[]{:S(2)}) collective-permute-start(bf16[288,256]{1,0:T(8,128)(2,1)S(1)} %get-tuple-element.132.refs_0_), channel_id=1, source_target_pairs={{0,8},{4,12},{8,0},{12,4},{1,9},{5,13},{9,1},{13,5},{2,10},{6,14},... | collective-permute-start | bytes 442376 | tf_op jit(solution)/shard_map/ppermute | solution.py:522
  67.6 3.2 %collective-permute-done.15.refs_1_ = bf16[128,1024]{1,0:T(8,128)(2,1)S(1)} collective-permute-done((bf16[128,1024]{1,0:T(8,128)(2,1)S(1)}, bf16[128,1024]{1,0:T(8,128)(2,1)S(1)}, u32[]{:S(2)}, u32[]{:S(2)}) %collective-permute-start.15) | collective-permute-done | bytes 262176 | tf_op jit(solution)/shard_map/ppermute | solution.py:522
  70.8 1.2 %shard_map.147 = (f32[128,1024]{1,0:T(8,128)}, f32[512,256]{1,0:T(8,128)}, f32[8,128]{1,0:T(8,128)S(1)}) custom-call(bf16[128,1024]{1,0:T(8,128)(2,1)S(1)} %get-tuple-element.133.refs_0_, bf16[128,1024]{1,0:T(8,128)(2,1)S(1)} %collective-permute-done.15.refs_1_, f32[8,128]{1,0:T(8,128)S(1)} %get-tuple-element.134.refs_2_), custom_call_target="tpu_custom_call" | custom-call | bytes 524288 | tf_op jit(solution)/shard_map/pallas_call | solution.py:30
  72.0 1.9 %collective-permute-done.14.refs_1_ = bf16[288,256]{1,0:T(8,128)(2,1)S(1)} collective-permute-done((bf16[288,256]{1,0:T(8,128)(2,1)S(1)}, bf16[288,256]{1,0:T(8,128)(2,1)S(1)}, u32[]{:S(2)}, u32[]{:S(2)}) %collective-permute-start.14) | collective-permute-done | bytes 147488 | tf_op jit(solution)/shard_map/ppermute | solution.py:522
  73.9 0.8 %shard_map.148 = (f32[256,256]{1,0:T(8,128)}, f32[49,128]{1,0:T(8,128)}, f32[1,128]{1,0:T(1,128)}, f32[8,128]{1,0:T(8,128)}) custom-call(bf16[288,256]{1,0:T(8,128)(2,1)S(1)} %get-tuple-element.132.refs_0_, bf16[288,256]{1,0:T(8,128)(2,1)S(1)} %collective-permute-done.14.refs_1_, f32[8,128]{1,0:T(8,128)S(1)} %get-tuple-element.135.refs_2_), custom_call_target="tpu_custom_call" | custom-call | bytes 294912 | tf_op jit(solution)/shard_map/pallas_call | solution.py:30
  (21 shorter events, 0.2 us)
Async XLA Ops:
  0.6 1.2 %copy-start = (bf16[2,64,32,128]{3,2,1,0:T(8,128)(2,1)S(1)}, bf16[2,64,32,128]{3,2,1,0:T(8,128)(2,1)}, u32[]{:S(2)}) copy-start(bf16[2,64,32,128]{3,2,1,0:T(8,128)(2,1)} %param.7) | copy-start | bytes 3145732
  1.9 0.9 %copy-start.1 = (bf16[512,256]{1,0:T(8,128)(2,1)S(1)}, bf16[512,256]{1,0:T(8,128)(2,1)}, u32[]{:S(2)}) copy-start(bf16[512,256]{1,0:T(8,128)(2,1)} %refs_1_.5) | copy-start | bytes 786436
  4.8 5.4 %collective-permute-start = (bf16[96,256]{1,0:T(8,128)(2,1)S(1)}, bf16[96,256]{1,0:T(8,128)(2,1)S(1)}, u32[]{:S(2)}, u32[]{:S(2)}) collective-permute-start(bf16[96,256]{1,0:T(8,128)(2,1)S(1)} %get-tuple-element.75), channel_id=1, source_target_pairs={{0,2},{2,0},{1,3},{3,1},{4,6},{6,4},{5,7},{7,5},{8,10},{10,8},{9,1... | collective-permute-start | bytes 147464 | tf_op jit(solution)/shard_map/ppermute | solution.py:522
  7.7 1.0 %copy-start.2 = (bf16[2,32,16,256]{3,2,1,0:T(8,128)(2,1)S(1)}, bf16[2,32,16,256]{3,2,1,0:T(8,128)(2,1)}, u32[]{:S(2)}) copy-start(bf16[2,32,16,256]{3,2,1,0:T(8,128)(2,1)} %param.8) | copy-start | bytes 1572868
  8.7 6.3 %copy-start.3 = (bf16[256,1024]{1,0:T(8,128)(2,1)S(1)}, bf16[256,1024]{1,0:T(8,128)(2,1)}, u32[]{:S(2)}) copy-start(bf16[256,1024]{1,0:T(8,128)(2,1)} %refs_5_.1) | copy-start | bytes 1572868
  8.7 6.3 %copy-start.4 = (bf16[1024,256]{1,0:T(8,128)(2,1)S(1)}, bf16[1024,256]{1,0:T(8,128)(2,1)}, u32[]{:S(2)}) copy-start(bf16[1024,256]{1,0:T(8,128)(2,1)} %refs_6_.1) | copy-start | bytes 1572868
  8.7 6.3 %copy-start.5 = (f32[49,256]{1,0:T(8,128)S(1)}, f32[49,256]{1,0:T(8,128)}, u32[]{:S(2)}) copy-start(f32[49,256]{1,0:T(8,128)} %refs_3_.5) | copy-start | bytes 150532
  8.7 6.3 %copy-start.6 = (f32[256]{0:T(256)S(1)}, f32[256]{0:T(256)}, u32[]{:S(2)}) copy-start(f32[256]{0:T(256)} %param.10) | copy-start | bytes 3076
  11.3 12.3 %collective-permute-start.1 = (bf16[240,256]{1,0:T(8,128)(2,1)S(1)}, bf16[240,256]{1,0:T(8,128)(2,1)S(1)}, u32[]{:S(2)}, u32[]{:S(2)}) collective-permute-start(bf16[240,256]{1,0:T(8,128)(2,1)S(1)} %get-tuple-element.79), channel_id=1, source_target_pairs={{0,4},{4,8},{8,12},{12,0},{1,5},{5,9},{9,13},{13,1},{2,6},{6,10},{... | collective-permute-start | bytes 368648 | tf_op jit(solution)/shard_map/ppermute | solution.py:560
  13.0 10.6 %collective-permute-start.2 = (bf16[240,256]{1,0:T(8,128)(2,1)S(1)}, bf16[240,256]{1,0:T(8,128)(2,1)S(1)}, u32[]{:S(2)}, u32[]{:S(2)}) collective-permute-start(bf16[240,256]{1,0:T(8,128)(2,1)S(1)} %get-tuple-element.80), channel_id=1, source_target_pairs={{4,0},{8,4},{12,8},{0,12},{5,1},{9,5},{13,9},{1,13},{6,2},{10,6},{... | collective-permute-start | bytes 368648 | tf_op jit(solution)/shard_map/ppermute | solution.py:560
  30.2 1.9 %collective-permute-start.4 = (bf16[256,1024]{1,0:T(8,128)(2,1)S(1)}, bf16[256,1024]{1,0:T(8,128)(2,1)S(1)}, u32[]{:S(2)}, u32[]{:S(2)}) collective-permute-start(bf16[256,1024]{1,0:T(8,128)(2,1)S(1)} %get-tuple-element.89), channel_id=1, source_target_pairs={{0,1},{1,0},{2,3},{3,2},{4,5},{5,4},{6,7},{7,6},{8,9},{9,8},{10,11... | collective-permute-start | bytes 1572872 | tf_op jit(solution)/shard_map/ppermute | solution.py:522
  30.2 4.2 %collective-permute-start.3 = (bf16[96,256]{1,0:T(8,128)(2,1)S(1)}, bf16[96,256]{1,0:T(8,128)(2,1)S(1)}, u32[]{:S(2)}, u32[]{:S(2)}) collective-permute-start(bf16[96,256]{1,0:T(8,128)(2,1)S(1)} %get-tuple-element.87), channel_id=1, source_target_pairs={{0,2},{2,0},{1,3},{3,1},{4,6},{6,4},{5,7},{7,5},{8,10},{10,8},{9,1... | collective-permute-start | bytes 147464 | tf_op jit(solution)/shard_map/ppermute | solution.py:522
  32.2 8.8 %collective-permute-start.7 = (bf16[128,1024]{1,0:T(8,128)(2,1)S(1)}, bf16[128,1024]{1,0:T(8,128)(2,1)S(1)}, u32[]{:S(2)}, u32[]{:S(2)}) collective-permute-start(bf16[128,1024]{1,0:T(8,128)(2,1)S(1)} %get-tuple-element.100), channel_id=1, source_target_pairs={{0,2},{2,0},{1,3},{3,1},{4,6},{6,4},{5,7},{7,5},{8,10},{10,8},{9,1... | collective-permute-start | bytes 786440 | tf_op jit(solution)/shard_map/ppermute | solution.py:522
  34.9 14.1 %collective-permute-start.5 = (bf16[240,256]{1,0:T(8,128)(2,1)S(1)}, bf16[240,256]{1,0:T(8,128)(2,1)S(1)}, u32[]{:S(2)}, u32[]{:S(2)}) collective-permute-start(bf16[240,256]{1,0:T(8,128)(2,1)S(1)} %get-tuple-element.92), channel_id=1, source_target_pairs={{0,4},{4,8},{8,12},{12,0},{1,5},{5,9},{9,13},{13,1},{2,6},{6,10},{... | collective-permute-start | bytes 368648 | tf_op jit(solution)/shard_map/ppermute | solution.py:560
  35.0 14.1 %collective-permute-start.6 = (bf16[240,256]{1,0:T(8,128)(2,1)S(1)}, bf16[240,256]{1,0:T(8,128)(2,1)S(1)}, u32[]{:S(2)}, u32[]{:S(2)}) collective-permute-start(bf16[240,256]{1,0:T(8,128)(2,1)S(1)} %get-tuple-element.93), channel_id=1, source_target_pairs={{4,0},{8,4},{12,8},{0,12},{5,1},{9,5},{13,9},{1,13},{6,2},{10,6},{... | collective-permute-start | bytes 368648 | tf_op jit(solution)/shard_map/ppermute | solution.py:560
  43.3 5.0 %collective-permute-start.8 = (bf16[64,1024]{1,0:T(8,128)(2,1)S(1)}, bf16[64,1024]{1,0:T(8,128)(2,1)S(1)}, u32[]{:S(2)}, u32[]{:S(2)}) collective-permute-start(bf16[64,1024]{1,0:T(8,128)(2,1)S(1)} %get-tuple-element.109), channel_id=1, source_target_pairs={{0,4},{4,0},{8,12},{12,8},{1,5},{5,1},{9,13},{13,9},{2,6},{6,2},{1... | collective-permute-start | bytes 393224 | tf_op jit(solution)/shard_map/ppermute | solution.py:522
  48.4 7.6 %collective-permute-start.11 = (bf16[64,1024]{1,0:T(8,128)(2,1)S(1)}, bf16[64,1024]{1,0:T(8,128)(2,1)S(1)}, u32[]{:S(2)}, u32[]{:S(2)}) collective-permute-start(bf16[64,1024]{1,0:T(8,128)(2,1)S(1)} %get-tuple-element.119.refs_0_), channel_id=1, source_target_pairs={{0,8},{4,12},{8,0},{12,4},{1,9},{5,13},{9,1},{13,5},{2,10},{6,14},... | collective-permute-start | bytes 393224 | tf_op jit(solution)/shard_map/ppermute | solution.py:522
  51.4 1.7 %collective-permute-start.9 = (bf16[288,256]{1,0:T(8,128)(2,1)S(1)}, bf16[288,256]{1,0:T(8,128)(2,1)S(1)}, u32[]{:S(2)}, u32[]{:S(2)}) collective-permute-start(bf16[288,256]{1,0:T(8,128)(2,1)S(1)} %get-tuple-element.113), channel_id=1, source_target_pairs={{0,1},{1,0},{2,3},{3,2},{4,5},{5,4},{6,7},{7,6},{8,9},{9,8},{10,11... | collective-permute-start | bytes 442376 | tf_op jit(solution)/shard_map/ppermute | solution.py:522
  53.2 6.3 %collective-permute-start.10 = (bf16[288,256]{1,0:T(8,128)(2,1)S(1)}, bf16[288,256]{1,0:T(8,128)(2,1)S(1)}, u32[]{:S(2)}, u32[]{:S(2)}) collective-permute-start(bf16[288,256]{1,0:T(8,128)(2,1)S(1)} %get-tuple-element.118.refs_0_), channel_id=1, source_target_pairs={{0,2},{2,0},{1,3},{3,1},{4,6},{6,4},{5,7},{7,5},{8,10},{10,8},{9,1... | collective-permute-start | bytes 442376 | tf_op jit(solution)/shard_map/ppermute | solution.py:522
  56.1 7.0 %collective-permute-start.13 = (bf16[64,1024]{1,0:T(8,128)(2,1)S(1)}, bf16[64,1024]{1,0:T(8,128)(2,1)S(1)}, u32[]{:S(2)}, u32[]{:S(2)}) collective-permute-start(bf16[64,1024]{1,0:T(8,128)(2,1)S(1)} %get-tuple-element.129.refs_0_), channel_id=1, source_target_pairs={{0,4},{4,0},{8,12},{12,8},{1,5},{5,1},{9,13},{13,9},{2,6},{6,2},{1... | collective-permute-start | bytes 393224 | tf_op jit(solution)/shard_map/ppermute | solution.py:522
  59.6 5.5 %collective-permute-start.12 = (bf16[288,256]{1,0:T(8,128)(2,1)S(1)}, bf16[288,256]{1,0:T(8,128)(2,1)S(1)}, u32[]{:S(2)}, u32[]{:S(2)}) collective-permute-start(bf16[288,256]{1,0:T(8,128)(2,1)S(1)} %get-tuple-element.128.refs_0_), channel_id=1, source_target_pairs={{0,4},{4,0},{8,12},{12,8},{1,5},{5,1},{9,13},{13,9},{2,6},{6,2},{1... | collective-permute-start | bytes 442376 | tf_op jit(solution)/shard_map/ppermute | solution.py:522
  63.1 7.7 %collective-permute-start.15 = (bf16[128,1024]{1,0:T(8,128)(2,1)S(1)}, bf16[128,1024]{1,0:T(8,128)(2,1)S(1)}, u32[]{:S(2)}, u32[]{:S(2)}) collective-permute-start(bf16[128,1024]{1,0:T(8,128)(2,1)S(1)} %get-tuple-element.133.refs_0_), channel_id=1, source_target_pairs={{0,2},{2,0},{1,3},{3,1},{4,6},{6,4},{5,7},{7,5},{8,10},{10,8},{9,1... | collective-permute-start | bytes 786440 | tf_op jit(solution)/shard_map/ppermute | solution.py:522
  65.2 8.7 %collective-permute-start.14 = (bf16[288,256]{1,0:T(8,128)(2,1)S(1)}, bf16[288,256]{1,0:T(8,128)(2,1)S(1)}, u32[]{:S(2)}, u32[]{:S(2)}) collective-permute-start(bf16[288,256]{1,0:T(8,128)(2,1)S(1)} %get-tuple-element.132.refs_0_), channel_id=1, source_target_pairs={{0,8},{4,12},{8,0},{12,4},{1,9},{5,13},{9,1},{13,5},{2,10},{6,14},... | collective-permute-start | bytes 442376 | tf_op jit(solution)/shard_map/ppermute | solution.py:522

commit v5 on v4

--- a/solution.py
+++ b/solution.py
@@ -235,13 +235,7 @@
 
 
 def gelu_parts(x):
-    t = 1.0 / (1.0 + jnp.abs(x) * (0.3275911 * 0.7071067811865476))
-    bell = jnp.exp(-0.5 * x * x)
-    poly = 0.5 * 1.061405429
-    for c in (-1.453152027, 1.421413741, -0.284496736, 0.254829592):
-        poly = poly * t + 0.5 * c
-    tail = poly * t * bell
-    return jnp.where(x >= 0, 1.0 - tail, tail), x * bell * 0.3989422804014327
+    return 0.5 + 0.5 * lax.erf(x * 0.7071067811865476), x * jnp.exp(-0.5 * x * x) * 0.3989422804014327
 
 
 def row_mean(z, x):
@@ -268,7 +262,7 @@
             normed_s[at, lanes] = (unit * gain_ref[:, lanes]).astype(BF16)
         return 0
 
-    lax.fori_loop(0, count // z.col, step, 0, unroll=2)
+    lax.fori_loop(0, count // z.col, step, 0, unroll=count // z.col // 2)
     for low, full, size in groups:
         weighted_s[low : low + size, :] = weighted_ref[full : full + size, :]
     gain_sum = jnp.zeros((SUB, z.channels), F32)
@@ -303,7 +297,7 @@
     size = (z.cols - 2 * M) * z.col
     refs = (gain_ref, we_ref, wc_ref, coarse_ref, weighted_ref)
     gain_sum_ref[...] = section(
-        z, pad_ref, lambda j: j, [(0, M * z.col, size)], refs, scratch, size // 2, section_ref, mixed_ref, taps_s
+        z, pad_ref, lambda j: j, [(0, M * z.col, size)], refs, scratch, size, section_ref, mixed_ref, taps_s
     )
     unit_s, inv_s, normed_s, hidden_s, slope_s, weighted_s = scratch
     expand_ref[...] = dot_tn(normed_s[...], slope_s[...])
@@ -315,7 +309,7 @@
     expand_ref, contract_ref, gain_sum_ref, inner_mixed_ref,
     section_ref, mixed_ref, mine_ref, other_ref, low_ref, gain_out_ref, left_out_ref, right_out_ref, *rest,
 ):
-    *edge_refs, taps_s, edge_s, sum_s, split_s, slab_s = rest[:-6]
+    *edge_refs, taps_s, edge_s, split_s, slab_s = rest[:-6]
     scratch = rest[-6:]
     spread_taps(z, kern_ref, taps_s)
     edge_columns(z, left_ref, pad_ref, right_ref, edge_s, slab_s)
@@ -329,16 +323,16 @@
     )
     unit_s, inv_s, normed_s, hidden_s, slope_s, weighted_s = scratch
     gain_out_ref[...] = gain_sum + gain_sum_ref[...]
-    sum_s[0, :, :] = expand_ref[...] + dot_tn(normed_s[...], slope_s[...])
-    sum_s[1, :, :] = contract_ref[...] + dot_tn(weighted_s[...], hidden_s[...])
-    own = lax.axis_index("dp")
     half, cut = z.channels // 2, z.wide // 2
-    for ref, owner in ((mine_ref, own), (other_ref, 1 - own)):
-        ref[0:half, :] = sum_s[0, rows16(owner * half, half), :].astype(BF16)
-        for t in range(2):
-            ref[half:, t * cut : (t + 1) * cut] = sum_s[1, t * half : (t + 1) * half, lanes_at(owner * cut, cut)].astype(
-                BF16
-            )
+    first = lax.axis_index("dp") == 0
+    total = (expand_ref[...] + dot_tn(normed_s[...], slope_s[...])).astype(BF16)
+    mine_ref[0:half, :] = jnp.where(first, total[:half], total[half:])
+    other_ref[0:half, :] = jnp.where(first, total[half:], total[:half])
+    total = (contract_ref[...] + dot_tn(weighted_s[...], hidden_s[...])).astype(BF16)
+    for t in range(2):
+        low, high = total[t * half : (t + 1) * half, :cut], total[t * half : (t + 1) * half, cut:]
+        mine_ref[half:, t * cut : (t + 1) * cut] = jnp.where(first, low, high)
+        other_ref[half:, t * cut : (t + 1) * cut] = jnp.where(first, high, low)
     low_ref[0:size, :] = mixed_ref[0:size, :].astype(BF16)
     low_ref[size : z.cells - size, :] = inner_mixed_ref[...].astype(BF16)
     low_ref[z.cells - size :, :] = mixed_ref[size:, :].astype(BF16)
@@ -365,7 +359,7 @@
             return tuple(sums[a] + jnp.sum(column[a : a + z.block_rows] * back, axis=0) for a in range(KS))
 
         zeros = tuple(jnp.zeros((SUB, LANE), F32) for _ in range(KS))
-        sums = lax.fori_loop(0, z.cols, step, zeros, unroll=2)
+        sums = lax.fori_loop(0, z.cols, step, zeros, unroll=4)
         for a in range(KS):
             t = a * KS + e
             out_ref[t : t + 1, :] = jnp.sum(sums[a], axis=0, keepdims=True)
@@ -388,7 +382,7 @@
         )
         return 0
 
-    lax.fori_loop(0, z.cols - 2 * M, step, 0, unroll=2)
+    lax.fori_loop(0, z.cols - 2 * M, step, 0, unroll=5)
 
 
 def edge_columns(z, left_ref, pad_ref, right_ref, edge_s, slab_s):
@@ -412,7 +406,7 @@
             spread(z, edge_s, taps_s, source + j, at, at, weighted_ref, coarse_ref)
         return 0
 
-    lax.fori_loop(0, M, step, 0)
+    lax.fori_loop(0, M, step, 0, unroll=True)
     size = M * z.col
     coarse_ref[size : z.cells - size, :] = inner_ref[...]
     sum_s[...] = dot_tn(coarse_ref[...], patches_ref[...])
@@ -626,7 +620,7 @@
         ],
         (pad, left, right, conv_kernel, gain, w_expand, w_contract, coarse, weighted)
         + (expand, contract, gain_sum, mixed_in),
-        [taps_s, ((6 * M * z.pad_col, ch), F32), ((2, ch, ff), F32), split, slab_s] + section_scratch(outer),
+        [taps_s, ((6 * M * z.pad_col, ch), F32), split, slab_s] + section_scratch(outer),
         flops=8_000_000_000,
     )
     before, after = lat_margins(*send)
@@ -652,7 +646,7 @@
     wide, away, token = add(wide, swap(away, *steps[0]), after=(token,), halve=steps[1])
     high_aux, token = terms(1, token)
     back_inner, token = kernel_call(
-        part(back_inner_kernel, z), [bf(inner, ch)], (pad_low, conv_kernel, weighted), [taps_s], 4_000_000_000, (token,)
+        part(back_inner_kernel, z), [bf(inner, ch)], (pad_low, conv_kernel, weighted), [taps_s], 500_000_000, (token,)
     )
     for n in range(1, halvings - 1):
         wide, away, token = add(wide, swap(away, *steps[n]), after=(token,), halve=steps[n + 1])

time: 75 us -> 70.4 us (0.939)
  Pallas kernels: 37 us -> 32.7 us
    pallas_call x23, Pallas kernels: 37 us -> 32.7 us  [kernel_call(): pl.pallas_call(run, out_shape=[jax.ShapeDtypeStruct(s, d) for s, d in out...]
  transfers between devices with their start and end apart: 16 -> 16, of which waited for: 7 -> 7; matrix products, arithmetic and copies ran while one was open for 0% -> 0% of each run, Pallas kernels for 36% -> 34%
where the time goes in v5:
time: 70.4 us; the launch traced here: 70.2 us
  Pallas kernels  32.7 us (46%)
  starting transfers between devices  22.9 us (33%)
  waiting for transfers between devices  10.6 us (15%)
  local copies, waits for them, and re-layouts  3.22 us (5%)
  between operations  0.81 us (1%)
    pallas_call x23, Pallas kernels, kernel_call(): pl.pallas_call(run, out_shape=[jax.ShapeDtypeStruct(s, d) for s, d in out...  32.7 us
    ppermute x12, starting transfers between devices, swap(): return lax.ppermute(x, axis, [(i, i ^ distance) for i in range(size)])  15.2 us
    ppermute x12, waiting for transfers between devices, swap(): return lax.ppermute(x, axis, [(i, i ^ distance) for i in range(size)])  10.6 us
    ppermute x2, starting transfers between devices, lon_margins(): lax.ppermute(left, 'lon', [(j, i) for i, j in up])  5.9 us
    unnamed x14, local copies, waits for them, and re-layouts  3.22 us
    ppermute x2, starting transfers between devices, lon_margins(): lax.ppermute(right, 'lon', up)  1.79 us
  transfers between devices with their start and end apart: 16, of which 7 were waited for; matrix products, arithmetic and copies ran while one was open for 0% of the time, Pallas kernels for 34%

profile of v5, /device:TPU:0, one launch (start us, length us, event | category | flops | bytes accessed | tf_op | source)
XLA Modules:
  0.0 70.2 jit_solution(906756427602715421)
XLA Ops:
  0.6 1.2 %copy-done = bf16[2,64,32,128]{3,2,1,0:T(8,128)(2,1)S(1)} copy-done((bf16[2,64,32,128]{3,2,1,0:T(8,128)(2,1)S(1)}, bf16[2,64,32,128]{3,2,1,0:T(8,128)(2,1)}, u32[]{:S(2)}) %copy-start) | copy-done | bytes 1048600
  1.9 0.9 %copy-done.1 = bf16[512,256]{1,0:T(8,128)(2,1)S(1)} copy-done((bf16[512,256]{1,0:T(8,128)(2,1)S(1)}, bf16[512,256]{1,0:T(8,128)(2,1)}, u32[]{:S(2)}) %copy-start.1) | copy-done | bytes 262168
  2.8 2.0 %shard_map.126 = (bf16[1024,512]{1,0:T(8,128)(2,1)S(1)}, bf16[1024,256]{1,0:T(8,128)(2,1)S(1)}, f32[4096,128]{1,0:T(8,128)S(1)}, bf16[96,256]{1,0:T(8,128)(2,1)S(1)}, f32[8,128]{1,0:T(8,128)}) custom-call(bf16[4096,128]{1,0:T(8,128)(2,1)S(1)} %bitcast.6, bf16[512,256]{1,0:T(8,128)(2,1)S(1)} %copy-done.1), custom_call_target="tpu_custom_call" | custom-call | bytes 1310720 | tf_op jit(solution)/shard_map/pallas_call | solution.py:30
  4.8 2.9 %collective-permute-start = (bf16[96,256]{1,0:T(8,128)(2,1)S(1)}, bf16[96,256]{1,0:T(8,128)(2,1)S(1)}, u32[]{:S(2)}, u32[]{:S(2)}) collective-permute-start(bf16[96,256]{1,0:T(8,128)(2,1)S(1)} %get-tuple-element.75), channel_id=1, source_target_pairs={{0,2},{2,0},{1,3},{3,1},{4,6},{6,4},{5,7},{7,5},{8,10},{10,8},{9,1... | collective-permute-start | bytes 147464 | tf_op jit(solution)/shard_map/ppermute | solution.py:516
  7.7 1.0 %copy-done.3 = bf16[2,32,16,256]{3,2,1,0:T(8,128)(2,1)S(1)} copy-done((bf16[2,32,16,256]{3,2,1,0:T(8,128)(2,1)S(1)}, bf16[2,32,16,256]{3,2,1,0:T(8,128)(2,1)}, u32[]{:S(2)}) %copy-start.3) | copy-done | bytes 524312
  8.8 1.4 %shard_map.128 = (bf16[1024,256]{1,0:T(8,128)(2,1)S(1)}, bf16[512,512]{1,0:T(8,128)(2,1)S(1)}, f32[8,128]{1,0:T(8,128)}) custom-call(bf16[1024,256]{1,0:T(8,128)(2,1)S(1)} %bitcast.7, bf16[512,256]{1,0:T(8,128)(2,1)S(1)} %copy-done.1), custom_call_target="tpu_custom_call" | custom-call | flops 2000000000 | bytes 786432 | tf_op jit(solution)/shard_map/pallas_call | solution.py:30
  10.1 0.0 collective-permute-done.refs_1_.refs_2_
  10.1 1.1 %shard_map.127 = (f32[1792,256]{1,0:T(8,128)S(1)}, bf16[240,256]{1,0:T(8,128)(2,1)S(1)}, bf16[240,256]{1,0:T(8,128)(2,1)S(1)}, f32[8,128]{1,0:T(8,128)}) custom-call(bf16[1024,256]{1,0:T(8,128)(2,1)S(1)} %get-tuple-element.74.refs_0_.refs_5_.refs_7_, bf16[96,256]{1,0:T(8,128)(2,1)S(1)} %collective-permute-done.refs_1_.refs_2_, ...), custom_call_target="tpu_custom_call" | custom-call | bytes 622592 | tf_op jit(solution)/shard_map/pallas_call | solution.py:30
  11.3 1.7 %collective-permute-start.1 = (bf16[240,256]{1,0:T(8,128)(2,1)S(1)}, bf16[240,256]{1,0:T(8,128)(2,1)S(1)}, u32[]{:S(2)}, u32[]{:S(2)}) collective-permute-start(bf16[240,256]{1,0:T(8,128)(2,1)S(1)} %get-tuple-element.79), channel_id=1, source_target_pairs={{0,4},{4,8},{8,12},{12,0},{1,5},{5,9},{9,13},{13,1},{2,6},{6,10},{... | collective-permute-start | bytes 368648 | tf_op jit(solution)/shard_map/ppermute | solution.py:554
  13.0 2.1 %collective-permute-start.2 = (bf16[240,256]{1,0:T(8,128)(2,1)S(1)}, bf16[240,256]{1,0:T(8,128)(2,1)S(1)}, u32[]{:S(2)}, u32[]{:S(2)}) collective-permute-start(bf16[240,256]{1,0:T(8,128)(2,1)S(1)} %get-tuple-element.80), channel_id=1, source_target_pairs={{4,0},{8,4},{12,8},{0,12},{5,1},{9,5},{13,9},{1,13},{6,2},{10,6},{... | collective-permute-start | bytes 368648 | tf_op jit(solution)/shard_map/ppermute | solution.py:554
  15.1 6.8 %shard_map.129 = (bf16[640,256]{1,0:T(8,128)(2,1)S(1)}, f32[640,256]{1,0:T(8,128)S(1)}, f32[256,1024]{1,0:T(8,128)S(1)}, f32[256,1024]{1,0:T(8,128)S(1)}, f32[8,256]{1,0:T(8,128)S(1)}, /*index=5*/f32[8,128]{1,0:T(8,128)}) custom-call(f32[1792,256]{1,0:T(8,128)S(1)} %get-tuple-element.76.refs_0_, f32[49,256]{1,0:T(8,128)S(1)} %copy-done.2, ...), custom_call_target="tpu_custom_call" | custom-call | flops 8000000000 | bytes 3983360 | tf_op jit(solution)/shard_map/pallas_call | solution.py:30
  21.9 0.0 collective-permute-done.2.refs_2_
  21.9 5.1 %shard_map.130 = (bf16[384,256]{1,0:T(8,128)(2,1)S(1)}, f32[384,256]{1,0:T(8,128)S(1)}, bf16[256,1024]{1,0:T(8,128)(2,1)S(1)}, bf16[256,1024]{1,0:T(8,128)(2,1)S...) custom-call(f32[1792,256]{1,0:T(8,128)S(1)} %get-tuple-element.76.re, ...), custom_call_target="tpu_custom_call" | custom-call | flops 8000000000 | bytes 6989824 | tf_op jit(solution)/shard_map/pallas_call | solution.py:30
  27.0 0.1 collective-permute-start.4
  27.1 1.7 %collective-permute-start.3 = (bf16[96,256]{1,0:T(8,128)(2,1)S(1)}, bf16[96,256]{1,0:T(8,128)(2,1)S(1)}, u32[]{:S(2)}, u32[]{:S(2)}) collective-permute-start(bf16[96,256]{1,0:T(8,128)(2,1)S(1)} %get-tuple-element.87), channel_id=1, source_target_pairs={{0,2},{2,0},{1,3},{3,1},{4,6},{6,4},{5,7},{7,5},{8,10},{10,8},{9,1... | collective-permute-start | bytes 147464 | tf_op jit(solution)/shard_map/ppermute | solution.py:516
  28.8 0.2 collective-permute-done.4.refs_1_
  29.0 0.1 shard_map.131
  29.1 1.7 %collective-permute-start.7 = (bf16[128,1024]{1,0:T(8,128)(2,1)S(1)}, bf16[128,1024]{1,0:T(8,128)(2,1)S(1)}, u32[]{:S(2)}, u32[]{:S(2)}) collective-permute-start(bf16[128,1024]{1,0:T(8,128)(2,1)S(1)} %get-tuple-element.100), channel_id=1, source_target_pairs={{0,2},{2,0},{1,3},{3,1},{4,6},{6,4},{5,7},{7,5},{8,10},{10,8},{9,1... | collective-permute-start | bytes 786440 | tf_op jit(solution)/shard_map/ppermute | solution.py:516
  30.8 0.4 collective-permute-done.3.refs_1_.refs_2_
  31.2 0.6 shard_map.132
  31.8 0.1 collective-permute-start.5
  31.9 3.8 %collective-permute-start.6 = (bf16[240,256]{1,0:T(8,128)(2,1)S(1)}, bf16[240,256]{1,0:T(8,128)(2,1)S(1)}, u32[]{:S(2)}, u32[]{:S(2)}) collective-permute-start(bf16[240,256]{1,0:T(8,128)(2,1)S(1)} %get-tuple-element.93), channel_id=1, source_target_pairs={{4,0},{8,4},{12,8},{0,12},{5,1},{9,5},{13,9},{1,13},{6,2},{10,6},{... | collective-permute-start | bytes 368648 | tf_op jit(solution)/shard_map/ppermute | solution.py:554
  35.7 2.0 %shard_map.133 = (f32[64,128]{1,0:T(8,128)S(1)}, f32[8,128]{1,0:T(8,128)S(1)}) custom-call(f32[1792,256]{1,0:T(8,128)S(1)} %get-tuple-element.76.refs_0_, f32[336,256]{1,0:T(8,128)S(1)} %get-tuple-element.95.refs_1_, f32[336,256]{1,0:T(8,128)S(1)} %get-tuple-element.96.refs_2_, f32[640,256]{1,0:T(8,128)S(1)} %get-tuple-element.84.refs_12_.refs_3_, ...), custom_call_target="tpu_custom_call" | custom-call | flops 3000000000 | bytes 3579904 | tf_op jit(solution)/shard_map/pallas_call | solution.py:30
  37.7 0.1 shard_map.134
  37.8 0.1 collective-permute-start.8
  37.9 2.0 %shard_map.135 = (f32[64,128]{1,0:T(8,128)S(1)}, f32[8,128]{1,0:T(8,128)S(1)}) custom-call(f32[1792,256]{1,0:T(8,128)S(1)} %get-tuple-element.76.refs_0_, f32[336,256]{1,0:T(8,128)S(1)} %get-tuple-element.95.refs_1_, f32[336,256]{1,0:T(8,128)S(1)} %get-tuple-element.96.refs_2_, f32[640,256]{1,0:T(8,128)S(1)} %get-tuple-element.84.refs_12_.refs_3_, ...), custom_call_target="tpu_custom_call" | custom-call | flops 3000000000 | bytes 3579904 | tf_op jit(solution)/shard_map/pallas_call | solution.py:30
  39.9 2.5 %shard_map.136 = (bf16[640,256]{1,0:T(8,128)(2,1)S(1)}, f32[8,128]{1,0:T(8,128)S(1)}) custom-call(f32[1792,256]{1,0:T(8,128)S(1)} %get-tuple-element.91.refs_0_, f32[49,256]{1,0:T(8,128)S(1)} %copy-done.2, bf16[1024,256]{1,0:T(8,128)(2,1)S(1)} %get-tuple-element.77.refs_6_.refs_8_.refs_2_.refs_4_, f32[8,128]{1,0:T(8,128)S(1)} %get-tuple-element.104.refs_3_), custom_call_target="tpu_custom_call" | custom-call | flops 500000000 | bytes 2409472 | tf_op jit(solution)/shard_map/pallas_call | solution.py:30
  42.4 0.4 collective-permute-done.8.refs_1_
  42.9 1.9 %collective-permute-start.11 = (bf16[64,1024]{1,0:T(8,128)(2,1)S(1)}, bf16[64,1024]{1,0:T(8,128)(2,1)S(1)}, u32[]{:S(2)}, u32[]{:S(2)}) collective-permute-start(bf16[64,1024]{1,0:T(8,128)(2,1)S(1)} %get-tuple-element.119.refs_0_), channel_id=1, source_target_pairs={{0,8},{4,12},{8,0},{12,4},{1,9},{5,13},{9,1},{13,5},{2,10},{6,14},... | collective-permute-start | bytes 393224 | tf_op jit(solution)/shard_map/ppermute | solution.py:516
  44.8 0.0 collective-permute-done.5.refs_1_
  44.8 0.0 collective-permute-done.6.refs_2_
  44.8 2.1 %shard_map.138 = (bf16[1024,256]{1,0:T(8,128)(2,1)S(1)}, bf16[288,256]{1,0:T(8,128)(2,1)S(1)}, bf16[288,256]{1,0:T(8,128)(2,1)S(1)}, f32[8,128]{1,0:T(8,128)S(1)}) custom-call(f32[1792,256]{1,0:T(8,128)S(1)} %get-tuple-element.91.refs_0_, bf16[240,256]{1,0:T(8,128)(2,1)S(1)} %collective-permute-done.5.refs_1_, ...), custom_call_target="tpu_custom_call" | custom-call | flops 4000000000 | bytes 4097024 | tf_op jit(solution)/shard_map/pallas_call | solution.py:30
  46.9 0.1 collective-permute-start.9
  47.0 1.7 %shard_map.139 = (f32[4160,128]{1,0:T(8,128)S(1)}, f32[8,128]{1,0:T(8,128)S(1)}) custom-call(bf16[1024,256]{1,0:T(8,128)(2,1)S(1)} %get-tuple-element.114.refs_0_, bf16[512,512]{1,0:T(8,128)(2,1)S(1)} %get-tuple-element.115.refs_1_, bf16[1024,512]{1,0:T(8,128)(2,1)S(1)} %get-tuple-element.94.refs_5_.refs_2_, f32[8,128]{1,0:T(8,128)S(1)} %get-tuple-element.116.refs_3_), custom_call_target="tpu_custom_call" | custom-call | flops 3000000000 | bytes 2097152 | tf_op jit(solution)/shard_map/pallas_call | solution.py:30
  48.7 0.0 collective-permute-done.9.refs_1_
  48.7 1.6 %collective-permute-start.10 = (bf16[288,256]{1,0:T(8,128)(2,1)S(1)}, bf16[288,256]{1,0:T(8,128)(2,1)S(1)}, u32[]{:S(2)}, u32[]{:S(2)}) collective-permute-start(bf16[288,256]{1,0:T(8,128)(2,1)S(1)} %get-tuple-element.118.refs_0_), channel_id=1, source_target_pairs={{0,2},{2,0},{1,3},{3,1},{4,6},{6,4},{5,7},{7,5},{8,10},{10,8},{9,1... | collective-permute-start | bytes 442376 | tf_op jit(solution)/shard_map/ppermute | solution.py:516
  50.3 1.2 %shard_map.141 = (bf16[4096,128]{1,0:T(8,128)(2,1)}, f32[8,128]{1,0:T(8,128)S(1)}) custom-call(f32[4160,128]{1,0:T(8,128)S(1)} %get-tuple-element.120.refs_0_, f32[4096,128]{1,0:T(8,128)S(1)} %get-tuple-element.121.refs_1_, f32[8,128]{1,0:T(8,128)S(1)} %get-tuple-element.122.refs_2_), custom_call_target="tpu_custom_call" | custom-call | flops 2000000000 | bytes 4227072 | tf_op jit(solution)/shard_map/pallas_call | solution.py:30
  51.5 1.2 %collective-permute-start.13 = (bf16[64,1024]{1,0:T(8,128)(2,1)S(1)}, bf16[64,1024]{1,0:T(8,128)(2,1)S(1)}, u32[]{:S(2)}, u32[]{:S(2)}) collective-permute-start(bf16[64,1024]{1,0:T(8,128)(2,1)S(1)} %get-tuple-element.129.refs_0_), channel_id=1, source_target_pairs={{0,4},{4,0},{8,12},{12,8},{1,5},{5,1},{9,13},{13,9},{2,6},{6,2},{1... | collective-permute-start | bytes 393224 | tf_op jit(solution)/shard_map/ppermute | solution.py:516
  52.8 2.3 %collective-permute-done.10.refs_1_ = bf16[288,256]{1,0:T(8,128)(2,1)S(1)} collective-permute-done((bf16[288,256]{1,0:T(8,128)(2,1)S(1)}, bf16[288,256]{1,0:T(8,128)(2,1)S(1)}, u32[]{:S(2)}, u32[]{:S(2)}) %collective-permute-start.10) | collective-permute-done | bytes 147488 | tf_op jit(solution)/shard_map/ppermute | solution.py:516
  55.1 1.1 %collective-permute-start.12 = (bf16[288,256]{1,0:T(8,128)(2,1)S(1)}, bf16[288,256]{1,0:T(8,128)(2,1)S(1)}, u32[]{:S(2)}, u32[]{:S(2)}) collective-permute-start(bf16[288,256]{1,0:T(8,128)(2,1)S(1)} %get-tuple-element.128.refs_0_), channel_id=1, source_target_pairs={{0,4},{4,0},{8,12},{12,8},{1,5},{5,1},{9,13},{13,9},{2,6},{6,2},{1... | collective-permute-start | bytes 442376 | tf_op jit(solution)/shard_map/ppermute | solution.py:516
  56.2 1.8 %shard_map.144 = (bf16[1024,256]{1,0:T(8,128)(2,1)}, f32[8,128]{1,0:T(8,128)S(1)}) custom-call(bf16[640,256]{1,0:T(8,128)(2,1)S(1)} %get-tuple-element.78.refs_0_, bf16[384,256]{1,0:T(8,128)(2,1)S(1)} %get-tuple-element.85.refs_1_, f32[8,128]{1,0:T(8,128)S(1)} %get-tuple-element.125.refs_2_), custom_call_target="tpu_custom_call" | custom-call | flops 2000000000 | bytes 524288 | tf_op jit(solution)/shard_map/pallas_call | solution.py:30
  58.1 1.7 %collective-permute-start.15 = (bf16[128,1024]{1,0:T(8,128)(2,1)S(1)}, bf16[128,1024]{1,0:T(8,128)(2,1)S(1)}, u32[]{:S(2)}, u32[]{:S(2)}) collective-permute-start(bf16[128,1024]{1,0:T(8,128)(2,1)S(1)} %get-tuple-element.133.refs_0_), channel_id=1, source_target_pairs={{0,2},{2,0},{1,3},{3,1},{4,6},{6,4},{5,7},{7,5},{8,10},{10,8},{9,1... | collective-permute-start | bytes 786440 | tf_op jit(solution)/shard_map/ppermute | solution.py:516
  59.8 0.8 %collective-permute-done.12.refs_1_ = bf16[288,256]{1,0:T(8,128)(2,1)S(1)} collective-permute-done((bf16[288,256]{1,0:T(8,128)(2,1)S(1)}, bf16[288,256]{1,0:T(8,128)(2,1)S(1)}, u32[]{:S(2)}, u32[]{:S(2)}) %collective-permute-start.12) | collective-permute-done | bytes 147488 | tf_op jit(solution)/shard_map/ppermute | solution.py:516
  60.7 1.1 %collective-permute-start.14 = (bf16[288,256]{1,0:T(8,128)(2,1)S(1)}, bf16[288,256]{1,0:T(8,128)(2,1)S(1)}, u32[]{:S(2)}, u32[]{:S(2)}) collective-permute-start(bf16[288,256]{1,0:T(8,128)(2,1)S(1)} %get-tuple-element.132.refs_0_), channel_id=1, source_target_pairs={{0,8},{4,12},{8,0},{12,4},{1,9},{5,13},{9,1},{13,5},{2,10},{6,14},... | collective-permute-start | bytes 442376 | tf_op jit(solution)/shard_map/ppermute | solution.py:516
  61.8 4.0 %collective-permute-done.15.refs_1_ = bf16[128,1024]{1,0:T(8,128)(2,1)S(1)} collective-permute-done((bf16[128,1024]{1,0:T(8,128)(2,1)S(1)}, bf16[128,1024]{1,0:T(8,128)(2,1)S(1)}, u32[]{:S(2)}, u32[]{:S(2)}) %collective-permute-start.15) | collective-permute-done | bytes 262176 | tf_op jit(solution)/shard_map/ppermute | solution.py:516
  65.8 1.2 %shard_map.147 = (f32[128,1024]{1,0:T(8,128)}, f32[512,256]{1,0:T(8,128)}, f32[8,128]{1,0:T(8,128)S(1)}) custom-call(bf16[128,1024]{1,0:T(8,128)(2,1)S(1)} %get-tuple-element.133.refs_0_, bf16[128,1024]{1,0:T(8,128)(2,1)S(1)} %collective-permute-done.15.refs_1_, f32[8,128]{1,0:T(8,128)S(1)} %get-tuple-element.134.refs_2_), custom_call_target="tpu_custom_call" | custom-call | bytes 524288 | tf_op jit(solution)/shard_map/pallas_call | solution.py:30
  66.9 2.4 %collective-permute-done.14.refs_1_ = bf16[288,256]{1,0:T(8,128)(2,1)S(1)} collective-permute-done((bf16[288,256]{1,0:T(8,128)(2,1)S(1)}, bf16[288,256]{1,0:T(8,128)(2,1)S(1)}, u32[]{:S(2)}, u32[]{:S(2)}) %collective-permute-start.14) | collective-permute-done | bytes 147488 | tf_op jit(solution)/shard_map/ppermute | solution.py:516
  69.4 0.8 %shard_map.148 = (f32[256,256]{1,0:T(8,128)}, f32[49,128]{1,0:T(8,128)}, f32[1,128]{1,0:T(1,128)}, f32[8,128]{1,0:T(8,128)}) custom-call(bf16[288,256]{1,0:T(8,128)(2,1)S(1)} %get-tuple-element.132.refs_0_, bf16[288,256]{1,0:T(8,128)(2,1)S(1)} %collective-permute-done.14.refs_1_, f32[8,128]{1,0:T(8,128)S(1)} %get-tuple-element.135.refs_2_), custom_call_target="tpu_custom_call" | custom-call | bytes 294912 | tf_op jit(solution)/shard_map/pallas_call | solution.py:30
  (21 shorter events, 0.2 us)
Async XLA Ops:
  0.6 1.2 %copy-start = (bf16[2,64,32,128]{3,2,1,0:T(8,128)(2,1)S(1)}, bf16[2,64,32,128]{3,2,1,0:T(8,128)(2,1)}, u32[]{:S(2)}) copy-start(bf16[2,64,32,128]{3,2,1,0:T(8,128)(2,1)} %param.7) | copy-start | bytes 3145732
  1.9 0.9 %copy-start.1 = (bf16[512,256]{1,0:T(8,128)(2,1)S(1)}, bf16[512,256]{1,0:T(8,128)(2,1)}, u32[]{:S(2)}) copy-start(bf16[512,256]{1,0:T(8,128)(2,1)} %refs_1_.5) | copy-start | bytes 786436
  4.8 5.4 %collective-permute-start = (bf16[96,256]{1,0:T(8,128)(2,1)S(1)}, bf16[96,256]{1,0:T(8,128)(2,1)S(1)}, u32[]{:S(2)}, u32[]{:S(2)}) collective-permute-start(bf16[96,256]{1,0:T(8,128)(2,1)S(1)} %get-tuple-element.75), channel_id=1, source_target_pairs={{0,2},{2,0},{1,3},{3,1},{4,6},{6,4},{5,7},{7,5},{8,10},{10,8},{9,1... | collective-permute-start | bytes 147464 | tf_op jit(solution)/shard_map/ppermute | solution.py:516
  7.7 1.0 %copy-start.3 = (bf16[2,32,16,256]{3,2,1,0:T(8,128)(2,1)S(1)}, bf16[2,32,16,256]{3,2,1,0:T(8,128)(2,1)}, u32[]{:S(2)}) copy-start(bf16[2,32,16,256]{3,2,1,0:T(8,128)(2,1)} %param.8) | copy-start | bytes 1572868
  8.7 6.3 %copy-start.2 = (f32[49,256]{1,0:T(8,128)S(1)}, f32[49,256]{1,0:T(8,128)}, u32[]{:S(2)}) copy-start(f32[49,256]{1,0:T(8,128)} %refs_3_.5) | copy-start | bytes 150532
  8.7 6.3 %copy-start.4 = (bf16[256,1024]{1,0:T(8,128)(2,1)S(1)}, bf16[256,1024]{1,0:T(8,128)(2,1)}, u32[]{:S(2)}) copy-start(bf16[256,1024]{1,0:T(8,128)(2,1)} %refs_5_.1) | copy-start | bytes 1572868
  8.7 6.3 %copy-start.5 = (bf16[1024,256]{1,0:T(8,128)(2,1)S(1)}, bf16[1024,256]{1,0:T(8,128)(2,1)}, u32[]{:S(2)}) copy-start(bf16[1024,256]{1,0:T(8,128)(2,1)} %refs_6_.1) | copy-start | bytes 1572868
  8.7 6.3 %copy-start.6 = (f32[256]{0:T(256)S(1)}, f32[256]{0:T(256)}, u32[]{:S(2)}) copy-start(f32[256]{0:T(256)} %param.10) | copy-start | bytes 3076
  11.3 10.6 %collective-permute-start.1 = (bf16[240,256]{1,0:T(8,128)(2,1)S(1)}, bf16[240,256]{1,0:T(8,128)(2,1)S(1)}, u32[]{:S(2)}, u32[]{:S(2)}) collective-permute-start(bf16[240,256]{1,0:T(8,128)(2,1)S(1)} %get-tuple-element.79), channel_id=1, source_target_pairs={{0,4},{4,8},{8,12},{12,0},{1,5},{5,9},{9,13},{13,1},{2,6},{6,10},{... | collective-permute-start | bytes 368648 | tf_op jit(solution)/shard_map/ppermute | solution.py:554
  13.0 8.9 %collective-permute-start.2 = (bf16[240,256]{1,0:T(8,128)(2,1)S(1)}, bf16[240,256]{1,0:T(8,128)(2,1)S(1)}, u32[]{:S(2)}, u32[]{:S(2)}) collective-permute-start(bf16[240,256]{1,0:T(8,128)(2,1)S(1)} %get-tuple-element.80), channel_id=1, source_target_pairs={{4,0},{8,4},{12,8},{0,12},{5,1},{9,5},{13,9},{1,13},{6,2},{10,6},{... | collective-permute-start | bytes 368648 | tf_op jit(solution)/shard_map/ppermute | solution.py:554
  27.0 2.0 %collective-permute-start.4 = (bf16[256,1024]{1,0:T(8,128)(2,1)S(1)}, bf16[256,1024]{1,0:T(8,128)(2,1)S(1)}, u32[]{:S(2)}, u32[]{:S(2)}) collective-permute-start(bf16[256,1024]{1,0:T(8,128)(2,1)S(1)} %get-tuple-element.89), channel_id=1, source_target_pairs={{0,1},{1,0},{2,3},{3,2},{4,5},{5,4},{6,7},{7,6},{8,9},{9,8},{10,11... | collective-permute-start | bytes 1572872 | tf_op jit(solution)/shard_map/ppermute | solution.py:516
  27.1 4.2 %collective-permute-start.3 = (bf16[96,256]{1,0:T(8,128)(2,1)S(1)}, bf16[96,256]{1,0:T(8,128)(2,1)S(1)}, u32[]{:S(2)}, u32[]{:S(2)}) collective-permute-start(bf16[96,256]{1,0:T(8,128)(2,1)S(1)} %get-tuple-element.87), channel_id=1, source_target_pairs={{0,2},{2,0},{1,3},{3,1},{4,6},{6,4},{5,7},{7,5},{8,10},{10,8},{9,1... | collective-permute-start | bytes 147464 | tf_op jit(solution)/shard_map/ppermute | solution.py:516
  29.1 8.6 %collective-permute-start.7 = (bf16[128,1024]{1,0:T(8,128)(2,1)S(1)}, bf16[128,1024]{1,0:T(8,128)(2,1)S(1)}, u32[]{:S(2)}, u32[]{:S(2)}) collective-permute-start(bf16[128,1024]{1,0:T(8,128)(2,1)S(1)} %get-tuple-element.100), channel_id=1, source_target_pairs={{0,2},{2,0},{1,3},{3,1},{4,6},{6,4},{5,7},{7,5},{8,10},{10,8},{9,1... | collective-permute-start | bytes 786440 | tf_op jit(solution)/shard_map/ppermute | solution.py:516
  31.8 13.0 %collective-permute-start.5 = (bf16[240,256]{1,0:T(8,128)(2,1)S(1)}, bf16[240,256]{1,0:T(8,128)(2,1)S(1)}, u32[]{:S(2)}, u32[]{:S(2)}) collective-permute-start(bf16[240,256]{1,0:T(8,128)(2,1)S(1)} %get-tuple-element.92), channel_id=1, source_target_pairs={{0,4},{4,8},{8,12},{12,0},{1,5},{5,9},{9,13},{13,1},{2,6},{6,10},{... | collective-permute-start | bytes 368648 | tf_op jit(solution)/shard_map/ppermute | solution.py:554
  31.9 12.9 %collective-permute-start.6 = (bf16[240,256]{1,0:T(8,128)(2,1)S(1)}, bf16[240,256]{1,0:T(8,128)(2,1)S(1)}, u32[]{:S(2)}, u32[]{:S(2)}) collective-permute-start(bf16[240,256]{1,0:T(8,128)(2,1)S(1)} %get-tuple-element.93), channel_id=1, source_target_pairs={{4,0},{8,4},{12,8},{0,12},{5,1},{9,5},{13,9},{1,13},{6,2},{10,6},{... | collective-permute-start | bytes 368648 | tf_op jit(solution)/shard_map/ppermute | solution.py:554
  37.8 5.0 %collective-permute-start.8 = (bf16[64,1024]{1,0:T(8,128)(2,1)S(1)}, bf16[64,1024]{1,0:T(8,128)(2,1)S(1)}, u32[]{:S(2)}, u32[]{:S(2)}) collective-permute-start(bf16[64,1024]{1,0:T(8,128)(2,1)S(1)} %get-tuple-element.109), channel_id=1, source_target_pairs={{0,4},{4,0},{8,12},{12,8},{1,5},{5,1},{9,13},{13,9},{2,6},{6,2},{1... | collective-permute-start | bytes 393224 | tf_op jit(solution)/shard_map/ppermute | solution.py:516
  42.9 8.6 %collective-permute-start.11 = (bf16[64,1024]{1,0:T(8,128)(2,1)S(1)}, bf16[64,1024]{1,0:T(8,128)(2,1)S(1)}, u32[]{:S(2)}, u32[]{:S(2)}) collective-permute-start(bf16[64,1024]{1,0:T(8,128)(2,1)S(1)} %get-tuple-element.119.refs_0_), channel_id=1, source_target_pairs={{0,8},{4,12},{8,0},{12,4},{1,9},{5,13},{9,1},{13,5},{2,10},{6,14},... | collective-permute-start | bytes 393224 | tf_op jit(solution)/shard_map/ppermute | solution.py:516
  46.9 1.8 %collective-permute-start.9 = (bf16[288,256]{1,0:T(8,128)(2,1)S(1)}, bf16[288,256]{1,0:T(8,128)(2,1)S(1)}, u32[]{:S(2)}, u32[]{:S(2)}) collective-permute-start(bf16[288,256]{1,0:T(8,128)(2,1)S(1)} %get-tuple-element.113), channel_id=1, source_target_pairs={{0,1},{1,0},{2,3},{3,2},{4,5},{5,4},{6,7},{7,6},{8,9},{9,8},{10,11... | collective-permute-start | bytes 442376 | tf_op jit(solution)/shard_map/ppermute | solution.py:516
  48.7 6.3 %collective-permute-start.10 = (bf16[288,256]{1,0:T(8,128)(2,1)S(1)}, bf16[288,256]{1,0:T(8,128)(2,1)S(1)}, u32[]{:S(2)}, u32[]{:S(2)}) collective-permute-start(bf16[288,256]{1,0:T(8,128)(2,1)S(1)} %get-tuple-element.118.refs_0_), channel_id=1, source_target_pairs={{0,2},{2,0},{1,3},{3,1},{4,6},{6,4},{5,7},{7,5},{8,10},{10,8},{9,1... | collective-permute-start | bytes 442376 | tf_op jit(solution)/shard_map/ppermute | solution.py:516
  51.5 6.5 %collective-permute-start.13 = (bf16[64,1024]{1,0:T(8,128)(2,1)S(1)}, bf16[64,1024]{1,0:T(8,128)(2,1)S(1)}, u32[]{:S(2)}, u32[]{:S(2)}) collective-permute-start(bf16[64,1024]{1,0:T(8,128)(2,1)S(1)} %get-tuple-element.129.refs_0_), channel_id=1, source_target_pairs={{0,4},{4,0},{8,12},{12,8},{1,5},{5,1},{9,13},{13,9},{2,6},{6,2},{1... | collective-permute-start | bytes 393224 | tf_op jit(solution)/shard_map/ppermute | solution.py:516
  55.1 5.5 %collective-permute-start.12 = (bf16[288,256]{1,0:T(8,128)(2,1)S(1)}, bf16[288,256]{1,0:T(8,128)(2,1)S(1)}, u32[]{:S(2)}, u32[]{:S(2)}) collective-permute-start(bf16[288,256]{1,0:T(8,128)(2,1)S(1)} %get-tuple-element.128.refs_0_), channel_id=1, source_target_pairs={{0,4},{4,0},{8,12},{12,8},{1,5},{5,1},{9,13},{13,9},{2,6},{6,2},{1... | collective-permute-start | bytes 442376 | tf_op jit(solution)/shard_map/ppermute | solution.py:516
  58.1 7.7 %collective-permute-start.15 = (bf16[128,1024]{1,0:T(8,128)(2,1)S(1)}, bf16[128,1024]{1,0:T(8,128)(2,1)S(1)}, u32[]{:S(2)}, u32[]{:S(2)}) collective-permute-start(bf16[128,1024]{1,0:T(8,128)(2,1)S(1)} %get-tuple-element.133.refs_0_), channel_id=1, source_target_pairs={{0,2},{2,0},{1,3},{3,1},{4,6},{6,4},{5,7},{7,5},{8,10},{10,8},{9,1... | collective-permute-start | bytes 786440 | tf_op jit(solution)/shard_map/ppermute | solution.py:516
  60.7 8.7 %collective-permute-start.14 = (bf16[288,256]{1,0:T(8,128)(2,1)S(1)}, bf16[288,256]{1,0:T(8,128)(2,1)S(1)}, u32[]{:S(2)}, u32[]{:S(2)}) collective-permute-start(bf16[288,256]{1,0:T(8,128)(2,1)S(1)} %get-tuple-element.132.refs_0_), channel_id=1, source_target_pairs={{0,8},{4,12},{8,0},{12,4},{1,9},{5,13},{9,1},{13,5},{2,10},{6,14},... | collective-permute-start | bytes 442376 | tf_op jit(solution)/shard_map/ppermute | solution.py:516

commit v6 on v5

--- a/solution.py
+++ b/solution.py
@@ -203,15 +203,19 @@
     lax.fori_loop(0, z.cols, step, 0, unroll=4)
     own = M * z.col
     slab_s[own:, :] = jnp.zeros_like(slab_s[own:, :])
-    for ref, first in ((left_ref, 0), (right_ref, z.cols - M)):
+    sides = []
+    for first in (0, z.cols - M):
         for t in range(2 * M * z.samples):
             slab_s[own + t * M : own + (t + 1) * M, :] = halo_s[t * z.cols + first : t * z.cols + first + M, :]
-        ref[0:own, :] = own_ref[first * z.col : (first + M) * z.col, :]
-        ref[own:, :] = slab_s[own:, :].astype(BF16)
-
-
-def unpack_slab(z, slab_ref, slab_s, ref, start):
-    slab_s[...] = slab_ref[...].astype(F32)
+        lines = slab_s[own:, :].astype(BF16)
+        sides.append(jnp.concatenate([own_ref[first * z.col : (first + M) * z.col, :], lines], axis=0))
+    even = lax.axis_index("lon") % 2 == 0
+    left_ref[...] = jnp.where(even, sides[1], sides[0])
+    right_ref[...] = jnp.where(even, sides[0], sides[1])
+
+
+def unpack_slab(z, slab, slab_s, ref, start):
+    slab_s[...] = slab.astype(F32)
     for c in range(M):
         line = lambda side, r, s: slab_s[pl.ds(M * z.col + ((side * M + r) * z.samples + s) * M + c, 1), :]
         pad_column(z, slab_s[c * z.col : (c + 1) * z.col, :], line, ref, start + c * z.pad_col)
@@ -387,10 +391,12 @@
 
 def edge_columns(z, left_ref, pad_ref, right_ref, edge_s, slab_s):
     edge, near = M * z.pad_col, 2 * M * z.pad_col
-    unpack_slab(z, left_ref, slab_s, edge_s, 0)
+    even = lax.axis_index("lon") % 2 == 0
+    one, two = left_ref[...], right_ref[...]
+    unpack_slab(z, jnp.where(even, two, one), slab_s, edge_s, 0)
     edge_s[edge : edge + near, :] = pad_ref[0:near, :]
     edge_s[edge + near : edge + 2 * near, :] = pad_ref[z.cols * z.pad_col - near :, :]
-    unpack_slab(z, right_ref, slab_s, edge_s, edge + 2 * near)
+    unpack_slab(z, jnp.where(even, one, two), slab_s, edge_s, edge + 2 * near)
 
 
 def back_outer_kernel(
@@ -548,10 +554,10 @@
     return lax.ppermute(last, "lat", up), lax.ppermute(first, "lat", [(j, i) for i, j in up])
 
 
-def lon_margins(left, right):
+def lon_margins(one, two):
     size = lax.axis_size("lon")
-    up = [(i, (i + 1) % size) for i in range(size)]
-    return lax.ppermute(right, "lon", up), lax.ppermute(left, "lon", [(j, i) for i, j in up])
+    pairs = [(i, i ^ 1) for i in range(size)]
+    return lax.ppermute(one, "lon", pairs), lax.ppermute(two, "lon", [((i + 1) % size, (j + 1) % size) for i, j in pairs])
 
 
 def body(fine_field, grad_out, conv_kernel, norm_gain, w_expand, w_contract, w_merge):

time: 70.4 us -> 70.5 us (level)
  starting transfers between devices: 22.9 us -> 20.4 us
  waiting for transfers between devices: 10.6 us -> 12.9 us
    ppermute x12, waiting for transfers between devices: 10.6 us -> 12.9 us  [swap(): return lax.ppermute(x, axis, [(i, i ^ distance) for i in range(size)])]
    ppermute x4, starting transfers between devices: 7.69 us -> 6.01 us  [the longest x2 3.54 us: lon_margins(): lax.ppermute(two, 'lon', [((i + 1) % size, (j + 1) % size) for i, j in pa...]
    ppermute x12, starting transfers between devices: 15.2 us -> 14.4 us  [swap(): return lax.ppermute(x, axis, [(i, i ^ distance) for i in range(size)])]
  transfers between devices with their start and end apart: 16 -> 16, of which waited for: 7 -> 8; matrix products, arithmetic and copies ran while one was open for 0% -> 0% of each run, Pallas kernels for 34% -> 34%
where the time goes in v6:
time: 70.5 us; the launch traced here: 70.2 us
  Pallas kernels  32.9 us (47%)
  starting transfers between devices  20.4 us (29%)
  waiting for transfers between devices  12.9 us (18%)
  local copies, waits for them, and re-layouts  3.22 us (5%)
  between operations  0.8 us (1%)
    pallas_call x23, Pallas kernels, kernel_call(): pl.pallas_call(run, out_shape=[jax.ShapeDtypeStruct(s, d) for s, d in out...  32.9 us
    ppermute x12, starting transfers between devices, swap(): return lax.ppermute(x, axis, [(i, i ^ distance) for i in range(size)])  14.4 us
    ppermute x12, waiting for transfers between devices, swap(): return lax.ppermute(x, axis, [(i, i ^ distance) for i in range(size)])  12.9 us
    ppermute x2, starting transfers between devices, lon_margins(): lax.ppermute(two, 'lon', [((i + 1) % size, (j + 1) % size) for i, j in pa...  3.54 us
    unnamed x14, local copies, waits for them, and re-layouts  3.22 us
    ppermute x2, starting transfers between devices, lon_margins(): lax.ppermute(one, 'lon', pairs)  2.47 us
  transfers between devices with their start and end apart: 16, of which 8 were waited for; matrix products, arithmetic and copies ran while one was open for 0% of the time, Pallas kernels for 34%

profile of v6, /device:TPU:0, one launch (start us, length us, event | category | flops | bytes accessed | tf_op | source)
XLA Modules:
  0.0 70.2 jit_solution(654362448797053442)
XLA Ops:
  0.6 1.2 %copy-done = bf16[2,64,32,128]{3,2,1,0:T(8,128)(2,1)S(1)} copy-done((bf16[2,64,32,128]{3,2,1,0:T(8,128)(2,1)S(1)}, bf16[2,64,32,128]{3,2,1,0:T(8,128)(2,1)}, u32[]{:S(2)}) %copy-start) | copy-done | bytes 1048600
  1.9 0.9 %copy-done.1 = bf16[512,256]{1,0:T(8,128)(2,1)S(1)} copy-done((bf16[512,256]{1,0:T(8,128)(2,1)S(1)}, bf16[512,256]{1,0:T(8,128)(2,1)}, u32[]{:S(2)}) %copy-start.1) | copy-done | bytes 262168
  2.8 2.0 %shard_map.126 = (bf16[1024,512]{1,0:T(8,128)(2,1)S(1)}, bf16[1024,256]{1,0:T(8,128)(2,1)S(1)}, f32[4096,128]{1,0:T(8,128)S(1)}, bf16[96,256]{1,0:T(8,128)(2,1)S(1)}, f32[8,128]{1,0:T(8,128)}) custom-call(bf16[4096,128]{1,0:T(8,128)(2,1)S(1)} %bitcast.6, bf16[512,256]{1,0:T(8,128)(2,1)S(1)} %copy-done.1), custom_call_target="tpu_custom_call" | custom-call | bytes 1310720 | tf_op jit(solution)/shard_map/pallas_call | solution.py:30
  4.8 2.9 %collective-permute-start = (bf16[96,256]{1,0:T(8,128)(2,1)S(1)}, bf16[96,256]{1,0:T(8,128)(2,1)S(1)}, u32[]{:S(2)}, u32[]{:S(2)}) collective-permute-start(bf16[96,256]{1,0:T(8,128)(2,1)S(1)} %get-tuple-element.75), channel_id=1, source_target_pairs={{0,2},{2,0},{1,3},{3,1},{4,6},{6,4},{5,7},{7,5},{8,10},{10,8},{9,1... | collective-permute-start | bytes 147464 | tf_op jit(solution)/shard_map/ppermute | solution.py:522
  7.7 1.0 %copy-done.3 = bf16[2,32,16,256]{3,2,1,0:T(8,128)(2,1)S(1)} copy-done((bf16[2,32,16,256]{3,2,1,0:T(8,128)(2,1)S(1)}, bf16[2,32,16,256]{3,2,1,0:T(8,128)(2,1)}, u32[]{:S(2)}) %copy-start.3) | copy-done | bytes 524312
  8.8 1.4 %shard_map.128 = (bf16[1024,256]{1,0:T(8,128)(2,1)S(1)}, bf16[512,512]{1,0:T(8,128)(2,1)S(1)}, f32[8,128]{1,0:T(8,128)}) custom-call(bf16[1024,256]{1,0:T(8,128)(2,1)S(1)} %bitcast.7, bf16[512,256]{1,0:T(8,128)(2,1)S(1)} %copy-done.1), custom_call_target="tpu_custom_call" | custom-call | flops 2000000000 | bytes 786432 | tf_op jit(solution)/shard_map/pallas_call | solution.py:30
  10.1 0.0 collective-permute-done.refs_1_.refs_2_
  10.1 1.1 %shard_map.127 = (f32[1792,256]{1,0:T(8,128)S(1)}, bf16[240,256]{1,0:T(8,128)(2,1)S(1)}, bf16[240,256]{1,0:T(8,128)(2,1)S(1)}, f32[8,128]{1,0:T(8,128)}) custom-call(bf16[1024,256]{1,0:T(8,128)(2,1)S(1)} %get-tuple-element.74.refs_0_.refs_5_.refs_7_, bf16[96,256]{1,0:T(8,128)(2,1)S(1)} %collective-permute-done.refs_1_.refs_2_, ...), custom_call_target="tpu_custom_call" | custom-call | bytes 622592 | tf_op jit(solution)/shard_map/pallas_call | solution.py:30
  11.3 1.7 %collective-permute-start.1 = (bf16[240,256]{1,0:T(8,128)(2,1)S(1)}, bf16[240,256]{1,0:T(8,128)(2,1)S(1)}, u32[]{:S(2)}, u32[]{:S(2)}) collective-permute-start(bf16[240,256]{1,0:T(8,128)(2,1)S(1)} %get-tuple-element.79), channel_id=1, source_target_pairs={{0,4},{4,0},{8,12},{12,8},{1,5},{5,1},{9,13},{13,9},{2,6},{6,2},{1... | collective-permute-start | bytes 368648 | tf_op jit(solution)/shard_map/ppermute | solution.py:560
  13.0 2.5 %collective-permute-start.2 = (bf16[240,256]{1,0:T(8,128)(2,1)S(1)}, bf16[240,256]{1,0:T(8,128)(2,1)S(1)}, u32[]{:S(2)}, u32[]{:S(2)}) collective-permute-start(bf16[240,256]{1,0:T(8,128)(2,1)S(1)} %get-tuple-element.80), channel_id=1, source_target_pairs={{4,8},{8,4},{12,0},{0,12},{5,9},{9,5},{13,1},{1,13},{6,10},{10,6},... | collective-permute-start | bytes 368648 | tf_op jit(solution)/shard_map/ppermute | solution.py:560
  15.5 6.8 %shard_map.129 = (bf16[640,256]{1,0:T(8,128)(2,1)S(1)}, f32[640,256]{1,0:T(8,128)S(1)}, f32[256,1024]{1,0:T(8,128)S(1)}, f32[256,1024]{1,0:T(8,128)S(1)}, f32[8,256]{1,0:T(8,128)S(1)}, /*index=5*/f32[8,128]{1,0:T(8,128)}) custom-call(f32[1792,256]{1,0:T(8,128)S(1)} %get-tuple-element.76.refs_0_, f32[49,256]{1,0:T(8,128)S(1)} %copy-done.2, ...), custom_call_target="tpu_custom_call" | custom-call | flops 8000000000 | bytes 3983360 | tf_op jit(solution)/shard_map/pallas_call | solution.py:30
  22.3 0.0 collective-permute-done.1.refs_1_
  22.3 0.0 collective-permute-done.2.refs_2_
  22.3 5.2 %shard_map.130 = (bf16[384,256]{1,0:T(8,128)(2,1)S(1)}, f32[384,256]{1,0:T(8,128)S(1)}, bf16[256,1024]{1,0:T(8,128)(2,1)S(1)}, bf16[256,1024]{1,0:T(8,128)(2,1)S...) custom-call(f32[1792,256]{1,0:T(8,128)S(1)} %get-tuple-element.76.re, ...), custom_call_target="tpu_custom_call" | custom-call | flops 8000000000 | bytes 6989824 | tf_op jit(solution)/shard_map/pallas_call | solution.py:30
  27.4 0.1 collective-permute-start.4
  27.5 1.6 %collective-permute-start.3 = (bf16[96,256]{1,0:T(8,128)(2,1)S(1)}, bf16[96,256]{1,0:T(8,128)(2,1)S(1)}, u32[]{:S(2)}, u32[]{:S(2)}) collective-permute-start(bf16[96,256]{1,0:T(8,128)(2,1)S(1)} %get-tuple-element.87), channel_id=1, source_target_pairs={{0,2},{2,0},{1,3},{3,1},{4,6},{6,4},{5,7},{7,5},{8,10},{10,8},{9,1... | collective-permute-start | bytes 147464 | tf_op jit(solution)/shard_map/ppermute | solution.py:522
  29.1 0.3 collective-permute-done.4.refs_1_
  29.4 0.1 shard_map.131
  29.5 1.6 %collective-permute-start.7 = (bf16[128,1024]{1,0:T(8,128)(2,1)S(1)}, bf16[128,1024]{1,0:T(8,128)(2,1)S(1)}, u32[]{:S(2)}, u32[]{:S(2)}) collective-permute-start(bf16[128,1024]{1,0:T(8,128)(2,1)S(1)} %get-tuple-element.100), channel_id=1, source_target_pairs={{0,2},{2,0},{1,3},{3,1},{4,6},{6,4},{5,7},{7,5},{8,10},{10,8},{9,1... | collective-permute-start | bytes 786440 | tf_op jit(solution)/shard_map/ppermute | solution.py:522
  31.1 0.6 collective-permute-done.3.refs_1_.refs_2_
  31.7 0.6 shard_map.132
  32.3 0.7 %collective-permute-start.5 = (bf16[240,256]{1,0:T(8,128)(2,1)S(1)}, bf16[240,256]{1,0:T(8,128)(2,1)S(1)}, u32[]{:S(2)}, u32[]{:S(2)}) collective-permute-start(bf16[240,256]{1,0:T(8,128)(2,1)S(1)} %get-tuple-element.92), channel_id=1, source_target_pairs={{0,4},{4,0},{8,12},{12,8},{1,5},{5,1},{9,13},{13,9},{2,6},{6,2},{1... | collective-permute-start | bytes 368648 | tf_op jit(solution)/shard_map/ppermute | solution.py:560
  33.0 1.1 %collective-permute-start.6 = (bf16[240,256]{1,0:T(8,128)(2,1)S(1)}, bf16[240,256]{1,0:T(8,128)(2,1)S(1)}, u32[]{:S(2)}, u32[]{:S(2)}) collective-permute-start(bf16[240,256]{1,0:T(8,128)(2,1)S(1)} %get-tuple-element.93), channel_id=1, source_target_pairs={{4,8},{8,4},{12,0},{0,12},{5,9},{9,5},{13,1},{1,13},{6,10},{10,6},... | collective-permute-start | bytes 368648 | tf_op jit(solution)/shard_map/ppermute | solution.py:560
  34.1 2.0 %shard_map.133 = (f32[64,128]{1,0:T(8,128)S(1)}, f32[8,128]{1,0:T(8,128)S(1)}) custom-call(f32[1792,256]{1,0:T(8,128)S(1)} %get-tuple-element.76.refs_0_, f32[336,256]{1,0:T(8,128)S(1)} %get-tuple-element.95.refs_1_, f32[336,256]{1,0:T(8,128)S(1)} %get-tuple-element.96.refs_2_, f32[640,256]{1,0:T(8,128)S(1)} %get-tuple-element.84.refs_12_.refs_3_, ...), custom_call_target="tpu_custom_call" | custom-call | flops 3000000000 | bytes 3579904 | tf_op jit(solution)/shard_map/pallas_call | solution.py:30
  36.1 1.9 %collective-permute-done.7.refs_1_ = bf16[128,1024]{1,0:T(8,128)(2,1)S(1)} collective-permute-done((bf16[128,1024]{1,0:T(8,128)(2,1)S(1)}, bf16[128,1024]{1,0:T(8,128)(2,1)S(1)}, u32[]{:S(2)}, u32[]{:S(2)}) %collective-permute-start.7) | collective-permute-done | bytes 262176 | tf_op jit(solution)/shard_map/ppermute | solution.py:522
  37.9 0.1 shard_map.134
  38.0 0.7 %collective-permute-start.8 = (bf16[64,1024]{1,0:T(8,128)(2,1)S(1)}, bf16[64,1024]{1,0:T(8,128)(2,1)S(1)}, u32[]{:S(2)}, u32[]{:S(2)}) collective-permute-start(bf16[64,1024]{1,0:T(8,128)(2,1)S(1)} %get-tuple-element.109), channel_id=1, source_target_pairs={{0,4},{4,0},{8,12},{12,8},{1,5},{5,1},{9,13},{13,9},{2,6},{6,2},{1... | collective-permute-start | bytes 393224 | tf_op jit(solution)/shard_map/ppermute | solution.py:522
  38.8 2.0 %shard_map.135 = (f32[64,128]{1,0:T(8,128)S(1)}, f32[8,128]{1,0:T(8,128)S(1)}) custom-call(f32[1792,256]{1,0:T(8,128)S(1)} %get-tuple-element.76.refs_0_, f32[336,256]{1,0:T(8,128)S(1)} %get-tuple-element.95.refs_1_, f32[336,256]{1,0:T(8,128)S(1)} %get-tuple-element.96.refs_2_, f32[640,256]{1,0:T(8,128)S(1)} %get-tuple-element.84.refs_12_.refs_3_, ...), custom_call_target="tpu_custom_call" | custom-call | flops 3000000000 | bytes 3579904 | tf_op jit(solution)/shard_map/pallas_call | solution.py:30
  40.8 2.7 %shard_map.136 = (bf16[640,256]{1,0:T(8,128)(2,1)S(1)}, f32[8,128]{1,0:T(8,128)S(1)}) custom-call(f32[1792,256]{1,0:T(8,128)S(1)} %get-tuple-element.91.refs_0_, f32[49,256]{1,0:T(8,128)S(1)} %copy-done.2, bf16[1024,256]{1,0:T(8,128)(2,1)S(1)} %get-tuple-element.77.refs_6_.refs_8_.refs_2_.refs_4_, f32[8,128]{1,0:T(8,128)S(1)} %get-tuple-element.104.refs_3_), custom_call_target="tpu_custom_call" | custom-call | flops 500000000 | bytes 2409472 | tf_op jit(solution)/shard_map/pallas_call | solution.py:30
  43.5 0.0 collective-permute-done.8.refs_1_
  43.5 1.3 %collective-permute-start.11 = (bf16[64,1024]{1,0:T(8,128)(2,1)S(1)}, bf16[64,1024]{1,0:T(8,128)(2,1)S(1)}, u32[]{:S(2)}, u32[]{:S(2)}) collective-permute-start(bf16[64,1024]{1,0:T(8,128)(2,1)S(1)} %get-tuple-element.119.refs_0_), channel_id=1, source_target_pairs={{0,8},{4,12},{8,0},{12,4},{1,9},{5,13},{9,1},{13,5},{2,10},{6,14},... | collective-permute-start | bytes 393224 | tf_op jit(solution)/shard_map/ppermute | solution.py:522
  44.8 2.1 %shard_map.138 = (bf16[1024,256]{1,0:T(8,128)(2,1)S(1)}, bf16[288,256]{1,0:T(8,128)(2,1)S(1)}, bf16[288,256]{1,0:T(8,128)(2,1)S(1)}, f32[8,128]{1,0:T(8,128)S(1)}) custom-call(f32[1792,256]{1,0:T(8,128)S(1)} %get-tuple-element.91.refs_0_, bf16[240,256]{1,0:T(8,128)(2,1)S(1)} %collective-permute-done.5.refs_1_, ...), custom_call_target="tpu_custom_call" | custom-call | flops 4000000000 | bytes 4097024 | tf_op jit(solution)/shard_map/pallas_call | solution.py:30
  46.9 0.1 collective-permute-start.9
  47.0 1.7 %shard_map.139 = (f32[4160,128]{1,0:T(8,128)S(1)}, f32[8,128]{1,0:T(8,128)S(1)}) custom-call(bf16[1024,256]{1,0:T(8,128)(2,1)S(1)} %get-tuple-element.114.refs_0_, bf16[512,512]{1,0:T(8,128)(2,1)S(1)} %get-tuple-element.115.refs_1_, bf16[1024,512]{1,0:T(8,128)(2,1)S(1)} %get-tuple-element.94.refs_5_.refs_2_, f32[8,128]{1,0:T(8,128)S(1)} %get-tuple-element.116.refs_3_), custom_call_target="tpu_custom_call" | custom-call | flops 3000000000 | bytes 2097152 | tf_op jit(solution)/shard_map/pallas_call | solution.py:30
  48.8 1.6 %collective-permute-start.10 = (bf16[288,256]{1,0:T(8,128)(2,1)S(1)}, bf16[288,256]{1,0:T(8,128)(2,1)S(1)}, u32[]{:S(2)}, u32[]{:S(2)}) collective-permute-start(bf16[288,256]{1,0:T(8,128)(2,1)S(1)} %get-tuple-element.118.refs_0_), channel_id=1, source_target_pairs={{0,2},{2,0},{1,3},{3,1},{4,6},{6,4},{5,7},{7,5},{8,10},{10,8},{9,1... | collective-permute-start | bytes 442376 | tf_op jit(solution)/shard_map/ppermute | solution.py:522
  50.3 1.2 %shard_map.141 = (bf16[4096,128]{1,0:T(8,128)(2,1)}, f32[8,128]{1,0:T(8,128)S(1)}) custom-call(f32[4160,128]{1,0:T(8,128)S(1)} %get-tuple-element.120.refs_0_, f32[4096,128]{1,0:T(8,128)S(1)} %get-tuple-element.121.refs_1_, f32[8,128]{1,0:T(8,128)S(1)} %get-tuple-element.122.refs_2_), custom_call_target="tpu_custom_call" | custom-call | flops 2000000000 | bytes 4227072 | tf_op jit(solution)/shard_map/pallas_call | solution.py:30
  51.5 0.2 collective-permute-done.11.refs_1_
  51.7 0.5 collective-permute-start.13
  52.3 2.8 %collective-permute-done.10.refs_1_ = bf16[288,256]{1,0:T(8,128)(2,1)S(1)} collective-permute-done((bf16[288,256]{1,0:T(8,128)(2,1)S(1)}, bf16[288,256]{1,0:T(8,128)(2,1)S(1)}, u32[]{:S(2)}, u32[]{:S(2)}) %collective-permute-start.10) | collective-permute-done | bytes 147488 | tf_op jit(solution)/shard_map/ppermute | solution.py:522
  55.1 0.7 %collective-permute-start.12 = (bf16[288,256]{1,0:T(8,128)(2,1)S(1)}, bf16[288,256]{1,0:T(8,128)(2,1)S(1)}, u32[]{:S(2)}, u32[]{:S(2)}) collective-permute-start(bf16[288,256]{1,0:T(8,128)(2,1)S(1)} %get-tuple-element.128.refs_0_), channel_id=1, source_target_pairs={{0,4},{4,0},{8,12},{12,8},{1,5},{5,1},{9,13},{13,9},{2,6},{6,2},{1... | collective-permute-start | bytes 442376 | tf_op jit(solution)/shard_map/ppermute | solution.py:522
  55.8 1.8 %shard_map.144 = (bf16[1024,256]{1,0:T(8,128)(2,1)}, f32[8,128]{1,0:T(8,128)S(1)}) custom-call(bf16[640,256]{1,0:T(8,128)(2,1)S(1)} %get-tuple-element.78.refs_0_, bf16[384,256]{1,0:T(8,128)(2,1)S(1)} %get-tuple-element.85.refs_1_, f32[8,128]{1,0:T(8,128)S(1)} %get-tuple-element.125.refs_2_), custom_call_target="tpu_custom_call" | custom-call | flops 2000000000 | bytes 524288 | tf_op jit(solution)/shard_map/pallas_call | solution.py:30
  57.7 1.6 %collective-permute-start.15 = (bf16[128,1024]{1,0:T(8,128)(2,1)S(1)}, bf16[128,1024]{1,0:T(8,128)(2,1)S(1)}, u32[]{:S(2)}, u32[]{:S(2)}) collective-permute-start(bf16[128,1024]{1,0:T(8,128)(2,1)S(1)} %get-tuple-element.133.refs_0_), channel_id=1, source_target_pairs={{0,2},{2,0},{1,3},{3,1},{4,6},{6,4},{5,7},{7,5},{8,10},{10,8},{9,1... | collective-permute-start | bytes 786440 | tf_op jit(solution)/shard_map/ppermute | solution.py:522
  59.3 1.3 %collective-permute-done.12.refs_1_ = bf16[288,256]{1,0:T(8,128)(2,1)S(1)} collective-permute-done((bf16[288,256]{1,0:T(8,128)(2,1)S(1)}, bf16[288,256]{1,0:T(8,128)(2,1)S(1)}, u32[]{:S(2)}, u32[]{:S(2)}) %collective-permute-start.12) | collective-permute-done | bytes 147488 | tf_op jit(solution)/shard_map/ppermute | solution.py:522
  60.7 1.8 %collective-permute-start.14 = (bf16[288,256]{1,0:T(8,128)(2,1)S(1)}, bf16[288,256]{1,0:T(8,128)(2,1)S(1)}, u32[]{:S(2)}, u32[]{:S(2)}) collective-permute-start(bf16[288,256]{1,0:T(8,128)(2,1)S(1)} %get-tuple-element.132.refs_0_), channel_id=1, source_target_pairs={{0,8},{4,12},{8,0},{12,4},{1,9},{5,13},{9,1},{13,5},{2,10},{6,14},... | collective-permute-start | bytes 442376 | tf_op jit(solution)/shard_map/ppermute | solution.py:522
  62.4 3.0 %collective-permute-done.15.refs_1_ = bf16[128,1024]{1,0:T(8,128)(2,1)S(1)} collective-permute-done((bf16[128,1024]{1,0:T(8,128)(2,1)S(1)}, bf16[128,1024]{1,0:T(8,128)(2,1)S(1)}, u32[]{:S(2)}, u32[]{:S(2)}) %collective-permute-start.15) | collective-permute-done | bytes 262176 | tf_op jit(solution)/shard_map/ppermute | solution.py:522
  65.5 1.2 %shard_map.147 = (f32[128,1024]{1,0:T(8,128)}, f32[512,256]{1,0:T(8,128)}, f32[8,128]{1,0:T(8,128)S(1)}) custom-call(bf16[128,1024]{1,0:T(8,128)(2,1)S(1)} %get-tuple-element.133.refs_0_, bf16[128,1024]{1,0:T(8,128)(2,1)S(1)} %collective-permute-done.15.refs_1_, f32[8,128]{1,0:T(8,128)S(1)} %get-tuple-element.134.refs_2_), custom_call_target="tpu_custom_call" | custom-call | bytes 524288 | tf_op jit(solution)/shard_map/pallas_call | solution.py:30
  66.6 2.8 %collective-permute-done.14.refs_1_ = bf16[288,256]{1,0:T(8,128)(2,1)S(1)} collective-permute-done((bf16[288,256]{1,0:T(8,128)(2,1)S(1)}, bf16[288,256]{1,0:T(8,128)(2,1)S(1)}, u32[]{:S(2)}, u32[]{:S(2)}) %collective-permute-start.14) | collective-permute-done | bytes 147488 | tf_op jit(solution)/shard_map/ppermute | solution.py:522
  69.4 0.8 %shard_map.148 = (f32[256,256]{1,0:T(8,128)}, f32[49,128]{1,0:T(8,128)}, f32[1,128]{1,0:T(1,128)}, f32[8,128]{1,0:T(8,128)}) custom-call(bf16[288,256]{1,0:T(8,128)(2,1)S(1)} %get-tuple-element.132.refs_0_, bf16[288,256]{1,0:T(8,128)(2,1)S(1)} %collective-permute-done.14.refs_1_, f32[8,128]{1,0:T(8,128)S(1)} %get-tuple-element.135.refs_2_), custom_call_target="tpu_custom_call" | custom-call | bytes 294912 | tf_op jit(solution)/shard_map/pallas_call | solution.py:30
  (21 shorter events, 0.2 us)
Async XLA Ops:
  0.6 1.2 %copy-start = (bf16[2,64,32,128]{3,2,1,0:T(8,128)(2,1)S(1)}, bf16[2,64,32,128]{3,2,1,0:T(8,128)(2,1)}, u32[]{:S(2)}) copy-start(bf16[2,64,32,128]{3,2,1,0:T(8,128)(2,1)} %param.7) | copy-start | bytes 3145732
  1.9 0.9 %copy-start.1 = (bf16[512,256]{1,0:T(8,128)(2,1)S(1)}, bf16[512,256]{1,0:T(8,128)(2,1)}, u32[]{:S(2)}) copy-start(bf16[512,256]{1,0:T(8,128)(2,1)} %refs_1_.5) | copy-start | bytes 786436
  4.8 5.4 %collective-permute-start = (bf16[96,256]{1,0:T(8,128)(2,1)S(1)}, bf16[96,256]{1,0:T(8,128)(2,1)S(1)}, u32[]{:S(2)}, u32[]{:S(2)}) collective-permute-start(bf16[96,256]{1,0:T(8,128)(2,1)S(1)} %get-tuple-element.75), channel_id=1, source_target_pairs={{0,2},{2,0},{1,3},{3,1},{4,6},{6,4},{5,7},{7,5},{8,10},{10,8},{9,1... | collective-permute-start | bytes 147464 | tf_op jit(solution)/shard_map/ppermute | solution.py:522
  7.7 1.0 %copy-start.3 = (bf16[2,32,16,256]{3,2,1,0:T(8,128)(2,1)S(1)}, bf16[2,32,16,256]{3,2,1,0:T(8,128)(2,1)}, u32[]{:S(2)}) copy-start(bf16[2,32,16,256]{3,2,1,0:T(8,128)(2,1)} %param.8) | copy-start | bytes 1572868
  8.7 6.7 %copy-start.2 = (f32[49,256]{1,0:T(8,128)S(1)}, f32[49,256]{1,0:T(8,128)}, u32[]{:S(2)}) copy-start(f32[49,256]{1,0:T(8,128)} %refs_3_.5) | copy-start | bytes 150532
  8.7 6.7 %copy-start.4 = (bf16[256,1024]{1,0:T(8,128)(2,1)S(1)}, bf16[256,1024]{1,0:T(8,128)(2,1)}, u32[]{:S(2)}) copy-start(bf16[256,1024]{1,0:T(8,128)(2,1)} %refs_5_.1) | copy-start | bytes 1572868
  8.7 6.7 %copy-start.5 = (bf16[1024,256]{1,0:T(8,128)(2,1)S(1)}, bf16[1024,256]{1,0:T(8,128)(2,1)}, u32[]{:S(2)}) copy-start(bf16[1024,256]{1,0:T(8,128)(2,1)} %refs_6_.1) | copy-start | bytes 1572868
  8.7 6.7 %copy-start.6 = (f32[256]{0:T(256)S(1)}, f32[256]{0:T(256)}, u32[]{:S(2)}) copy-start(f32[256]{0:T(256)} %param.10) | copy-start | bytes 3076
  11.3 11.0 %collective-permute-start.1 = (bf16[240,256]{1,0:T(8,128)(2,1)S(1)}, bf16[240,256]{1,0:T(8,128)(2,1)S(1)}, u32[]{:S(2)}, u32[]{:S(2)}) collective-permute-start(bf16[240,256]{1,0:T(8,128)(2,1)S(1)} %get-tuple-element.79), channel_id=1, source_target_pairs={{0,4},{4,0},{8,12},{12,8},{1,5},{5,1},{9,13},{13,9},{2,6},{6,2},{1... | collective-permute-start | bytes 368648 | tf_op jit(solution)/shard_map/ppermute | solution.py:560
  13.0 9.3 %collective-permute-start.2 = (bf16[240,256]{1,0:T(8,128)(2,1)S(1)}, bf16[240,256]{1,0:T(8,128)(2,1)S(1)}, u32[]{:S(2)}, u32[]{:S(2)}) collective-permute-start(bf16[240,256]{1,0:T(8,128)(2,1)S(1)} %get-tuple-element.80), channel_id=1, source_target_pairs={{4,8},{8,4},{12,0},{0,12},{5,9},{9,5},{13,1},{1,13},{6,10},{10,6},... | collective-permute-start | bytes 368648 | tf_op jit(solution)/shard_map/ppermute | solution.py:560
  27.4 2.0 %collective-permute-start.4 = (bf16[256,1024]{1,0:T(8,128)(2,1)S(1)}, bf16[256,1024]{1,0:T(8,128)(2,1)S(1)}, u32[]{:S(2)}, u32[]{:S(2)}) collective-permute-start(bf16[256,1024]{1,0:T(8,128)(2,1)S(1)} %get-tuple-element.89), channel_id=1, source_target_pairs={{0,1},{1,0},{2,3},{3,2},{4,5},{5,4},{6,7},{7,6},{8,9},{9,8},{10,11... | collective-permute-start | bytes 1572872 | tf_op jit(solution)/shard_map/ppermute | solution.py:522
  27.5 4.2 %collective-permute-start.3 = (bf16[96,256]{1,0:T(8,128)(2,1)S(1)}, bf16[96,256]{1,0:T(8,128)(2,1)S(1)}, u32[]{:S(2)}, u32[]{:S(2)}) collective-permute-start(bf16[96,256]{1,0:T(8,128)(2,1)S(1)} %get-tuple-element.87), channel_id=1, source_target_pairs={{0,2},{2,0},{1,3},{3,1},{4,6},{6,4},{5,7},{7,5},{8,10},{10,8},{9,1... | collective-permute-start | bytes 147464 | tf_op jit(solution)/shard_map/ppermute | solution.py:522
  29.5 8.4 %collective-permute-start.7 = (bf16[128,1024]{1,0:T(8,128)(2,1)S(1)}, bf16[128,1024]{1,0:T(8,128)(2,1)S(1)}, u32[]{:S(2)}, u32[]{:S(2)}) collective-permute-start(bf16[128,1024]{1,0:T(8,128)(2,1)S(1)} %get-tuple-element.100), channel_id=1, source_target_pairs={{0,2},{2,0},{1,3},{3,1},{4,6},{6,4},{5,7},{7,5},{8,10},{10,8},{9,1... | collective-permute-start | bytes 786440 | tf_op jit(solution)/shard_map/ppermute | solution.py:522
  32.3 12.6 %collective-permute-start.5 = (bf16[240,256]{1,0:T(8,128)(2,1)S(1)}, bf16[240,256]{1,0:T(8,128)(2,1)S(1)}, u32[]{:S(2)}, u32[]{:S(2)}) collective-permute-start(bf16[240,256]{1,0:T(8,128)(2,1)S(1)} %get-tuple-element.92), channel_id=1, source_target_pairs={{0,4},{4,0},{8,12},{12,8},{1,5},{5,1},{9,13},{13,9},{2,6},{6,2},{1... | collective-permute-start | bytes 368648 | tf_op jit(solution)/shard_map/ppermute | solution.py:560
  33.0 11.8 %collective-permute-start.6 = (bf16[240,256]{1,0:T(8,128)(2,1)S(1)}, bf16[240,256]{1,0:T(8,128)(2,1)S(1)}, u32[]{:S(2)}, u32[]{:S(2)}) collective-permute-start(bf16[240,256]{1,0:T(8,128)(2,1)S(1)} %get-tuple-element.93), channel_id=1, source_target_pairs={{4,8},{8,4},{12,0},{0,12},{5,9},{9,5},{13,1},{1,13},{6,10},{10,6},... | collective-permute-start | bytes 368648 | tf_op jit(solution)/shard_map/ppermute | solution.py:560
  38.0 5.4 %collective-permute-start.8 = (bf16[64,1024]{1,0:T(8,128)(2,1)S(1)}, bf16[64,1024]{1,0:T(8,128)(2,1)S(1)}, u32[]{:S(2)}, u32[]{:S(2)}) collective-permute-start(bf16[64,1024]{1,0:T(8,128)(2,1)S(1)} %get-tuple-element.109), channel_id=1, source_target_pairs={{0,4},{4,0},{8,12},{12,8},{1,5},{5,1},{9,13},{13,9},{2,6},{6,2},{1... | collective-permute-start | bytes 393224 | tf_op jit(solution)/shard_map/ppermute | solution.py:522
  43.5 8.2 %collective-permute-start.11 = (bf16[64,1024]{1,0:T(8,128)(2,1)S(1)}, bf16[64,1024]{1,0:T(8,128)(2,1)S(1)}, u32[]{:S(2)}, u32[]{:S(2)}) collective-permute-start(bf16[64,1024]{1,0:T(8,128)(2,1)S(1)} %get-tuple-element.119.refs_0_), channel_id=1, source_target_pairs={{0,8},{4,12},{8,0},{12,4},{1,9},{5,13},{9,1},{13,5},{2,10},{6,14},... | collective-permute-start | bytes 393224 | tf_op jit(solution)/shard_map/ppermute | solution.py:522
  46.9 1.8 %collective-permute-start.9 = (bf16[288,256]{1,0:T(8,128)(2,1)S(1)}, bf16[288,256]{1,0:T(8,128)(2,1)S(1)}, u32[]{:S(2)}, u32[]{:S(2)}) collective-permute-start(bf16[288,256]{1,0:T(8,128)(2,1)S(1)} %get-tuple-element.113), channel_id=1, source_target_pairs={{0,1},{1,0},{2,3},{3,2},{4,5},{5,4},{6,7},{7,6},{8,9},{9,8},{10,11... | collective-permute-start | bytes 442376 | tf_op jit(solution)/shard_map/ppermute | solution.py:522
  48.8 6.3 %collective-permute-start.10 = (bf16[288,256]{1,0:T(8,128)(2,1)S(1)}, bf16[288,256]{1,0:T(8,128)(2,1)S(1)}, u32[]{:S(2)}, u32[]{:S(2)}) collective-permute-start(bf16[288,256]{1,0:T(8,128)(2,1)S(1)} %get-tuple-element.118.refs_0_), channel_id=1, source_target_pairs={{0,2},{2,0},{1,3},{3,1},{4,6},{6,4},{5,7},{7,5},{8,10},{10,8},{9,1... | collective-permute-start | bytes 442376 | tf_op jit(solution)/shard_map/ppermute | solution.py:522
  51.7 5.9 %collective-permute-start.13 = (bf16[64,1024]{1,0:T(8,128)(2,1)S(1)}, bf16[64,1024]{1,0:T(8,128)(2,1)S(1)}, u32[]{:S(2)}, u32[]{:S(2)}) collective-permute-start(bf16[64,1024]{1,0:T(8,128)(2,1)S(1)} %get-tuple-element.129.refs_0_), channel_id=1, source_target_pairs={{0,4},{4,0},{8,12},{12,8},{1,5},{5,1},{9,13},{13,9},{2,6},{6,2},{1... | collective-permute-start | bytes 393224 | tf_op jit(solution)/shard_map/ppermute | solution.py:522
  55.1 5.5 %collective-permute-start.12 = (bf16[288,256]{1,0:T(8,128)(2,1)S(1)}, bf16[288,256]{1,0:T(8,128)(2,1)S(1)}, u32[]{:S(2)}, u32[]{:S(2)}) collective-permute-start(bf16[288,256]{1,0:T(8,128)(2,1)S(1)} %get-tuple-element.128.refs_0_), channel_id=1, source_target_pairs={{0,4},{4,0},{8,12},{12,8},{1,5},{5,1},{9,13},{13,9},{2,6},{6,2},{1... | collective-permute-start | bytes 442376 | tf_op jit(solution)/shard_map/ppermute | solution.py:522
  57.7 7.7 %collective-permute-start.15 = (bf16[128,1024]{1,0:T(8,128)(2,1)S(1)}, bf16[128,1024]{1,0:T(8,128)(2,1)S(1)}, u32[]{:S(2)}, u32[]{:S(2)}) collective-permute-start(bf16[128,1024]{1,0:T(8,128)(2,1)S(1)} %get-tuple-element.133.refs_0_), channel_id=1, source_target_pairs={{0,2},{2,0},{1,3},{3,1},{4,6},{6,4},{5,7},{7,5},{8,10},{10,8},{9,1... | collective-permute-start | bytes 786440 | tf_op jit(solution)/shard_map/ppermute | solution.py:522
  60.7 8.7 %collective-permute-start.14 = (bf16[288,256]{1,0:T(8,128)(2,1)S(1)}, bf16[288,256]{1,0:T(8,128)(2,1)S(1)}, u32[]{:S(2)}, u32[]{:S(2)}) collective-permute-start(bf16[288,256]{1,0:T(8,128)(2,1)S(1)} %get-tuple-element.132.refs_0_), channel_id=1, source_target_pairs={{0,8},{4,12},{8,0},{12,4},{1,9},{5,13},{9,1},{13,5},{2,10},{6,14},... | collective-permute-start | bytes 442376 | tf_op jit(solution)/shard_map/ppermute | solution.py:522
